TPU v7x, 256 devices: a whole 4x4x8 slice. The times are simulated.
256 devices in a mesh: leaf: 64 (over z, x, core), cols: 4 (over y).
Axes of the slice: x: 4, y: 4, z: 8, core: 2. Of those that a mesh axis runs over, the one named last changes fastest.
Arguments:
- points: bfloat16 [131072, 256], P('leaf')
- weights: bfloat16 [131072, 512], P('leaf', 'cols'), may hold values from -0.1796875 to 0.1796875
- leaf_basis: bfloat16 [512, 256, 128], P('leaf'), may hold values from -0.375 to 0.375
- leaf_transfer: bfloat16 [512, 128, 128], P('leaf'), may hold values from -0.25 to 0.25
- node_transfer: bfloat16 [128, 128, 128], P('leaf'), may hold values from -0.25 to 0.25
- leaf_skeleton: int32 [512, 128], P('leaf'), may hold values from 0 to 255, as said below
- node_skeleton: int32 [128, 128], P('leaf'), may hold values from 0 to 511, as said below
- upper_skeleton: int32 [32, 128], replicated, may hold values from 0 to 511, as said below
- leaf_far: int32 [512, 12], P('leaf'), may hold values from 0 to 511, as said below
- leaf_count: int32 [512], P('leaf'), may hold values from 1 to 12
- node_far: int32 [128, 12], P('leaf'), may hold values from 0 to 127, as said below
- node_count: int32 [128], P('leaf'), may hold values from 1 to 8
- upper_far: int32 [32, 12], replicated, may hold values from 0 to 31, as said below
- upper_count: int32 [32], replicated, may hold values from 1 to 2
Outputs:
- potentials: bfloat16 [131072, 512], P('leaf', 'cols')
Inputs may be any that keep to these rules, and one draw needn't show every extreme that they name: `leaf_skeleton`: each row holds 128 different positions. `node_skeleton`: each row holds 128 different positions. `upper_skeleton`: each row holds 128 different positions. `leaf_far`: entries of row t are (t + e) mod 512 with 1 <= |e| <= 8; the used entries of a row are different. `node_far`: entries of row t are (t + e) mod 128 with 1 <= |e| <= 4; the used entries of a row are different. `upper_far`: entries of row t are (t + 1) or (t - 1) mod 32; the used entries of a row are different.
All inputs are finite; a program needn't handle non-finite values.
Results may differ from a plain program's by a relative error of at most 0.009.
Values may be sent and summed in bfloat16 or wider, within the bound.
No kernel may reach another device: no remote copies, remote signals or barrier semaphores. Data moves between devices by JAX's collectives and lax.ppermute only.
A program may use at most 128 MiB of HBM per device.

v0:
```python
import math

import jax
import jax.numpy as jnp
from jax import lax
from jax.sharding import PartitionSpec as P


def extended(block, sides, width):
    for axis, dim in sides:
        count = lax.axis_size(axis)
        forward = [(i, i + 1) for i in range(count - 1)]
        forward.append((count - 1, 0))
        backward = [(target, source) for source, target in forward]
        low = lax.ppermute(
            lax.slice_in_dim(block, block.shape[dim] - width, None, axis=dim), axis, forward
        )
        high = lax.ppermute(lax.slice_in_dim(block, 0, width, axis=dim), axis, backward)
        block = jnp.concatenate([low, block, high], axis=dim)
    return block


def shifted(value, axis, steps):
    count = lax.axis_size(axis)
    pairs = [(source, (source + steps) % count) for source in range(count)]
    return lax.ppermute(value, axis, pairs)


def kernel_block(left_pts, right_pts):
    inner_prod = jnp.einsum(
        "...af,...bf->...ab", left_pts, right_pts, preferred_element_type=jnp.float32
    )
    left_sq = jnp.sum(jnp.square(left_pts.astype(jnp.float32)), -1)
    right_sq = jnp.sum(jnp.square(right_pts.astype(jnp.float32)), -1)
    distance = left_sq[..., :, None] + right_sq[..., None, :] - 2.0 * inner_prod
    features = left_pts.shape[-1]
    gamma_scale = 1.0 / math.sqrt(8.0 * features)
    return jnp.exp(gamma_scale * (2.0 * features - distance))


def make_tiles(leaf_points):
    leaf_rows = leaf_points.shape[1]
    no_self = 1.0 - jnp.eye(leaf_rows, dtype=jnp.float32)
    return (kernel_block(leaf_points, leaf_points) * no_self).astype(jnp.bfloat16)


def far_blocks(own_pts, source_pts, live_counts):
    kslots = jnp.arange(source_pts.shape[1], dtype=jnp.int32)
    blocks = kernel_block(own_pts[:, None], source_pts)
    live_mask = (kslots[None, :] < live_counts[:, None]).astype(jnp.float32)
    return (blocks * live_mask[:, :, None, None]).astype(jnp.bfloat16)


def apply_blocks(blocks, source_charges):
    return jnp.einsum("mkrs,mksc->mrc", blocks, source_charges, preferred_element_type=jnp.float32)


def selection(far_list, live_counts, window_start, window_rows, total_rows):
    kslots = jnp.arange(far_list.shape[1], dtype=jnp.int32)
    spots = jnp.arange(window_rows, dtype=jnp.int32)
    source_ids = jnp.mod(window_start + spots, total_rows)
    live = kslots[None, :] < live_counts[:, None]
    hits = (far_list[:, :, None] == source_ids[None, None, :]) & live[:, :, None]
    hits = hits & (spots < total_rows)[None, None, :]
    return jnp.sum(hits.astype(jnp.float32), axis=1)


def window_blocks(own_pts, window_pts, picked):
    blocks = kernel_block(own_pts[:, None], window_pts[None])
    return (blocks * picked[:, :, None, None]).astype(jnp.bfloat16)


def apply_window(blocks, window_charges):
    return jnp.einsum("mjrs,jsc->mrc", blocks, window_charges, preferred_element_type=jnp.float32)


def per_device(
    points,
    weights,
    leaf_basis,
    leaf_transfer,
    node_transfer,
    leaf_skeleton,
    node_skeleton,
    upper_skeleton,
    leaf_far,
    leaf_count,
    node_far,
    node_count,
    upper_far,
    upper_count,
):
    leaves_here, leaf_rows, skel_rank = leaf_basis.shape
    nodes_here = node_transfer.shape[0]
    features = points.shape[1]
    col_width = weights.shape[1]
    leaf_points = points.reshape(leaves_here, leaf_rows, features)
    leaf_weights = weights.reshape(leaves_here, leaf_rows, col_width)
    devices = lax.axis_size("leaf")
    device = lax.axis_index("leaf")
    charges = jnp.einsum(
        "lpr,lpc->lrc", leaf_basis, leaf_weights, preferred_element_type=jnp.float32
    ).astype(jnp.bfloat16)
    skel_pts = jnp.take_along_axis(leaf_points, leaf_skeleton[:, :, None], axis=1)
    packed = jnp.concatenate([skel_pts, charges], axis=-1)
    rimmed = extended(packed, (("leaf", 0),), leaves_here)
    total_leaves = leaves_here * devices
    rim_pts = rimmed[..., :features]
    rim_charges = rimmed[..., features:]
    leaf_picked = selection(
        leaf_far, leaf_count, device * leaves_here - leaves_here, rimmed.shape[0], total_leaves
    )
    near_tiles = make_tiles(leaf_points)
    leaf_blocks = window_blocks(skel_pts, rim_pts, leaf_picked)
    near_field = jnp.einsum(
        "lpq,lqc->lpc", near_tiles, leaf_weights, preferred_element_type=jnp.float32
    )
    leaf_pot = apply_window(leaf_blocks, rim_charges)
    node_q = jnp.einsum(
        "nkrs,nkrc->nsc",
        leaf_transfer.reshape(nodes_here, 4, skel_rank, skel_rank),
        charges.reshape(nodes_here, 4, skel_rank, col_width),
        preferred_element_type=jnp.float32,
    ).astype(jnp.bfloat16)
    node_pts = jnp.take_along_axis(
        skel_pts.reshape(nodes_here, 4 * skel_rank, features), node_skeleton[:, :, None], axis=1
    )
    pieces = []
    reach_hops = (6 + nodes_here) // nodes_here
    node_pack = jnp.concatenate([node_pts, node_q, node_transfer], axis=-1)
    shift_list = list(range(reach_hops, 0, -1)) + [0] + list(range(-1, -reach_hops - 1, -1))
    for offset in shift_list:
        if offset == 0:
            pieces.append(node_pack)
        else:
            pieces.append(shifted(node_pack, "leaf", offset))
    window = jnp.concatenate(pieces, axis=0)
    total_nodes = nodes_here * devices
    window_start = device * nodes_here - reach_hops * nodes_here
    node_picked = selection(node_far, node_count, window_start, window.shape[0], total_nodes)
    node_blocks = window_blocks(node_pts, window[..., :features], node_picked)
    node_pot = apply_window(node_blocks, window[..., features : features + col_width])
    uppers = max(1, nodes_here // 4)
    first_upper = device * nodes_here // 4
    upper_ids = first_upper + jnp.arange(uppers, dtype=jnp.int32)
    members = jnp.concatenate([upper_ids[:, None], upper_far[upper_ids]], axis=1)
    children = members[:, :, None] * 4 + jnp.arange(4, dtype=jnp.int32)[None, None, :]
    child_data = window[jnp.mod(children - window_start, total_nodes)]
    child_pts = child_data[..., :features].reshape(
        uppers, members.shape[1], 4 * skel_rank, features
    )
    child_q = child_data[..., features : features + col_width]
    child_transfer = child_data[..., features + col_width :]
    upper_q = jnp.einsum(
        "umjrs,umjrc->umsc", child_transfer, child_q, preferred_element_type=jnp.float32
    ).astype(jnp.bfloat16)
    upper_pts = jnp.take_along_axis(child_pts, upper_skeleton[members][:, :, :, None], axis=2)
    upper_blocks = far_blocks(upper_pts[:, 0], upper_pts[:, 1:], upper_count[upper_ids])
    upper_down = apply_blocks(upper_blocks, upper_q[:, 1:]).astype(jnp.bfloat16)
    global_ids = device * nodes_here + jnp.arange(nodes_here, dtype=jnp.int32)
    parent_slot = global_ids // 4 - first_upper
    node_down = (
        node_pot
        + jnp.einsum(
            "nrs,nsc->nrc",
            node_transfer,
            upper_down[parent_slot],
            preferred_element_type=jnp.float32,
        )
    ).astype(jnp.bfloat16)
    leaf_down = (
        leaf_pot
        + jnp.einsum(
            "lrs,lsc->lrc",
            leaf_transfer,
            jnp.repeat(node_down, 4, axis=0),
            preferred_element_type=jnp.float32,
        )
    ).astype(jnp.bfloat16)
    result = near_field + jnp.einsum(
        "lpr,lrc->lpc", leaf_basis, leaf_down, preferred_element_type=jnp.float32
    )
    return result.reshape(leaves_here * leaf_rows, col_width).astype(jnp.bfloat16)


def solution(mesh):
    placed = (
        P("leaf", None),
        P("leaf", "cols"),
        P("leaf", None, None),
        P("leaf", None, None),
        P("leaf", None, None),
        P("leaf", None),
        P("leaf", None),
        P(),
        P("leaf", None),
        P("leaf"),
        P("leaf", None),
        P("leaf"),
        P(),
        P(),
    )
    return jax.shard_map(
        per_device, mesh=mesh, in_specs=placed, out_specs=P("leaf", "cols"), check_vma=False
    )
```

profile of v0, /device:TPU:92, one launch (start us, length us, event | category | flops | bytes accessed | tf_op | source)
XLA Modules:
  0.0 128.9 jit_solution(1223251875456248287)
XLA Ops:
  2.9 1.4 %convolution_convert_fusion = bf16[8,128,128]{1,2,0:T(8,128)(2,1)S(1)} fusion(bf16[8,256,128]{2,1,0:T(8,128)(2,1)} %param.16, bf16[8,256,128]{2,1,0:T(8,128)(2,1)S(1)} %bitcast.229), kind=kOutput, calls=%fused_computation.51 | convolution fusion | flops 67239936 | bytes 1310720 | tf_op jit(solution)/shard_map/lpr,lpc->lrc/dot_general | solution.py:101
  4.3 1.2 fusion.67
  5.6 5.8 %gather_fusion.2 = bf16[1024,256]{1,0:T(8,128)(2,1)S(1)} fusion(bf16[8,256,256]{2,1,0:T(8,128)(2,1)S(1)} %bitcast.231, s32[1024]{0:T(1024)S(1)} %fusion.110), kind=kCustom, calls=%fused_computation.2 | custom fusion | bytes 1056768 | tf_op jit(solution)/shard_map/jit(take_along_axis)/gather | solution.py:104
  11.7 1.7 %gather_fusion.3 = bf16[256,256]{1,0:T(8,128)(2,1)S(1)} fusion(bf16[2,512,256]{2,1,0:T(8,128)(2,1)S(1)} %broadcast_select_fusion.1, s32[256]{0:T(256)S(1)} %fusion.111), kind=kCustom, calls=%fused_computation.3 | custom fusion | bytes 264192 | tf_op jit(solution)/shard_map/jit(take_along_axis)/gather | solution.py:125
  14.9 1.9 %collective-permute-start.2 = (bf16[2,128,512]{2,1,0:T(8,128)(2,1)}, bf16[2,128,512]{2,1,0:T(8,128)(2,1)S(1)}, u32[]{:S(2)}, u32[]{:S(2)}) collective-permute-start(bf16[2,128,512]{2,1,0:T(8,128)(2,1)} %pad_maximum_fusion.2), channel_id=1, source_target_pairs={{0,16},{4,20},{8,24},{12,28},{16,32},{20,36},{24,40},{28,44},{32,4... | collective-permute-start | bytes 786440 | tf_op jit(solution)/shard_map/ppermute | solution.py:26
  16.7 1.3 collective-permute-start.3
  18.0 2.1 %collective-permute-start.4 = (bf16[2,128,512]{2,1,0:T(8,128)(2,1)}, bf16[2,128,512]{2,1,0:T(8,128)(2,1)}, u32[]{:S(2)}, u32[]{:S(2)}) collective-permute-start(bf16[2,128,512]{2,1,0:T(8,128)(2,1)} %pad_maximum_fusion.2), channel_id=1, source_target_pairs={{0,8},{4,12},{8,16},{12,20},{16,24},{20,28},{24,32},{28,36},{32,40... | collective-permute-start | bytes 786440 | tf_op jit(solution)/shard_map/ppermute | solution.py:26
  20.8 1.0 collective-permute-start.6
  27.6 1.7 %multiply_reduce_fusion.4 = (f32[8,128]{1,0:T(8,128)}, bf16[8,128,256]{2,1,0:T(8,128)(2,1)S(1)}) fusion(bf16[8,128,256]{2,1,0:T(8,128)(2,1)S(1)} %bitcast.236, pred[8,128]{1,0:T(8,128)(4,1)} %copy-done.9), kind=kLoop, calls=%fused_computation.68 | loop fusion | flops 1047552 | bytes 1053696 | tf_op jit(solution)/shard_map/reduce_sum | solution.py:33
  30.7 1.0 pad_maximum_fusion.1
  31.7 2.1 %fusion.20 = f32[8,256,128]{2,1,0:T(8,128)} fusion(bf16[8,256,128]{2,1,0:T(8,128)(2,1)S(1)} %bitcast.228, bf16[8,256,256]{2,1,0:T(8,128)(2,1)S(1)} %bitcast.232, f32[256,256]{1,0:T(8,128)S(1)} %convert_subtract_fusion, f32[8,256]{1,0:T(8,128)S(1)} %add.261), kind=kOutput, calls=%fused_computation.32 | convolution fusion | flops 406323200 | bytes 2891776 | tf_op jit(solution)/shard_map/lpq,lqc->lpc/dot_general | solution.py:115
  35.4 1.2 compare_convert_fusion
  38.4 2.3 %collective-permute-start.8 = (bf16[2,128,512]{2,1,0:T(8,128)(2,1)}, bf16[2,128,512]{2,1,0:T(8,128)(2,1)S(1)}, u32[]{:S(2)}, u32[]{:S(2)}) collective-permute-start(bf16[2,128,512]{2,1,0:T(8,128)(2,1)} %pad_maximum_fusion.2), channel_id=1, source_target_pairs={{0,244},{4,248},{8,252},{12,0},{16,4},{20,8},{24,12},{28,16},{32,2... | collective-permute-start | bytes 786440 | tf_op jit(solution)/shard_map/ppermute | solution.py:26
  46.1 1.2 collective-permute-start.1
  48.2 3.7 %collective-permute-done.8 = bf16[2,128,512]{2,1,0:T(8,128)(2,1)S(1)} collective-permute-done((bf16[2,128,512]{2,1,0:T(8,128)(2,1)}, bf16[2,128,512]{2,1,0:T(8,128)(2,1)S(1)}, u32[]{:S(2)}, u32[]{:S(2)}) %collective-permute-start.8) | collective-permute-done | bytes 262176 | tf_op jit(solution)/shard_map/ppermute | solution.py:26
  52.0 11.9 %collective-permute-done.9 = bf16[2,128,512]{2,1,0:T(8,128)(2,1)S(1)} collective-permute-done((bf16[2,128,512]{2,1,0:T(8,128)(2,1)}, bf16[2,128,512]{2,1,0:T(8,128)(2,1)S(1)}, u32[]{:S(2)}, u32[]{:S(2)}) %collective-permute-start.9) | collective-permute-done | bytes 262176 | tf_op jit(solution)/shard_map/ppermute | solution.py:26
  63.9 5.0 %gather_fusion.1 = bf16[52,128,512]{2,1,0:T(8,128)(2,1)} fusion(bf16[18,128,512]{2,1,0:T(8,128)(2,1)S(1)} %constant_dynamic-update-slice_fusion, s32[1024]{0:T(1024)S(1)} %pad_clamp_fusion), kind=kCustom, calls=%fused_computation.1 | custom fusion | bytes 13631696 | tf_op jit(solution)/shard_map/gather | solution.py:148
  68.9 4.1 %slice.65 = bf16[1,13,4,128,256]{4,3,2,1,0:T(8,128)(2,1)} slice(bf16[1,13,4,128,512]{4,3,2,1,0:T(8,128)(2,1)} %bitcast.233), slice={[0:1], [0:13], [0:4], [0:128], [0:256]} | slice | bytes 6815744 | tf_op jit(solution)/shard_map/slice | solution.py:149
  73.0 22.7 %gather_fusion.4 = bf16[1664,256]{1,0:T(8,128)(2,1)} fusion(bf16[13,512,256]{2,1,0:T(8,128)(2,1)} %bitcast.230, s32[1664]{0:T(1024)S(1)} %fusion.108), kind=kCustom, calls=%fused_computation.4 | custom fusion | bytes 1717248 | tf_op jit(solution)/shard_map/jit(take_along_axis)/gather | solution.py:157
  95.8 2.4 %broadcast_select_fusion = bf16[1,13,128,256]{3,2,1,0:T(8,128)(2,1)} fusion(bf16[1,13,128,256]{3,2,1,0:T(8,128)(2,1)} %bitcast.237, pred[13,128]{1,0:T(8,128)(4,1)S(1)} %copy-done.10), kind=kLoop, calls=%fused_computation.76 | loop fusion | flops 425984 | bytes 1705600 | tf_op jit(solution)/shard_map/jit(take_along_axis)/select_n | solution.py:157
  98.1 1.4 %multiply_reduce_fusion.3 = f32[12,128]{1,0:T(8,128)S(1)} fusion(bf16[1,13,128,256]{3,2,1,0:T(8,128)(2,1)} %broadcast_select_fusion), kind=kLoop, calls=%fused_computation.28 | loop fusion | flops 1178112 | bytes 792576 | tf_op jit(solution)/shard_map/reduce_sum | solution.py:34
  99.5 1.5 %multiply_reduce_fusion.6 = f32[128]{0:T(128)} fusion(bf16[1,13,128,256]{3,2,1,0:T(8,128)(2,1)} %broadcast_select_fusion), kind=kLoop, calls=%fused_computation.104 | loop fusion | flops 98176 | bytes 66048 | tf_op jit(solution)/shard_map/reduce_sum | solution.py:33
  101.0 3.4 %fusion.37 = bf16[1,13,128,128]{3,2,1,0:T(8,128)(2,1)} fusion(bf16[1,13,4,128,512]{4,3,2,1,0:T(8,128)(2,1)} %bitcast.234), kind=kOutput, calls=%fused_computation.47 | convolution fusion | flops 218316800 | bytes 3833856 | tf_op jit(solution)/shard_map/umjrs,umjrc->umsc/dot_general | solution.py:154
  104.4 2.6 %fusion.68 = bf16[128,128]{1,0:T(8,128)(2,1)} fusion(bf16[1,13,128,256]{3,2,1,0:T(8,128)(2,1)} %broadcast_select_fusion, bf16[1,13,128,128]{3,2,1,0:T(8,128)(2,1)} %fusion.37, f32[12]{0:T(128)} %compare_convert_fusion, f32[12,128]{1,0:T(8,128)S(1)} %multiply_reduce_fusion.3, f32[128]{0:T(128)} %multiply_reduce_fusion.6), kind=kOutput, calls=%fused_computation.67 | convolution fusion | flops 152387584 | bytes 1285120 | tf_op jit(solution)/shard_map/mkrs,mksc->mrc/dot_general | solution.py:55
  107.1 1.5 %copy.36 = bf16[128,128]{0,1:T(8,128)(2,1)} copy(bf16[128,128]{1,0:T(8,128)(2,1)} %fusion.68) | data formatting | bytes 65536 | tf_op jit(solution)/shard_map/convert_element_type | solution.py:159
  108.5 1.7 %convolution_bitcast_fusion.3 = f32[2,128,128]{2,1,0:T(8,128)} fusion(bf16[2,128,128]{2,1,0:T(8,128)(2,1)} %param.18, bf16[128,128]{0,1:T(8,128)(2,1)} %copy.36), kind=kOutput, calls=%fused_computation.61 | convolution fusion | flops 8388608 | bytes 229376 | tf_op jit(solution)/shard_map/nrs,nsc->nrc/dot_general | solution.py:164
  110.2 1.0 multiply_reduce_fusion.1
  111.2 2.9 %fusion.63 = bf16[2,128,128]{2,1,0:T(8,128)(2,1)} fusion(f32[2,128,128]{2,1,0:T(8,128)} %convolution_bitcast_fusion.3, f32[2,18]{1,0:T(2,128)} %fusion.103, f32[18,128]{1,0:T(8,128)} %multiply_reduce_fusion.1, f32[2,128]{1,0:T(2,128)S(1)} %copy-done.14, bf16[18,128,512]{2,1,0:T(8,128)(2,1)S(1)} %constant_dynamic-update-slice_fusion, ...), kind=kOutput, calls=%fused_computation.63 | convolution fusion | flops 457179136 | bytes 2107536 | tf_op jit(solution)/shard_map/mjrs,jsc->mrc/dot_general | solution.py:74
  115.1 2.0 %convolution_bitcast_fusion.1 = f32[8,128,128]{2,1,0:T(8,128)} fusion(bf16[8,128,128]{1,2,0:T(8,128)(2,1)S(1)} %bitcast.239, bf16[8,128,128]{2,1,0:T(8,128)(2,1)} %param.17), kind=kOutput, calls=%fused_computation.45 | convolution fusion | flops 33554432 | bytes 1048576 | tf_op jit(solution)/shard_map/lrs,lsc->lrc/dot_general | solution.py:173
  117.1 1.8 %pad_maximum_fusion = bf16[24,128,384]{2,1,0:T(8,128)(2,1)S(1)} fusion(bf16[8,128,384]{2,1,0:T(8,128)(2,1)} %collective-permute-done.1, bf16[8,128,128]{2,1,0:T(8,128)(2,1)} %copy-done.2, bf16[8,128,256]{2,1,0:T(8,128)(2,1)S(1)} %get-tuple-element.28, bf16[8,128,384]{2,1,0:T(8,128)(2,1)} %collective-permute-done), kind=kLoop, calls=%fused_computation.14 | loop fusion | flops 9437184 | bytes 4718592 | tf_op jit(solution)/shard_map/concatenate | solution.py:19
  119.4 7.0 %fusion.43 = bf16[8,128,128]{2,1,0:T(8,128)(2,1)} fusion(f32[8,128,128]{2,1,0:T(8,128)} %convolution_bitcast_fusion.1, f32[8,24]{1,0:T(8,128)S(1)} %convert_reduce_fusion, f32[24,128]{1,0:T(8,128)S(1)} %multiply_reduce_fusion, f32[8,128]{1,0:T(8,128)S(1)} %copy-done.13, bf16[24,128,384]{2,1,0:T(8,128)(2,1)S(1)} %pad_maximum_fusion, ...), kind=kOutput, calls=%fused_computation.49 | convolution fusion | flops 2441347072 | bytes 5263360 | tf_op jit(solution)/shard_map/mjrs,jsc->mrc/dot_general | solution.py:74
  126.4 2.5 %fusion.23 = bf16[8,256,128]{2,1,0:T(8,128)(2,1)} fusion(f32[8,256,128]{2,1,0:T(8,128)} %fusion.20, bf16[8,256,128]{2,1,0:T(8,128)(2,1)} %param.16, bf16[8,128,128]{2,1,0:T(8,128)(2,1)} %fusion.43), kind=kOutput, calls=%fused_computation.36 | convolution fusion | flops 67633152 | bytes 2359296 | tf_op jit(solution)/shard_map/lpr,lrc->lpc/dot_general | solution.py:180
  (100 shorter events, 23.7 us)
Async XLA Ops:
  0.0 2.9 %copy-start = (bf16[2048,128]{1,0:T(8,128)(2,1)S(1)}, bf16[2048,128]{1,0:T(8,128)(2,1)}, u32[]{:S(2)}) copy-start(bf16[2048,128]{1,0:T(8,128)(2,1)} %param.15) | copy-start | bytes 1572868
  0.0 5.6 %copy-start.1 = (bf16[2048,256]{1,0:T(8,128)(2,1)S(1)}, bf16[2048,256]{1,0:T(8,128)(2,1)}, u32[]{:S(2)}) copy-start(bf16[2048,256]{1,0:T(8,128)(2,1)} %param.14) | copy-start | bytes 3145732
  1.5 4.1 %copy-start.9 = (pred[8,128]{1,0:T(8,128)(4,1)}, pred[8,128]{1,0:T(8,128)(4,1)S(1)}, u32[]{:S(2)}) copy-start(pred[8,128]{1,0:T(8,128)(4,1)S(1)} %compare_and_fusion.1) | copy-start | bytes 3076
  5.6 8.5 %copy-start.4 = (bf16[2,128,128]{2,1,0:T(8,128)(2,1)}, bf16[2,128,128]{2,1,0:T(8,128)(2,1)S(1)}, u32[]{:S(2)}) copy-start(bf16[2,128,128]{2,1,0:T(8,128)(2,1)S(1)} %copy.31) | copy-start | bytes 196612
  11.4 2.7 %copy-start.3 = (bf16[2,128,128]{2,1,0:T(8,128)(2,1)S(1)}, bf16[2,128,128]{2,1,0:T(8,128)(2,1)}, u32[]{:S(2)}) copy-start(bf16[2,128,128]{2,1,0:T(8,128)(2,1)} %param.18) | copy-start | bytes 196612
  11.5 10.4 %copy-start.11 = (s32[32,12]{0,1:T(8,128)S(1)}, s32[32,12]{0,1:T(8,128)}, u32[]{:S(2)}) copy-start(s32[32,12]{0,1:T(8,128)} %param.26) | copy-start | bytes 4612
  11.5 10.6 %copy-start.5 = (s32[32,128]{1,0:T(8,128)S(1)}, s32[32,128]{1,0:T(8,128)}, u32[]{:S(2)}) copy-start(s32[32,128]{1,0:T(8,128)} %param.21) | copy-start | bytes 49156
  11.5 14.8 %copy-start.15 = (s32[2,12]{1,0:T(2,128)S(1)}, s32[2,12]{1,0:T(2,128)}, u32[]{:S(2)}) copy-start(s32[2,12]{1,0:T(2,128)} %param.24) | copy-start | bytes 292
  11.5 15.5 %copy-start.16 = (s32[2]{0:T(128)S(1)}, s32[2]{0:T(128)}, u32[]{:S(2)}) copy-start(s32[2]{0:T(128)} %param.25) | copy-start | bytes 28
  14.9 21.8 %collective-permute-start.2 = (bf16[2,128,512]{2,1,0:T(8,128)(2,1)}, bf16[2,128,512]{2,1,0:T(8,128)(2,1)S(1)}, u32[]{:S(2)}, u32[]{:S(2)}) collective-permute-start(bf16[2,128,512]{2,1,0:T(8,128)(2,1)} %pad_maximum_fusion.2), channel_id=1, source_target_pairs={{0,16},{4,20},{8,24},{12,28},{16,32},{20,36},{24,40},{28,44},{32,4... | collective-permute-start | bytes 786440 | tf_op jit(solution)/shard_map/ppermute | solution.py:26
  16.7 21.6 %collective-permute-start.3 = (bf16[2,128,512]{2,1,0:T(8,128)(2,1)}, bf16[2,128,512]{2,1,0:T(8,128)(2,1)}, u32[]{:S(2)}, u32[]{:S(2)}) collective-permute-start(bf16[2,128,512]{2,1,0:T(8,128)(2,1)} %pad_maximum_fusion.2), channel_id=1, source_target_pairs={{0,12},{4,16},{8,20},{12,24},{16,28},{20,32},{24,36},{28,40},{32,4... | collective-permute-start | bytes 786440 | tf_op jit(solution)/shard_map/ppermute | solution.py:26
  18.0 23.6 %collective-permute-start.4 = (bf16[2,128,512]{2,1,0:T(8,128)(2,1)}, bf16[2,128,512]{2,1,0:T(8,128)(2,1)}, u32[]{:S(2)}, u32[]{:S(2)}) collective-permute-start(bf16[2,128,512]{2,1,0:T(8,128)(2,1)} %pad_maximum_fusion.2), channel_id=1, source_target_pairs={{0,8},{4,12},{8,16},{12,20},{16,24},{20,28},{24,32},{28,36},{32,40... | collective-permute-start | bytes 786440 | tf_op jit(solution)/shard_map/ppermute | solution.py:26
  20.1 23.2 %collective-permute-start.5 = (bf16[2,128,512]{2,1,0:T(8,128)(2,1)}, bf16[2,128,512]{2,1,0:T(8,128)(2,1)}, u32[]{:S(2)}, u32[]{:S(2)}) collective-permute-start(bf16[2,128,512]{2,1,0:T(8,128)(2,1)} %pad_maximum_fusion.2), channel_id=1, source_target_pairs={{0,4},{4,8},{8,12},{12,16},{16,20},{20,24},{24,28},{28,32},{32,36}... | collective-permute-start | bytes 786440 | tf_op jit(solution)/shard_map/ppermute | solution.py:26
  20.8 25.3 %collective-permute-start.6 = (bf16[2,128,512]{2,1,0:T(8,128)(2,1)}, bf16[2,128,512]{2,1,0:T(8,128)(2,1)}, u32[]{:S(2)}, u32[]{:S(2)}) collective-permute-start(bf16[2,128,512]{2,1,0:T(8,128)(2,1)} %pad_maximum_fusion.2), channel_id=1, source_target_pairs={{0,252},{4,0},{8,4},{12,8},{16,12},{20,16},{24,20},{28,24},{32,28}... | collective-permute-start | bytes 786440 | tf_op jit(solution)/shard_map/ppermute | solution.py:26
  24.0 9.8 %copy-start.2 = (bf16[8,128,128]{2,1,0:T(8,128)(2,1)}, bf16[8,128,128]{2,1,0:T(8,128)(2,1)S(1)}, u32[]{:S(2)}) copy-start(bf16[8,128,128]{2,1,0:T(8,128)(2,1)S(1)} %copy.28) | copy-start | bytes 786436
  31.7 2.1 %copy-start.7 = (s32[2,12]{0,1:T(8,128)S(1)}, s32[2,12]{0,1:T(8,128)}, u32[]{:S(2)}) copy-start(s32[2,12]{0,1:T(8,128)} %copy.32) | copy-start | bytes 292
  31.7 2.1 %copy-start.12 = (pred[2,12]{0,1:T(8,128)(4,1)S(1)}, pred[2,12]{0,1:T(8,128)(4,1)}, u32[]{:S(2)}) copy-start(pred[2,12]{0,1:T(8,128)(4,1)} %iota_compare_fusion.1) | copy-start | bytes 76
  31.7 2.1 %copy-start.18 = (pred[18]{0:T(512)(128)(4,1)S(1)}, pred[18]{0:T(512)(128)(4,1)}, u32[]{:S(2)}) copy-start(pred[18]{0:T(512)(128)(4,1)} %iota_compare_fusion.3) | copy-start | bytes 58
  31.7 2.2 %copy-start.19 = (s32[18]{0:T(128)S(1)}, s32[18]{0:T(128)}, u32[]{:S(2)}) copy-start(s32[18]{0:T(128)} %and_select_fusion) | copy-start | bytes 220
  31.7 2.9 %copy-start.17 = (pred[24]{0:T(512)(128)(4,1)S(1)}, pred[24]{0:T(512)(128)(4,1)}, u32[]{:S(2)}) copy-start(pred[24]{0:T(512)(128)(4,1)} %iota_compare_fusion.4) | copy-start | bytes 76
  31.7 2.9 %copy-start.8 = (s32[1,13,4,1]{2,1,3,0:T(8,128)S(1)}, s32[1,13,4,1]{2,1,3,0:T(8,128)}, u32[]{:S(2)}) copy-start(s32[1,13,4,1]{2,1,3,0:T(8,128)} %compare_select_fusion.1) | copy-start | bytes 628
  31.7 3.0 %copy-start.20 = (s32[32]{0:T(128)S(1)}, s32[32]{0:T(128)}, u32[]{:S(2)}) copy-start(s32[32]{0:T(128)} %param.27) | copy-start | bytes 388
  36.6 0.7 copy-start.6
  37.4 10.8 %collective-permute-start.7 = (bf16[2,128,512]{2,1,0:T(8,128)(2,1)}, bf16[2,128,512]{2,1,0:T(8,128)(2,1)S(1)}, u32[]{:S(2)}, u32[]{:S(2)}) collective-permute-start(bf16[2,128,512]{2,1,0:T(8,128)(2,1)} %pad_maximum_fusion.2), channel_id=1, source_target_pairs={{0,248},{4,252},{8,0},{12,4},{16,8},{20,12},{24,16},{28,20},{32,24... | collective-permute-start | bytes 786440 | tf_op jit(solution)/shard_map/ppermute | solution.py:26
  38.4 13.6 %collective-permute-start.8 = (bf16[2,128,512]{2,1,0:T(8,128)(2,1)}, bf16[2,128,512]{2,1,0:T(8,128)(2,1)S(1)}, u32[]{:S(2)}, u32[]{:S(2)}) collective-permute-start(bf16[2,128,512]{2,1,0:T(8,128)(2,1)} %pad_maximum_fusion.2), channel_id=1, source_target_pairs={{0,244},{4,248},{8,252},{12,0},{16,4},{20,8},{24,12},{28,16},{32,2... | collective-permute-start | bytes 786440 | tf_op jit(solution)/shard_map/ppermute | solution.py:26
  41.6 22.2 %collective-permute-start.9 = (bf16[2,128,512]{2,1,0:T(8,128)(2,1)}, bf16[2,128,512]{2,1,0:T(8,128)(2,1)S(1)}, u32[]{:S(2)}, u32[]{:S(2)}) collective-permute-start(bf16[2,128,512]{2,1,0:T(8,128)(2,1)} %pad_maximum_fusion.2), channel_id=1, source_target_pairs={{0,240},{4,244},{8,248},{12,252},{16,0},{20,4},{24,8},{28,12},{32,... | collective-permute-start | bytes 786440 | tf_op jit(solution)/shard_map/ppermute | solution.py:26
  43.3 73.8 %collective-permute-start = (bf16[8,128,384]{2,1,0:T(8,128)(2,1)}, bf16[8,128,384]{2,1,0:T(8,128)(2,1)}, u32[]{:S(2)}, u32[]{:S(2)}) collective-permute-start(bf16[8,128,384]{2,1,0:T(8,128)(2,1)} %pad_maximum_fusion.1), channel_id=1, source_target_pairs={{0,4},{4,8},{8,12},{12,16},{16,20},{20,24},{24,28},{28,32},{32,36}... | collective-permute-start | bytes 2359304 | tf_op jit(solution)/shard_map/ppermute | solution.py:15
  46.1 71.0 %collective-permute-start.1 = (bf16[8,128,384]{2,1,0:T(8,128)(2,1)}, bf16[8,128,384]{2,1,0:T(8,128)(2,1)}, u32[]{:S(2)}, u32[]{:S(2)}) collective-permute-start(bf16[8,128,384]{2,1,0:T(8,128)(2,1)} %pad_maximum_fusion.1), channel_id=1, source_target_pairs={{4,0},{8,4},{12,8},{16,12},{20,16},{24,20},{28,24},{32,28},{36,32}... | collective-permute-start | bytes 2359304 | tf_op jit(solution)/shard_map/ppermute | solution.py:18
  73.0 22.7 %copy-start.10 = (pred[13,128]{1,0:T(8,128)(4,1)S(1)}, pred[13,128]{1,0:T(8,128)(4,1)}, u32[]{:S(2)}) copy-start(pred[13,128]{1,0:T(8,128)(4,1)} %compare_and_fusion) | copy-start | bytes 4996
  104.4 6.7 %copy-start.14 = (f32[2,128]{1,0:T(2,128)S(1)}, f32[2,128]{1,0:T(2,128)}, u32[]{:S(2)}) copy-start(f32[2,128]{1,0:T(2,128)} %get-tuple-element.29) | copy-start | bytes 3076
  117.1 2.3 %copy-start.13 = (f32[8,128]{1,0:T(8,128)S(1)}, f32[8,128]{1,0:T(8,128)}, u32[]{:S(2)}) copy-start(f32[8,128]{1,0:T(8,128)} %get-tuple-element.27) | copy-start | bytes 12292
where the time goes:
time: 130 us; the launch traced here: 129 us
  local copies, waits for them, and re-layouts  50.7 us (39%)
  matrix products  26.8 us (21%)
  other arithmetic  23.4 us (18%)
  waiting for transfers between devices  15.6 us (12%)
  starting transfers between devices  12 us (9%)
    gather x1, local copies, waits for them, and re-layouts, per_device(): jnp.take_along_axis(child_pts, upper_skeleton[members][:, :, :, None], ax...  22.7 us
    ppermute x8, waiting for transfers between devices, shifted(): return lax.ppermute(value, axis, pairs)  15.6 us
    ppermute x8, starting transfers between devices, shifted(): return lax.ppermute(value, axis, pairs)  9.93 us
    dot_general x2, matrix products, apply_window(): jnp.einsum('mjrs,jsc->mrc', blocks, window_charges, preferred_element_typ...  9.86 us
    unnamed x51, local copies, waits for them, and re-layouts  7.14 us
    gather x1, local copies, waits for them, and re-layouts, per_device(): jnp.take_along_axis(leaf_points, leaf_skeleton[:, :, None], axis=1)  5.8 us
    gather x1, local copies, waits for them, and re-layouts, per_device(): child_data = window[jnp.mod(children - window_start, total_nodes)]  4.95 us
    reduce_sum x4, other arithmetic, kernel_block(): left_sq = jnp.sum(jnp.square(left_pts.astype(jnp.float32)), -1)  4.33 us
  transfers between devices with their start and end apart: 10, of which 2 were waited for; matrix products, arithmetic and copies ran while one was open for 57% of the time, Pallas kernels for 0%

commit v1 on v0

v1 whole, which is shorter than its diff:
```python
import functools
import math

import jax
import jax.numpy as jnp
from jax import lax
from jax.experimental import pallas as pl
from jax.experimental.pallas import tpu as pltpu
from jax.sharding import PartitionSpec as P

NEG = -1e38
VMEM = pltpu.VMEM
SMEM = pltpu.SMEM
LIMIT = 48 * 1024 * 1024


def mm(a, b):
    return jnp.dot(a, b, preferred_element_type=jnp.float32)


def mm_nt(a, b):
    return lax.dot_general(a, b, (((1,), (1,)), ((), ())), preferred_element_type=jnp.float32)


def mm_tn(a, b):
    return lax.dot_general(a, b, (((0,), (0,)), ((), ())), preferred_element_type=jnp.float32)


def scale_of(features):
    return math.log2(math.e) / math.sqrt(8.0 * features)


def split_squares(pts):
    wide = pts.astype(jnp.float32)
    square = wide * wide
    high = square.astype(jnp.bfloat16)
    low = (square - high.astype(jnp.float32)).astype(jnp.bfloat16)
    return high, low


def col_term(high, low):
    features = high.shape[1]
    ones = jnp.ones((features, 128), jnp.bfloat16)
    return scale_of(features) * (features - (mm(high, ones) + mm(low, ones)))


def row_term(high, low):
    features = high.shape[1]
    ones = jnp.ones((8, features), jnp.bfloat16)
    return scale_of(features) * (features - (mm_nt(ones, high) + mm_nt(ones, low)))


def wide(col, lanes):
    return jnp.concatenate([col] * (lanes // 128), axis=1)


def hits(far, counts, first):
    rows, slots = far.shape
    ids = lax.broadcasted_iota(jnp.int32, (rows, 128), 1) + first
    found = jnp.zeros((rows, 128), jnp.float32)
    for k in range(slots):
        same = (far[:, k : k + 1] == ids) & (counts > k)
        found = jnp.where(same, 1.0, found)
    return found


def count_column(count_ref, rows):
    spot = lax.broadcasted_iota(jnp.int32, (rows, 128), 0)
    column = jnp.zeros((rows, 128), jnp.int32)
    for t in range(rows):
        column = jnp.where(spot == t, count_ref[t], column)
    return column


def one_hot_rows(index_columns, at, choices):
    spots = lax.broadcasted_iota(jnp.int32, (index_columns.shape[0], choices), 1)
    same = index_columns[:, at : at + 1] == spots
    return jnp.where(same, 1.0, 0.0).astype(jnp.bfloat16)


def neighbours(cores_axis_size):
    me = lax.axis_index("leaf")
    core = lax.rem(me, 2)
    chips = cores_axis_size // 2
    chip = me // 2
    step = 2 * core - 1
    side_b = lax.rem(chip + step + chips, chips)
    side_a = lax.rem(chip - step + chips, chips)
    return me, core, chip, side_a, side_b


def front_kernel(
    points_ref, weights_ref, basis_ref, lt_ref, t_ref, ls_ref, ns_ref, leaf_ref, node_ref
):
    leaves, rows, rank = basis_ref.shape
    nodes = t_ref.shape[0]
    features = points_ref.shape[1]
    cols = weights_ref.shape[1]
    leaf_columns = jnp.transpose(ls_ref[...])
    node_columns = jnp.transpose(jnp.concatenate([ns_ref[...]] * 4, axis=0))
    for leaf in range(leaves):
        own = slice(leaf * rank, (leaf + 1) * rank)
        pts = points_ref[leaf * rows : (leaf + 1) * rows, :]
        picked = mm(one_hot_rows(leaf_columns, leaf, rows), pts)
        leaf_ref[own, 0:features] = picked.astype(jnp.bfloat16)
        charge = mm_tn(basis_ref[leaf], weights_ref[leaf * rows : (leaf + 1) * rows, :])
        leaf_ref[own, features : features + cols] = charge.astype(jnp.bfloat16)
    for node in range(nodes):
        own = slice(node * rank, (node + 1) * rank)
        kids = slice(node * 4 * rank, (node + 1) * 4 * rank)
        picked = mm(one_hot_rows(node_columns, node, 4 * rank), leaf_ref[kids, 0:features])
        node_ref[own, 0:features] = picked.astype(jnp.bfloat16)
        transfer = lt_ref[node * 4 : node * 4 + 4].reshape(4 * rank, rank)
        charge = mm_tn(transfer, leaf_ref[kids, features : features + cols])
        node_ref[own, features : features + cols] = charge.astype(jnp.bfloat16)
        node_ref[own, features + cols :] = t_ref[node]


def upper_kernel(own_ref, other_ref, us_ref, out_ref, stacked, *, total):
    _, core, chip, _, _ = neighbours(total)
    half, width = own_ref.shape
    kept = out_ref.shape[1]
    rank = width - kept
    features = kept - rank
    mine = pl.multiple_of(core * half, half)
    theirs = pl.multiple_of((1 - core) * half, half)
    stacked[pl.ds(mine, half), :] = own_ref[...]
    stacked[pl.ds(theirs, half), :] = other_ref[...]
    out_ref[0 : 2 * half, :] = stacked[:, 0:kept]
    index = us_ref[pl.ds(chip, 1), :]
    columns = jnp.transpose(jnp.broadcast_to(index, (8, index.shape[1])))
    picked = mm(one_hot_rows(columns, 0, 2 * half), stacked[:, 0:features])
    out_ref[2 * half :, 0:features] = picked.astype(jnp.bfloat16)
    charge = mm_tn(stacked[:, kept:], stacked[:, features:kept])
    out_ref[2 * half :, features:] = charge.astype(jnp.bfloat16)


def near_kernel(points_ref, weights_ref, out_ref, *, rows):
    features = points_ref.shape[1]
    same = lax.broadcasted_iota(jnp.int32, (rows, rows), 0) == lax.broadcasted_iota(
        jnp.int32, (rows, rows), 1
    )
    for leaf in range(points_ref.shape[0] // rows):
        own = slice(leaf * rows, (leaf + 1) * rows)
        pts = points_ref[own, :]
        high, low = split_squares(pts)
        inner = mm_nt(pts, pts)
        power = (
            inner * (2.0 * scale_of(features))
            + wide(col_term(high, low), rows)
            + row_term(high, low)[0:1]
        )
        tile = jnp.exp2(jnp.where(same, NEG, power)).astype(jnp.bfloat16)
        out_ref[own, :] = mm(tile, weights_ref[own, :])


def unit(left, col, right, row_top, row_bottom, charge):
    features = left.shape[1]
    power = mm_nt(left, right) * (2.0 * scale_of(features)) + wide(col, right.shape[0])
    half = left.shape[0] // 2
    block = jnp.concatenate(
        [jnp.exp2(power[:half] + row_top), jnp.exp2(power[half:] + row_bottom)], axis=0
    )
    return mm(block.astype(jnp.bfloat16), charge)


def fill_rows(source_ref, rows_ref, found, features):
    for group in range(rows_ref.shape[0]):
        high, low = split_squares(source_ref[group * 256 : (group + 1) * 256, 0:features])
        term = row_term(high, low)[0 : found.shape[0]]
        for half in range(2):
            j = group * 2 + half
            lanes = slice(half * 128, half * 128 + 128)
            rows_ref[group, :, lanes] = jnp.where(found[:, j : j + 1] > 0.0, term[:, lanes], NEG)


def own_far_kernel(
    leaf_ref, side_ref, far_ref, nodes_ref, nfar_ref, count_ref, ncount_ref,
    pot_ref, npot_ref, own_rows, side_rows, node_rows, *, total,
):
    me, core, chip, _, _ = neighbours(total)
    features = leaf_ref.shape[1] - pot_ref.shape[1]
    targets = far_ref.shape[0]
    counts = count_column(count_ref, targets)
    fill_rows(leaf_ref, own_rows, hits(far_ref[...], counts, me * targets), features)
    other = me + 1 - 2 * core
    fill_rows(side_ref, side_rows, hits(far_ref[...], counts, other * targets), features)
    groups = targets // 2
    for group in range(groups):
        at = group + core * (groups - 1 - 2 * group)
        own = pl.ds(pl.multiple_of(at * 256, 256), 256)
        left = leaf_ref[own, 0:features]
        col = col_term(*split_squares(left))
        total_here = jnp.zeros((256, pot_ref.shape[1]), jnp.float32)
        for source in range(groups):
            here = slice(source * 256, source * 256 + 256)
            total_here += unit(
                left, col, leaf_ref[here, 0:features],
                own_rows[source, pl.ds(2 * at, 1), :],
                own_rows[source, pl.ds(2 * at + 1, 1), :],
                leaf_ref[here, features:],
            )
        for source in range(group + 1):
            src = source + core * (groups - 1 - 2 * source)
            here = pl.ds(pl.multiple_of(src * 256, 256), 256)
            total_here += unit(
                left, col, side_ref[here, 0:features],
                side_rows[src, pl.ds(2 * at, 1), :],
                side_rows[src, pl.ds(2 * at + 1, 1), :],
                side_ref[here, features:],
            )
        pot_ref[own, :] = total_here
    ncounts = count_column(ncount_ref, 2)
    fill_rows(nodes_ref, node_rows, hits(nfar_ref[...], ncounts, chip * 4), features)
    left = nodes_ref[pl.ds(pl.multiple_of(core * 256, 256), 256), 0:features]
    col = col_term(*split_squares(left))
    total_here = jnp.zeros((256, pot_ref.shape[1]), jnp.float32)
    for source in range(2):
        here = slice(source * 256, source * 256 + 256)
        total_here += unit(
            left, col, nodes_ref[here, 0:features],
            node_rows[source, 0:1, :], node_rows[source, 1:2, :], nodes_ref[here, features:],
        )
    npot_ref[...] = total_here


def rim_far_kernel(
    leaf_ref, rim_ref, far_ref, start_ref, count_ref, pot_ref, rim_rows, *, total
):
    me, core, _, _, _ = neighbours(total)
    features = leaf_ref.shape[1] - pot_ref.shape[1]
    targets = far_ref.shape[0]
    counts = count_column(count_ref, targets)
    partner = lax.rem(me + 2 * core - 1 + total, total)
    fill_rows(rim_ref, rim_rows, hits(far_ref[...], counts, partner * targets), features)
    groups = targets // 2
    for group in range(groups):
        at = group + core * (groups - 1 - 2 * group)
        own = pl.ds(pl.multiple_of(at * 256, 256), 256)
        left = leaf_ref[own, 0:features]
        col = col_term(*split_squares(left))
        total_here = start_ref[own, :]
        for source in range(group, groups):
            src = source + core * (groups - 1 - 2 * source)
            here = pl.ds(pl.multiple_of(src * 256, 256), 256)
            total_here += unit(
                left, col, rim_ref[here, 0:features],
                rim_rows[src, pl.ds(2 * at, 1), :],
                rim_rows[src, pl.ds(2 * at + 1, 1), :],
                rim_ref[here, features:],
            )
        pot_ref[own, :] = total_here


def last_kernel(
    near_ref, pot_ref, npot_ref, nodes_ref, side_b_ref, side_a_ref, nfar_ref,
    t_ref, lt_ref, basis_ref, ncount_ref, ufar_ref, ucount_ref,
    out_ref, rows_b, rows_a, *, total,
):
    _, core, chip, side_a, side_b = neighbours(total)
    cols = pot_ref.shape[1]
    features = nodes_ref.shape[1] - cols
    own_upper = nodes_ref[512:640, 0:features]
    upper_col = col_term(*split_squares(own_upper))
    live = ucount_ref[chip]
    far2 = jnp.zeros((128, cols), jnp.float32)
    for ref, ident in ((side_b_ref, side_b), (side_a_ref, side_a)):
        source = ref[512:640, 0:features]
        used = jnp.int32(0)
        for k in range(ufar_ref.shape[1]):
            used = jnp.where((ufar_ref[chip, k] == ident) & (k < live), 1, used)
        row = jnp.where(used > 0, row_term(*split_squares(source))[0:1], NEG)
        power = mm_nt(own_upper, source) * (2.0 * scale_of(features)) + upper_col + row
        far2 += mm(jnp.exp2(power).astype(jnp.bfloat16), ref[512:640, features:])
    down2 = far2.astype(jnp.bfloat16)
    ncounts = count_column(ncount_ref, 2)
    left = nodes_ref[pl.ds(pl.multiple_of(core * 256, 256), 256), 0:features]
    col = col_term(*split_squares(left))
    far1 = npot_ref[...]
    for ref, ident, rows_ref in ((side_b_ref, side_b, rows_b), (side_a_ref, side_a, rows_a)):
        fill_rows(ref, rows_ref, hits(nfar_ref[...], ncounts, ident * 4), features)
        for source in range(2):
            here = slice(source * 256, source * 256 + 256)
            far1 += unit(
                left, col, ref[here, 0:features],
                rows_ref[source, 0:1, :], rows_ref[source, 1:2, :], ref[here, features:],
            )
    leaves, rows, rank = basis_ref.shape
    for node in range(2):
        down1 = (far1[node * 128 : node * 128 + 128] + mm(t_ref[node], down2)).astype(jnp.bfloat16)
        for leaf in range(node * 4, node * 4 + 4):
            down0 = pot_ref[leaf * rank : (leaf + 1) * rank, :] + mm(lt_ref[leaf], down1)
            own = slice(leaf * rows, (leaf + 1) * rows)
            result = near_ref[own, :] + mm(basis_ref[leaf], down0.astype(jnp.bfloat16))
            out_ref[own, :] = result.astype(jnp.bfloat16)


def call(kernel, outs, args, smem=0, scratch=(), mmacs=0, name=None):
    n = len(args) - smem
    bytes_moved = sum(a.size * a.dtype.itemsize for a in list(args) + list(outs))
    return pl.pallas_call(
        kernel,
        out_shape=outs,
        in_specs=[pl.BlockSpec(memory_space=VMEM)] * n + [pl.BlockSpec(memory_space=SMEM)] * smem,
        out_specs=[pl.BlockSpec(memory_space=VMEM)] * len(outs),
        scratch_shapes=list(scratch),
        compiler_params=pltpu.CompilerParams(vmem_limit_bytes=LIMIT),
        cost_estimate=pl.CostEstimate(
            flops=int(2e6 * mmacs), bytes_accessed=int(bytes_moved), transcendentals=0
        ),
        name=name,
    )(*args)


def per_device(
    points, weights, leaf_basis, leaf_transfer, node_transfer, leaf_skeleton, node_skeleton,
    upper_skeleton, leaf_far, leaf_count, node_far, node_count, upper_far, upper_count,
):
    leaves, rows, rank = leaf_basis.shape
    features = points.shape[1]
    cols = weights.shape[1]
    total = lax.axis_size("leaf")
    pack = features + cols
    bf16, f32 = jnp.bfloat16, jnp.float32
    across = [(d, d ^ 1) for d in range(total)]
    outward = [(d, (d + 1) % total if d % 2 else (d - 1) % total) for d in range(total)]
    shape = jax.ShapeDtypeStruct

    leaf_pack, node_pack = call(
        front_kernel,
        [shape((leaves * rank, pack), bf16), shape((2 * rank, pack + rank), bf16)],
        [points, weights, leaf_basis, leaf_transfer, node_transfer, leaf_skeleton, node_skeleton],
        mmacs=250, name="front",
    )
    other_nodes = lax.ppermute(node_pack, "leaf", across)
    rim = lax.ppermute(leaf_pack, "leaf", outward)
    side = lax.ppermute(leaf_pack, "leaf", across)
    (nodes,) = call(
        functools.partial(upper_kernel, total=total),
        [shape((5 * rank, pack), bf16)],
        [node_pack, other_nodes, upper_skeleton],
        scratch=[pltpu.VMEM((4 * rank, pack + rank), bf16)],
        mmacs=30, name="upper",
    )
    nodes_b = lax.ppermute(nodes, "leaf", outward)
    nodes_a = lax.ppermute(nodes_b, "leaf", across)
    (near,) = call(
        functools.partial(near_kernel, rows=rows),
        [shape((leaves * rows, cols), f32)],
        [points, weights],
        mmacs=1500, name="near",
    )
    pot_start, node_pot = call(
        functools.partial(own_far_kernel, total=total),
        [shape((leaves * rank, cols), f32), shape((2 * rank, cols), f32)],
        [leaf_pack, side, leaf_far, nodes, node_far, leaf_count, node_count],
        smem=2,
        scratch=[
            pltpu.VMEM((leaves // 2, leaves, 256), f32),
            pltpu.VMEM((leaves // 2, leaves, 256), f32),
            pltpu.VMEM((2, 2, 256), f32),
        ],
        mmacs=2000, name="own_far",
    )
    (pot,) = call(
        functools.partial(rim_far_kernel, total=total),
        [shape((leaves * rank, cols), f32)],
        [leaf_pack, rim, leaf_far, pot_start, leaf_count],
        smem=1,
        scratch=[pltpu.VMEM((leaves // 2, leaves, 256), f32)],
        mmacs=1000, name="rim_far",
    )
    (out,) = call(
        functools.partial(last_kernel, total=total),
        [shape((leaves * rows, cols), bf16)],
        [near, pot, node_pot, nodes, nodes_b, nodes_a, node_far, node_transfer, leaf_transfer,
         leaf_basis, node_count, upper_far, upper_count],
        smem=3,
        scratch=[pltpu.VMEM((2, 2, 256), f32), pltpu.VMEM((2, 2, 256), f32)],
        mmacs=500, name="last",
    )
    return out


def solution(mesh):
    placed = (
        P("leaf", None),
        P("leaf", "cols"),
        P("leaf", None, None),
        P("leaf", None, None),
        P("leaf", None, None),
        P("leaf", None),
        P("leaf", None),
        P(),
        P("leaf", None),
        P("leaf"),
        P("leaf", None),
        P("leaf"),
        P(),
        P(),
    )
    return jax.shard_map(
        per_device, mesh=mesh, in_specs=placed, out_specs=P("leaf", "cols"), check_vma=False
    )
```

time: 130 us -> 41.3 us (0.32)
  the two profiles are of different devices: /device:TPU:92 before, /device:TPU:16 now
where the time goes in v1:
time: 41.3 us; the launch traced here: 40.9 us
  Pallas kernels  15.6 us (38%)
  waiting for transfers between devices  9.33 us (23%)
  starting transfers between devices  8.57 us (21%)
  local copies, waits for them, and re-layouts  7.21 us (17%)
    pallas_call x6, Pallas kernels, call(): pl.pallas_call(kernel, out_shape=outs, in_specs=[pl.BlockSpec(memory_spac...  15.6 us
    ppermute x1, starting transfers between devices, per_device(): nodes_b = lax.ppermute(nodes, 'leaf', outward)  7.88 us
    unnamed x39, local copies, waits for them, and re-layouts  7.21 us
    ppermute x1, waiting for transfers between devices, per_device(): nodes_b = lax.ppermute(nodes, 'leaf', outward)  3.8 us
    ppermute x1, waiting for transfers between devices, per_device(): rim = lax.ppermute(leaf_pack, 'leaf', outward)  3.38 us
    ppermute x1, waiting for transfers between devices, per_device(): other_nodes = lax.ppermute(node_pack, 'leaf', across)  2.15 us
  transfers between devices with their start and end apart: 5, of which 3 were waited for; matrix products, arithmetic and copies ran while one was open for 0% of the time, Pallas kernels for 27%

profile of v1, /device:TPU:16, one launch (start us, length us, event | category | flops | bytes accessed | tf_op | source)
XLA Modules:
  0.0 40.9 jit_solution(3001412165045305505)
XLA Ops:
  0.0 1.0 %copy-done = bf16[8,256,128]{2,1,0:T(8,128)(2,1)S(1)} copy-done((bf16[8,256,128]{2,1,0:T(8,128)(2,1)S(1)}, bf16[8,256,128]{2,1,0:T(8,128)(2,1)}, u32[]{:S(2)}) %copy-start) | copy-done | bytes 524312
  1.0 0.9 %copy-done.2 = bf16[8,128,128]{2,1,0:T(8,128)(2,1)S(1)} copy-done((bf16[8,128,128]{2,1,0:T(8,128)(2,1)S(1)}, bf16[8,128,128]{2,1,0:T(8,128)(2,1)}, u32[]{:S(2)}) %copy-start.2) | copy-done | bytes 262168
  2.0 1.2 %copy-done.4 = bf16[2048,256]{1,0:T(8,128)(2,1)S(1)} copy-done((bf16[2048,256]{1,0:T(8,128)(2,1)S(1)}, bf16[2048,256]{1,0:T(8,128)(2,1)}, u32[]{:S(2)}) %copy-start.4) | copy-done | bytes 1048600
  3.2 1.0 %copy-done.6 = bf16[2048,128]{1,0:T(8,128)(2,1)S(1)} copy-done((bf16[2048,128]{1,0:T(8,128)(2,1)S(1)}, bf16[2048,128]{1,0:T(8,128)(2,1)}, u32[]{:S(2)}) %copy-start.6) | copy-done | bytes 524312
  4.3 0.8 %copy-done.8 = bf16[2,128,128]{2,1,0:T(8,128)(2,1)S(1)} copy-done((bf16[2,128,128]{2,1,0:T(8,128)(2,1)S(1)}, bf16[2,128,128]{2,1,0:T(8,128)(2,1)}, u32[]{:S(2)}) %copy-start.8) | copy-done | bytes 65560
  5.1 0.7 %copy-done.11 = s32[8,128]{1,0:T(8,128)S(1)} copy-done((s32[8,128]{1,0:T(8,128)S(1)}, s32[8,128]{1,0:T(8,128)}, u32[]{:S(2)}) %copy-start.11) | copy-done | bytes 4120
  5.8 0.7 %copy-done.12 = s32[2,128]{1,0:T(2,128)S(1)} copy-done((s32[2,128]{1,0:T(2,128)S(1)}, s32[2,128]{1,0:T(2,128)}, u32[]{:S(2)}) %copy-start.12) | copy-done | bytes 1048
  6.5 0.8 %front.1 = (bf16[1024,384]{1,0:T(8,128)(2,1)S(1)}, bf16[256,512]{1,0:T(8,128)(2,1)S(1)}) custom-call(bf16[2048,256]{1,0:T(8,128)(2,1)S(1)} %copy-done.4, bf16[2048,128]{1,0:T(8,128)(2,1)S(1)} %copy-done.6, bf16[8,256,128]{2,1,0:T(8,128)(2,1)S(1)} %copy-done, bf16[8,128,128]{2,1,0:T(8,128)(2,1)S(1)} %copy-done.2, bf16[2,128,128]{2,1,0:T(8,128)(2,1)S(1)} %copy-done.8, ...), custom_call_target="tpu_custom_call" | custom-call | flops 500000000 | bytes 3478528 | tf_op jit(solution)/shard_map/front/pallas_call | solution.py:301
  7.3 0.0 copy-start.5
  7.3 0.1 collective-permute-start.1
  7.4 0.5 %collective-permute-start.2 = (bf16[256,512]{1,0:T(8,128)(2,1)S(1)}, bf16[256,512]{1,0:T(8,128)(2,1)S(1)}, u32[]{:S(2)}, u32[]{:S(2)}) collective-permute-start(bf16[256,512]{1,0:T(8,128)(2,1)S(1)} %get-tuple-element.10.own_ref), channel_id=1, source_target_pairs={{0,4},{4,0},{8,12},{12,8},{16,20},{20,16},{24,28},{28,24},{32,36},... | collective-permute-start | bytes 786440 | tf_op jit(solution)/shard_map/ppermute | solution.py:335
  7.9 2.1 %collective-permute-done.2.other_ref = bf16[256,512]{1,0:T(8,128)(2,1)S(1)} collective-permute-done((bf16[256,512]{1,0:T(8,128)(2,1)S(1)}, bf16[256,512]{1,0:T(8,128)(2,1)S(1)}, u32[]{:S(2)}, u32[]{:S(2)}) %collective-permute-start.2) | collective-permute-done | bytes 262176 | tf_op jit(solution)/shard_map/ppermute | solution.py:335
  10.0 0.4 upper.1.nodes_ref
  10.4 7.9 %collective-permute-start.3 = (bf16[640,384]{1,0:T(8,128)(2,1)S(1)}, bf16[640,384]{1,0:T(8,128)(2,1)S(1)}, u32[]{:S(2)}, u32[]{:S(2)}) collective-permute-start(bf16[640,384]{1,0:T(8,128)(2,1)S(1)} %upper.1.nodes_ref), channel_id=1, source_target_pairs={{0,252},{4,8},{8,4},{12,16},{16,12},{20,24},{24,20},{28,32},{32,28... | collective-permute-start | bytes 1474568 | tf_op jit(solution)/shard_map/ppermute | solution.py:345
  18.3 0.1 collective-permute-start
  18.4 0.1 copy.15.ufar_ref
  18.5 0.0 copy-done.7
  18.5 0.0 copy-start.14
  18.5 0.0 copy-start.16
  18.5 0.0 copy-start.17
  18.6 2.5 %near.1.near_ref = f32[2048,128]{1,0:T(8,128)S(1)} custom-call(bf16[2048,256]{1,0:T(8,128)(2,1)S(1)} %copy-done.5, bf16[2048,128]{1,0:T(8,128)(2,1)S(1)} %copy-done.7), custom_call_target="tpu_custom_call" | custom-call | flops 3000000000 | bytes 2621440 | tf_op jit(solution)/shard_map/near/pallas_call | solution.py:301
  21.0 3.8 %collective-permute-done.3.side_b_ref = bf16[640,384]{1,0:T(8,128)(2,1)S(1)} collective-permute-done((bf16[640,384]{1,0:T(8,128)(2,1)S(1)}, bf16[640,384]{1,0:T(8,128)(2,1)S(1)}, u32[]{:S(2)}, u32[]{:S(2)}) %collective-permute-start.3) | collective-permute-done | bytes 491552 | tf_op jit(solution)/shard_map/ppermute | solution.py:345
  24.8 0.0 collective-permute-start.4
  24.8 0.0 collective-permute-done.1.side_ref
  24.8 0.0 copy-done.14
  24.9 5.1 %own_far.1 = (f32[1024,128]{1,0:T(8,128)S(1)}, f32[256,128]{1,0:T(8,128)S(1)}) custom-call(bf16[1024,384]{1,0:T(8,128)(2,1)S(1)} %get-tuple-element.9.leaf_ref, bf16[1024,384]{1,0:T(8,128)(2,1)} %collective-permute-done.1.side_ref, s32[8,12]{1,0:T(8,128)S(1)} %copy-done.16, bf16[640,384]{1,0:T(8,128)(2,1)S(1)} %upper.1.nodes_ref, s32[2,12]{1,0:T(2,128)S(1)} %copy-done.13, ...), custom_call_target="tpu_custom_call" | custom-call | flops 4000000000 | bytes 2720264 | tf_op jit(solution)/shard_map/own_far/pallas_call | solution.py:301
  30.0 3.4 %collective-permute-done.rim_ref = bf16[1024,384]{1,0:T(8,128)(2,1)} collective-permute-done((bf16[1024,384]{1,0:T(8,128)(2,1)S(1)}, bf16[1024,384]{1,0:T(8,128)(2,1)}, u32[]{:S(2)}, u32[]{:S(2)}) %collective-permute-start) | collective-permute-done | bytes 786464 | tf_op jit(solution)/shard_map/ppermute | solution.py:336
  33.4 3.0 %rim_far.1.pot_ref = f32[1024,128]{1,0:T(8,128)S(1)} custom-call(bf16[1024,384]{1,0:T(8,128)(2,1)S(1)} %get-tuple-element.9.leaf_ref, bf16[1024,384]{1,0:T(8,128)(2,1)} %collective-permute-done.rim_ref, s32[8,12]{1,0:T(8,128)S(1)} %copy-done.16, f32[1024,128]{1,0:T(8,128)S(1)} %get-tuple-element.11.start_ref, s32[8]{0:T(128)S(1)} %copy-done.17), custom_call_target="tpu_custom_call" | custom-call | flops 2000000000 | bytes 2621856 | tf_op jit(solution)/shard_map/rim_far/pallas_call | solution.py:301
  36.4 0.0 copy-start.15
  36.4 0.0 collective-permute-done.4.side_a_ref
  36.4 0.6 %copy-done.15 = s32[32]{0:T(128)S(1)} copy-done((s32[32]{0:T(128)S(1)}, s32[32]{0:T(128)}, u32[]{:S(2)}) %copy-start.15) | copy-done | bytes 152
  37.0 3.8 %last.1 = bf16[2048,128]{1,0:T(8,128)(2,1)} custom-call(f32[2048,128]{1,0:T(8,128)S(1)} %near.1.near_ref, f32[1024,128]{1,0:T(8,128)S(1)} %rim_far.1.pot_ref, f32[256,128]{1,0:T(8,128)S(1)} %get-tuple-element.12.npot_ref, bf16[640,384]{1,0:T(8,128)(2,1)S(1)} %upper.1.nodes_ref, bf16[640,384]{1,0:T(8,128)(2,1)S(1)} %collective-permute-done.3.side_b_ref, ...), custom_call_target="tpu_custom_call" | custom-call | flops 1000000000 | bytes 4556520 | tf_op jit(solution)/shard_map/last/pallas_call | solution.py:301
  (23 shorter events, 0.0 us)
Async XLA Ops:
  0.0 1.0 %copy-start = (bf16[8,256,128]{2,1,0:T(8,128)(2,1)S(1)}, bf16[8,256,128]{2,1,0:T(8,128)(2,1)}, u32[]{:S(2)}) copy-start(bf16[8,256,128]{2,1,0:T(8,128)(2,1)} %basis_ref.3) | copy-start | bytes 1572868
  1.0 0.9 %copy-start.2 = (bf16[8,128,128]{2,1,0:T(8,128)(2,1)S(1)}, bf16[8,128,128]{2,1,0:T(8,128)(2,1)}, u32[]{:S(2)}) copy-start(bf16[8,128,128]{2,1,0:T(8,128)(2,1)} %lt_ref.3) | copy-start | bytes 786436
  2.0 1.2 %copy-start.4 = (bf16[2048,256]{1,0:T(8,128)(2,1)S(1)}, bf16[2048,256]{1,0:T(8,128)(2,1)}, u32[]{:S(2)}) copy-start(bf16[2048,256]{1,0:T(8,128)(2,1)} %points_ref.3) | copy-start | bytes 3145732
  3.2 1.0 %copy-start.6 = (bf16[2048,128]{1,0:T(8,128)(2,1)S(1)}, bf16[2048,128]{1,0:T(8,128)(2,1)}, u32[]{:S(2)}) copy-start(bf16[2048,128]{1,0:T(8,128)(2,1)} %weights_ref.3) | copy-start | bytes 1572868
  4.3 0.8 %copy-start.8 = (bf16[2,128,128]{2,1,0:T(8,128)(2,1)S(1)}, bf16[2,128,128]{2,1,0:T(8,128)(2,1)}, u32[]{:S(2)}) copy-start(bf16[2,128,128]{2,1,0:T(8,128)(2,1)} %t_ref.3) | copy-start | bytes 196612
  5.1 0.7 %copy-start.11 = (s32[8,128]{1,0:T(8,128)S(1)}, s32[8,128]{1,0:T(8,128)}, u32[]{:S(2)}) copy-start(s32[8,128]{1,0:T(8,128)} %ls_ref.1) | copy-start | bytes 12292
  5.8 0.7 %copy-start.12 = (s32[2,128]{1,0:T(2,128)S(1)}, s32[2,128]{1,0:T(2,128)}, u32[]{:S(2)}) copy-start(s32[2,128]{1,0:T(2,128)} %ns_ref.1) | copy-start | bytes 3076
  6.5 3.6 %copy-start.10 = (s32[32,128]{1,0:T(8,128)S(1)}, s32[32,128]{1,0:T(8,128)}, u32[]{:S(2)}) copy-start(s32[32,128]{1,0:T(8,128)} %us_ref.1) | copy-start | bytes 49156
  6.5 12.0 %copy-start.18 = (s32[32,12]{0,1:T(8,128)S(1)}, s32[32,12]{0,1:T(8,128)}, u32[]{:S(2)}) copy-start(s32[32,12]{0,1:T(8,128)} %param.26) | copy-start | bytes 4612
  6.5 12.0 %copy-start.7 = (bf16[2048,128]{1,0:T(8,128)(2,1)S(1)}, bf16[2048,128]{1,0:T(8,128)(2,1)}, u32[]{:S(2)}) copy-start(bf16[2048,128]{1,0:T(8,128)(2,1)} %weights_ref.3) | copy-start | bytes 1572868
  7.3 11.2 %copy-start.5 = (bf16[2048,256]{1,0:T(8,128)(2,1)S(1)}, bf16[2048,256]{1,0:T(8,128)(2,1)}, u32[]{:S(2)}) copy-start(bf16[2048,256]{1,0:T(8,128)(2,1)} %points_ref.3) | copy-start | bytes 3145732
  7.3 17.6 %collective-permute-start.1 = (bf16[1024,384]{1,0:T(8,128)(2,1)S(1)}, bf16[1024,384]{1,0:T(8,128)(2,1)}, u32[]{:S(2)}, u32[]{:S(2)}) collective-permute-start(bf16[1024,384]{1,0:T(8,128)(2,1)S(1)} %get-tuple-element.9.leaf_ref), channel_id=1, source_target_pairs={{0,4},{4,0},{8,12},{12,8},{16,20},{20,16},{24,28},{28,24},{32,36},... | collective-permute-start | bytes 2359304 | tf_op jit(solution)/shard_map/ppermute | solution.py:337
  7.4 2.6 %collective-permute-start.2 = (bf16[256,512]{1,0:T(8,128)(2,1)S(1)}, bf16[256,512]{1,0:T(8,128)(2,1)S(1)}, u32[]{:S(2)}, u32[]{:S(2)}) collective-permute-start(bf16[256,512]{1,0:T(8,128)(2,1)S(1)} %get-tuple-element.10.own_ref), channel_id=1, source_target_pairs={{0,4},{4,0},{8,12},{12,8},{16,20},{20,16},{24,28},{28,24},{32,36},... | collective-permute-start | bytes 786440 | tf_op jit(solution)/shard_map/ppermute | solution.py:335
  10.4 14.4 %collective-permute-start.3 = (bf16[640,384]{1,0:T(8,128)(2,1)S(1)}, bf16[640,384]{1,0:T(8,128)(2,1)S(1)}, u32[]{:S(2)}, u32[]{:S(2)}) collective-permute-start(bf16[640,384]{1,0:T(8,128)(2,1)S(1)} %upper.1.nodes_ref), channel_id=1, source_target_pairs={{0,252},{4,8},{8,4},{12,16},{16,12},{20,24},{24,20},{28,32},{32,28... | collective-permute-start | bytes 1474568 | tf_op jit(solution)/shard_map/ppermute | solution.py:345
  18.3 15.0 %collective-permute-start = (bf16[1024,384]{1,0:T(8,128)(2,1)S(1)}, bf16[1024,384]{1,0:T(8,128)(2,1)}, u32[]{:S(2)}, u32[]{:S(2)}) collective-permute-start(bf16[1024,384]{1,0:T(8,128)(2,1)S(1)} %get-tuple-element.9.leaf_ref), channel_id=1, source_target_pairs={{0,252},{4,8},{8,4},{12,16},{16,12},{20,24},{24,20},{28,32},{32,28... | collective-permute-start | bytes 2359304 | tf_op jit(solution)/shard_map/ppermute | solution.py:336
  18.5 6.3 %copy-start.13 = (s32[2,12]{1,0:T(2,128)S(1)}, s32[2,12]{1,0:T(2,128)}, u32[]{:S(2)}) copy-start(s32[2,12]{1,0:T(2,128)} %nfar_ref.3) | copy-start | bytes 292
  18.5 6.3 %copy-start.14 = (s32[2]{0:T(128)S(1)}, s32[2]{0:T(128)}, u32[]{:S(2)}) copy-start(s32[2]{0:T(128)} %ncount_ref.3) | copy-start | bytes 28
  18.5 6.3 %copy-start.16 = (s32[8,12]{1,0:T(8,128)S(1)}, s32[8,12]{1,0:T(8,128)}, u32[]{:S(2)}) copy-start(s32[8,12]{1,0:T(8,128)} %far_ref.3) | copy-start | bytes 1156
  18.5 6.3 %copy-start.17 = (s32[8]{0:T(128)S(1)}, s32[8]{0:T(128)}, u32[]{:S(2)}) copy-start(s32[8]{0:T(128)} %count_ref.3) | copy-start | bytes 100
  24.8 11.6 %collective-permute-start.4 = (bf16[640,384]{1,0:T(8,128)(2,1)S(1)}, bf16[640,384]{1,0:T(8,128)(2,1)S(1)}, u32[]{:S(2)}, u32[]{:S(2)}) collective-permute-start(bf16[640,384]{1,0:T(8,128)(2,1)S(1)} %collective-permute-done.3.side_b_ref), channel_id=1, source_target_pairs={{0,4},{4,0},{8,12},{12,8},{16,20},{20,16},{24,28},{28,24},{32,36},... | collective-permute-start | bytes 1474568 | tf_op jit(solution)/shard_map/ppermute | solution.py:346
  33.4 3.0 %copy-start.1 = (bf16[8,256,128]{2,1,0:T(8,128)(2,1)S(1)}, bf16[8,256,128]{2,1,0:T(8,128)(2,1)}, u32[]{:S(2)}) copy-start(bf16[8,256,128]{2,1,0:T(8,128)(2,1)} %basis_ref.3) | copy-start | bytes 1572868
  33.4 3.1 %copy-start.3 = (bf16[8,128,128]{2,1,0:T(8,128)(2,1)S(1)}, bf16[8,128,128]{2,1,0:T(8,128)(2,1)}, u32[]{:S(2)}) copy-start(bf16[8,128,128]{2,1,0:T(8,128)(2,1)} %lt_ref.3) | copy-start | bytes 786436
  33.4 3.1 %copy-start.9 = (bf16[2,128,128]{2,1,0:T(8,128)(2,1)S(1)}, bf16[2,128,128]{2,1,0:T(8,128)(2,1)}, u32[]{:S(2)}) copy-start(bf16[2,128,128]{2,1,0:T(8,128)(2,1)} %t_ref.3) | copy-start | bytes 196612
  36.4 0.7 %copy-start.15 = (s32[32]{0:T(128)S(1)}, s32[32]{0:T(128)}, u32[]{:S(2)}) copy-start(s32[32]{0:T(128)} %ucount_ref.1) | copy-start | bytes 388

commit v2 on v1

v2 whole, which is shorter than its diff:
```python
import functools
import math

import jax
import jax.numpy as jnp
from jax import lax
from jax.experimental import pallas as pl
from jax.experimental.pallas import tpu as pltpu
from jax.sharding import PartitionSpec as P

NEG = -1e38
VMEM = pltpu.VMEM
SMEM = pltpu.SMEM
HBM = pltpu.HBM
LIMIT = 48 * 1024 * 1024


def mm(a, b):
    return jnp.dot(a, b, preferred_element_type=jnp.float32)


def mm_nt(a, b):
    return lax.dot_general(a, b, (((1,), (1,)), ((), ())), preferred_element_type=jnp.float32)


def mm_tn(a, b):
    return lax.dot_general(a, b, (((0,), (0,)), ((), ())), preferred_element_type=jnp.float32)


def scale_of(features):
    return math.log2(math.e) / math.sqrt(8.0 * features)


def split_squares(pts):
    wide = pts.astype(jnp.float32)
    square = wide * wide
    high = square.astype(jnp.bfloat16)
    low = (square - high.astype(jnp.float32)).astype(jnp.bfloat16)
    return high, low


def col_term(high, low):
    features = high.shape[1]
    ones = jnp.ones((features, 128), jnp.bfloat16)
    return scale_of(features) * (features - (mm(high, ones) + mm(low, ones)))


def row_term(high, low):
    features = high.shape[1]
    ones = jnp.ones((8, features), jnp.bfloat16)
    return scale_of(features) * (features - (mm_nt(ones, high) + mm_nt(ones, low)))


def wide(col, lanes):
    return jnp.concatenate([col] * (lanes // 128), axis=1)


def hits(far, counts, first):
    rows, slots = far.shape
    ids = lax.broadcasted_iota(jnp.int32, (rows, 128), 1) + first
    found = jnp.zeros((rows, 128), jnp.float32)
    for k in range(slots):
        same = (far[:, k : k + 1] == ids) & (counts > k)
        found = jnp.where(same, 1.0, found)
    return found


def count_column(count_ref, rows):
    spot = lax.broadcasted_iota(jnp.int32, (rows, 128), 0)
    column = jnp.zeros((rows, 128), jnp.int32)
    for t in range(rows):
        column = jnp.where(spot == t, count_ref[t], column)
    return column


def one_hot_rows(index_columns, at, choices):
    spots = lax.broadcasted_iota(jnp.int32, (index_columns.shape[0], choices), 1)
    same = index_columns[:, at : at + 1] == spots
    return jnp.where(same, 1.0, 0.0).astype(jnp.bfloat16)


def place(total):
    me = lax.axis_index("leaf")
    core = lax.rem(me, 2)
    chips = total // 2
    chip = me // 2
    step = 2 * core - 1
    side_b = lax.rem(chip + step + chips, chips)
    side_a = lax.rem(chip - step + chips, chips)
    return me, core, chip, side_a, side_b


def outer_first(core, group, groups):
    return group + core * (groups - 1 - 2 * group)


def fetch(pairs, sems):
    copies = [pltpu.make_async_copy(s, d, sems.at[i]) for i, (s, d) in enumerate(pairs)]
    for copy in copies:
        copy.start()
    return copies


def group_rows(at):
    return pl.ds(pl.multiple_of(at * 256, 256), 256)


def fill_rows(source_ref, rows_ref, found, features, place_of):
    for group in range(rows_ref.shape[0]):
        high, low = split_squares(source_ref[place_of(group), 0:features])
        term = row_term(high, low)[0 : found.shape[0]]
        for half in range(2):
            j = group * 2 + half
            lanes = slice(half * 128, half * 128 + 128)
            rows_ref[group, :, lanes] = jnp.where(found[:, j : j + 1] > 0.0, term[:, lanes], NEG)


def unit(left, col, right, row_top, row_bottom, charge):
    features = left.shape[1]
    power = mm_nt(left, right) * (2.0 * scale_of(features)) + wide(col, right.shape[0])
    half = left.shape[0] // 2
    block = jnp.concatenate(
        [jnp.exp2(power[:half] + row_top), jnp.exp2(power[half:] + row_bottom)], axis=0
    )
    return mm(block.astype(jnp.bfloat16), charge)


def front_kernel(
    points_hbm, weights_hbm, basis_hbm, lt_hbm, t_hbm, ls_hbm, ns_hbm, far_hbm, count_hbm,
    pack_ref, rim_ref, mask_ref,
    points, weights, basis, lt, t, ls, ns, far, count, sems, *, total,
):
    me, core, _, _, _ = place(total)
    leaves, rows, rank = basis.shape
    nodes = t.shape[0]
    features = points.shape[1]
    cols = weights.shape[1]
    pairs = [(ls_hbm, ls), (ns_hbm, ns), (far_hbm, far), (count_hbm, count)]
    small = len(pairs)
    for leaf in range(leaves):
        own = pl.ds(leaf * rows, rows)
        pairs += [
            (points_hbm.at[own], points.at[own]),
            (weights_hbm.at[own], weights.at[own]),
            (basis_hbm.at[leaf], basis.at[leaf]),
        ]
    pairs += [(lt_hbm, lt), (t_hbm, t)]
    copies = fetch(pairs, sems)
    for copy in copies[:small]:
        copy.wait()
    counts = count_column(count, leaves)
    for at, first in enumerate((me, me + 1 - 2 * core, lax.rem(me + 2 * core - 1 + total, total))):
        found = hits(far[...], counts, first * leaves)
        mask_ref[at * 8 : at * 8 + 8, :] = found
    rim_ref[512:528, :] = jnp.zeros((16, rim_ref.shape[1]), jnp.bfloat16)
    rim_ref[512:528, 0:128] = jnp.concatenate(
        [found, jnp.zeros((8, 128), jnp.float32)], axis=0
    ).astype(jnp.bfloat16)
    leaf_columns = jnp.transpose(ls[...])
    node_columns = jnp.transpose(jnp.concatenate([ns[...]] * 4, axis=0))
    groups = leaves // 2
    picked, charges = [], []
    for leaf in range(leaves):
        for copy in copies[small + 3 * leaf : small + 3 * leaf + 3]:
            copy.wait()
        own = slice(leaf * rows, (leaf + 1) * rows)
        skel = mm(one_hot_rows(leaf_columns, leaf, rows), points[own, :]).astype(jnp.bfloat16)
        charge = mm_tn(basis[leaf], weights[own, :]).astype(jnp.bfloat16)
        start = outer_first(core, leaf // 2, groups) * 256 + (leaf % 2) * rank
        here = pl.ds(pl.multiple_of(start, 128), rank)
        pack_ref[here, 0:features] = skel
        pack_ref[here, features:] = charge
        picked.append(skel)
        charges.append(charge)
    rim_ref[0:512, :] = pack_ref[0:512, :]
    for copy in copies[small + 3 * leaves :]:
        copy.wait()
    base = leaves * rank
    for node in range(nodes):
        own = slice(base + node * rank, base + (node + 1) * rank)
        kids = jnp.concatenate(picked[node * 4 : node * 4 + 4], axis=0)
        rows_hot = one_hot_rows(node_columns, node, 4 * rank)
        pack_ref[own, 0:features] = mm(rows_hot, kids).astype(jnp.bfloat16)
        transfer = lt[node * 4 : node * 4 + 4].reshape(4 * rank, rank)
        charge = mm_tn(transfer, jnp.concatenate(charges[node * 4 : node * 4 + 4], axis=0))
        pack_ref[own, features:] = charge.astype(jnp.bfloat16)
        last = slice(base + 2 * rank, base + 3 * rank)
        pack_ref[last, node * rank : (node + 1) * rank] = t[node]
    pack_ref[base + 2 * rank :, 2 * rank :] = jnp.zeros((rank, rank), jnp.bfloat16)


def upper_kernel(own_ref, other_ref, us_hbm, out_ref, us, transfers, sems, *, total):
    _, core, chip, _, _ = place(total)
    (copy,) = fetch([(us_hbm, us)], sems)
    cols = 128
    features = own_ref.shape[1] - cols
    base = own_ref.shape[0] - 384
    mine = pl.multiple_of(core * 256, 256)
    theirs = pl.multiple_of((1 - core) * 256, 256)
    for start, ref in ((mine, own_ref), (theirs, other_ref)):
        out_ref[pl.ds(start, 256), :] = ref[base : base + 256, :]
        transfers[pl.ds(start, 128), :] = ref[base + 256 : base + 384, 0:128]
        transfers[pl.ds(start + 128, 128), :] = ref[base + 256 : base + 384, 128:256]
    charge = mm_tn(transfers[...], out_ref[0:512, features:])
    out_ref[512:640, features:] = charge.astype(jnp.bfloat16)
    copy.wait()
    index = us[pl.ds(chip, 1), :]
    columns = jnp.transpose(jnp.broadcast_to(index, (8, index.shape[1])))
    picked = mm(one_hot_rows(columns, 0, 512), out_ref[0:512, 0:features])
    out_ref[512:640, 0:features] = picked.astype(jnp.bfloat16)


def near_kernel(points_hbm, weights_hbm, out_ref, points, weights, sems, *, rows):
    features = points.shape[1]
    leaves = points.shape[0] // rows
    pairs = []
    for leaf in range(leaves):
        own = pl.ds(leaf * rows, rows)
        pairs += [
            (points_hbm.at[own], points.at[own]), (weights_hbm.at[own], weights.at[own])
        ]
    copies = fetch(pairs, sems)
    same = lax.broadcasted_iota(jnp.int32, (rows, rows), 0) == lax.broadcasted_iota(
        jnp.int32, (rows, rows), 1
    )
    for leaf in range(leaves):
        copies[2 * leaf].wait()
        copies[2 * leaf + 1].wait()
        own = slice(leaf * rows, (leaf + 1) * rows)
        pts = points[own, :]
        high, low = split_squares(pts)
        power = (
            mm_nt(pts, pts) * (2.0 * scale_of(features))
            + wide(col_term(high, low), rows)
            + row_term(high, low)[0:1]
        )
        tile = jnp.exp2(jnp.where(same, NEG, power)).astype(jnp.bfloat16)
        out_ref[own, :] = mm(tile, weights[own, :])


def far_groups(targets_ref, source_ref, rows_ref, start, pot_ref, core, pairs, features):
    groups = 4
    for group, sources in pairs:
        own = group_rows(group)
        at = outer_first(core[0], group, groups)
        left = targets_ref[own, 0:features]
        col = col_term(*split_squares(left))
        total_here = None if start is None else start[own, :]
        for source in sources:
            here = group_rows(source)
            src = outer_first(core[1], source, groups)
            part = unit(
                left, col, source_ref[here, 0:features],
                rows_ref[src, pl.ds(2 * at, 1), :], rows_ref[src, pl.ds(2 * at + 1, 1), :],
                source_ref[here, features:],
            )
            total_here = part if total_here is None else total_here + part
        pot_ref[own, :] = total_here.astype(pot_ref.dtype)


def own_kernel(pack_ref, mask_ref, pot_ref, rows_ref, *, total):
    _, core, _, _, _ = place(total)
    features = pack_ref.shape[1] - pot_ref.shape[1]
    fill_rows(
        pack_ref, rows_ref, mask_ref[0:8, :], features,
        lambda g: group_rows(outer_first(core, g, 4)),
    )
    pairs = [(g, range(4)) for g in range(4)]
    far_groups(pack_ref, pack_ref, rows_ref, None, pot_ref, (core, core), pairs, features)


def side_kernel(pack_ref, side_ref, mask_ref, start_ref, pot_ref, rows_ref, *, total):
    _, core, _, _, _ = place(total)
    features = pack_ref.shape[1] - pot_ref.shape[1]
    fill_rows(
        side_ref, rows_ref, mask_ref[8:16, :], features,
        lambda g: group_rows(outer_first(1 - core, g, 4)),
    )
    pairs = [(g, range(3 - g, 4)) for g in range(4)]
    far_groups(pack_ref, side_ref, rows_ref, start_ref, pot_ref, (core, 1 - core), pairs, features)


def back_kernel(pack_ref, rim_ref, ret_ref, rows_ref, *, total):
    _, core, _, _, _ = place(total)
    features = pack_ref.shape[1] - ret_ref.shape[1]
    found = rim_ref[512:528, 0:128].astype(jnp.float32)[0:8, :]
    fill_rows(
        pack_ref, rows_ref, found, features, lambda g: group_rows(outer_first(core, g, 4))
    )
    pairs = [(0, (2, 3)), (1, (2,))]
    far_groups(rim_ref, pack_ref, rows_ref, None, ret_ref, (1 - core, core), pairs, features)


def rim_kernel(pack_ref, rim_ref, mask_ref, start_ref, pot_ref, rows_ref, *, total):
    _, core, _, _, _ = place(total)
    features = pack_ref.shape[1] - pot_ref.shape[1]
    found = mask_ref[16:24, :]
    for source in range(2):
        tree = outer_first(1 - core, source, 4)
        high, low = split_squares(rim_ref[group_rows(source), 0:features])
        term = row_term(high, low)[0:8]
        for half in range(2):
            zero = found[:, 2 * source + half : 2 * source + half + 1]
            one = found[:, 2 * (3 - source) + half : 2 * (3 - source) + half + 1]
            used = jnp.where(core == 0, one, zero)
            lanes = slice(half * 128, half * 128 + 128)
            rows_ref[tree, :, lanes] = jnp.where(used > 0.0, term[:, lanes], NEG)
    pairs = [(0, (0, 1)), (1, (0, 1)), (2, (0, 1)), (3, (0,))]
    far_groups(pack_ref, rim_ref, rows_ref, start_ref, pot_ref, (core, 1 - core), pairs, features)


def node_kernel(
    nodes_ref, side_b_ref, side_a_ref, pot_ref, ufar_ref, t_hbm, lt_hbm, nfar_hbm,
    ncount_hbm, ucount_hbm, out_ref, rows_ref, t, lt, nfar, ncount, ucount, sems, *, total,
):
    _, core, chip, side_a, side_b = place(total)
    copies = fetch(
        [(nfar_hbm, nfar), (ncount_hbm, ncount), (ucount_hbm, ucount), (t_hbm, t), (lt_hbm, lt)],
        sems,
    )
    cols = pot_ref.shape[1]
    features = nodes_ref.shape[1] - cols
    scale = 2.0 * scale_of(features)
    own_upper = nodes_ref[512:640, 0:features]
    upper_col = col_term(*split_squares(own_upper))
    left = nodes_ref[group_rows(core), 0:features]
    col = col_term(*split_squares(left))
    for copy in copies[0:3]:
        copy.wait()
    ufar = ufar_ref[pl.ds(chip, 1), :]
    live = ucount[chip]
    far2 = jnp.zeros((128, cols), jnp.float32)
    for ref, ident in ((side_b_ref, side_b), (side_a_ref, side_a)):
        source = ref[512:640, 0:features]
        used = jnp.zeros((1, 128), jnp.float32)
        for k in range(ufar.shape[1]):
            same = (jnp.broadcast_to(ufar[:, k : k + 1], (1, 128)) == ident) & (k < live)
            used = jnp.where(same, 1.0, used)
        row = jnp.where(used > 0.0, row_term(*split_squares(source))[0:1], NEG)
        power = mm_nt(own_upper, source) * scale + upper_col + row
        far2 += mm(jnp.exp2(power).astype(jnp.bfloat16), ref[512:640, features:])
    down2 = far2.astype(jnp.bfloat16)
    ncounts = count_column(ncount, 2)
    far1 = None
    for ref, first in ((nodes_ref, chip), (side_b_ref, side_b), (side_a_ref, side_a)):
        found = hits(nfar[...], ncounts, first * 4)
        fill_rows(ref, rows_ref, found, features, group_rows)
        for source in range(2):
            here = group_rows(source)
            part = unit(
                left, col, ref[here, 0:features],
                rows_ref[source, 0:1, :], rows_ref[source, 1:2, :], ref[here, features:],
            )
            far1 = part if far1 is None else far1 + part
    for copy in copies[3:]:
        copy.wait()
    rank = t.shape[1]
    for node in range(2):
        down1 = (far1[node * rank : (node + 1) * rank] + mm(t[node], down2)).astype(jnp.bfloat16)
        for leaf in range(node * 4, node * 4 + 4):
            start = outer_first(core, leaf // 2, 4) * 256 + (leaf % 2) * rank
            here = pl.ds(pl.multiple_of(start, 128), rank)
            out_ref[leaf * rank : (leaf + 1) * rank, :] = pot_ref[here, :] + mm(lt[leaf], down1)


def last_kernel(near_ref, pot_ref, ret_ref, basis_hbm, out_ref, basis, sems, *, total):
    _, core, _, _, _ = place(total)
    (copy,) = fetch([(basis_hbm, basis)], sems)
    copy.wait()
    leaves, rows, rank = basis.shape
    for leaf in range(leaves):
        group = outer_first(core, leaf // 2, 4)
        inside = jnp.minimum(group, 1) * 256 + (leaf % 2) * rank
        back = ret_ref[pl.ds(pl.multiple_of(inside, 128), rank), :].astype(jnp.float32)
        down0 = pot_ref[leaf * rank : (leaf + 1) * rank, :] + jnp.where(group < 2, back, 0.0)
        own = slice(leaf * rows, (leaf + 1) * rows)
        result = near_ref[own, :] + mm(basis[leaf], down0.astype(jnp.bfloat16))
        out_ref[own, :] = result.astype(jnp.bfloat16)


def call(kernel, outs, args, spaces, scratch=(), mmacs=0, name=None):
    kinds = {"v": VMEM, "h": HBM, "s": SMEM}
    return pl.pallas_call(
        kernel,
        out_shape=outs,
        in_specs=[pl.BlockSpec(memory_space=kinds[k]) for k in spaces],
        out_specs=[pl.BlockSpec(memory_space=VMEM)] * len(outs),
        scratch_shapes=list(scratch),
        compiler_params=pltpu.CompilerParams(vmem_limit_bytes=LIMIT),
        cost_estimate=pl.CostEstimate(
            flops=int(2e6 * mmacs), bytes_accessed=0, transcendentals=0
        ),
        name=name,
    )(*[pltpu.with_memory_space_constraint(a, pltpu.HBM) if k == 'h' else a for a, k in zip(args, spaces)])


def like(array, space=None):
    return (space or VMEM)(array.shape, array.dtype)


def per_device(
    points, weights, leaf_basis, leaf_transfer, node_transfer, leaf_skeleton, node_skeleton,
    upper_skeleton, leaf_far, leaf_count, node_far, node_count, upper_far, upper_count,
):
    leaves, rows, rank = leaf_basis.shape
    features = points.shape[1]
    cols = weights.shape[1]
    total = lax.axis_size("leaf")
    width = features + cols
    bf16, f32 = jnp.bfloat16, jnp.float32
    across = [(d, d ^ 1) for d in range(total)]
    outward = [(d, (d + 1) % total if d % 2 else (d - 1) % total) for d in range(total)]
    shape = jax.ShapeDtypeStruct
    sems = pltpu.SemaphoreType.DMA
    bind = functools.partial
    rows_scratch = pltpu.VMEM((leaves // 2, leaves, 256), f32)
    pot_shape = shape((leaves * rank, cols), f32)

    pack, rim, mask = call(
        bind(front_kernel, total=total),
        [
            shape((leaves * rank + 3 * rank, width), bf16),
            shape((4 * rank + 16, width), bf16),
            shape((24, 128), f32),
        ],
        [points, weights, leaf_basis, leaf_transfer, node_transfer, leaf_skeleton, node_skeleton,
         leaf_far, leaf_count],
        "hhhhhhhhh",
        [like(points), like(weights), like(leaf_basis), like(leaf_transfer), like(node_transfer),
         like(leaf_skeleton), like(node_skeleton), like(leaf_far), like(leaf_count, SMEM),
         sems((3 * leaves + 6,))],
        mmacs=300, name="front",
    )
    rim_in = lax.ppermute(rim, "leaf", outward)
    side = lax.ppermute(pack, "leaf", across)
    (nodes,) = call(
        bind(upper_kernel, total=total),
        [shape((5 * rank, width), bf16)],
        [pack, side, upper_skeleton], "vvh",
        [like(upper_skeleton), pltpu.VMEM((4 * rank, rank), bf16), sems((1,))],
        mmacs=30, name="upper",
    )
    nodes_b = lax.ppermute(nodes, "leaf", outward)
    nodes_a = lax.ppermute(nodes_b, "leaf", across)
    (near,) = call(
        bind(near_kernel, rows=rows),
        [shape((leaves * rows, cols), f32)],
        [points, weights], "hh",
        [like(points), like(weights), sems((2 * leaves,))],
        mmacs=1000, name="near",
    )
    (pot,) = call(
        bind(own_kernel, total=total), [pot_shape], [pack, mask], "vv", [rows_scratch],
        mmacs=1000, name="own",
    )
    (ret,) = call(
        bind(back_kernel, total=total), [shape((4 * rank, cols), bf16)], [pack, rim_in], "vv",
        [rows_scratch], mmacs=300, name="back",
    )
    ret_in = lax.ppermute(ret, "leaf", outward)
    (pot,) = call(
        bind(side_kernel, total=total), [pot_shape], [pack, side, mask, pot], "vvvv",
        [rows_scratch], mmacs=800, name="side",
    )
    (pot,) = call(
        bind(rim_kernel, total=total), [pot_shape], [pack, rim_in, mask, pot], "vvvv",
        [rows_scratch], mmacs=600, name="rim",
    )
    (pot,) = call(
        bind(node_kernel, total=total), [pot_shape],
        [nodes, nodes_b, nodes_a, pot, upper_far, node_transfer, leaf_transfer, node_far,
         node_count, upper_count],
        "vvvvvhhhhh",
        [pltpu.VMEM((2, 2, 256), f32), like(node_transfer), like(leaf_transfer), like(node_far),
         like(node_count, SMEM), like(upper_count, SMEM), sems((5,))],
        mmacs=500, name="node",
    )
    (out,) = call(
        bind(last_kernel, total=total),
        [shape((leaves * rows, cols), bf16)],
        [near, pot, ret_in, leaf_basis], "vvvh",
        [like(leaf_basis), sems((1,))],
        mmacs=200, name="last",
    )
    return out


def solution(mesh):
    placed = (
        P("leaf", None),
        P("leaf", "cols"),
        P("leaf", None, None),
        P("leaf", None, None),
        P("leaf", None, None),
        P("leaf", None),
        P("leaf", None),
        P(),
        P("leaf", None),
        P("leaf"),
        P("leaf", None),
        P("leaf"),
        P(),
        P(),
    )
    return jax.shard_map(
        per_device, mesh=mesh, in_specs=placed, out_specs=P("leaf", "cols"), check_vma=False
    )
```

time: 41.3 us -> 44.2 us (1.070)
  Pallas kernels: 15.6 us -> 24.2 us
  local copies, waits for them, and re-layouts: 7.21 us -> 0.09 us
  starting transfers between devices: 8.57 us -> 13.4 us
  waiting for transfers between devices: 9.33 us -> 5.93 us
    pallas_call x6 -> x9, Pallas kernels: 15.6 us -> 24.2 us  [call(): pl.pallas_call(kernel, out_shape=outs, in_specs=[pl.BlockSpec(memory_spac...]
    unnamed x39 -> x3, local copies, waits for them, and re-layouts: 7.21 us -> 0.09 us
    ppermute x3, starting transfers between devices: 0.69 us -> 5.52 us  [the longest x1 5.33 us: per_device(): ret_in = lax.ppermute(ret, 'leaf', outward)]
    ppermute x1, waiting for transfers between devices: 3.8 us -> 1.38 us  [per_device(): nodes_b = lax.ppermute(nodes, 'leaf', outward)]
    ppermute x3, waiting for transfers between devices: 5.53 us -> 4.55 us  [the longest x1 2.69 us: per_device(): side = lax.ppermute(pack, 'leaf', across)]
  transfers between devices with their start and end apart: 5 -> 5, of which waited for: 3 -> 3; matrix products, arithmetic and copies ran while one was open for 0% -> 0% of each run, Pallas kernels for 27% -> 39%
where the time goes in v2:
time: 44.2 us; the launch traced here: 43.9 us
  Pallas kernels  24.2 us (55%)
  starting transfers between devices  13.4 us (30%)
  waiting for transfers between devices  5.93 us (13%)
    pallas_call x9, Pallas kernels, call(): pl.pallas_call(kernel, out_shape=outs, in_specs=[pl.BlockSpec(memory_spac...  24.2 us
    ppermute x1, starting transfers between devices, per_device(): nodes_b = lax.ppermute(nodes, 'leaf', outward)  7.88 us
    ppermute x1, starting transfers between devices, per_device(): ret_in = lax.ppermute(ret, 'leaf', outward)  5.33 us
    ppermute x1, waiting for transfers between devices, per_device(): side = lax.ppermute(pack, 'leaf', across)  2.69 us
    ppermute x1, waiting for transfers between devices, per_device(): rim_in = lax.ppermute(rim, 'leaf', outward)  1.85 us
    ppermute x1, waiting for transfers between devices, per_device(): nodes_b = lax.ppermute(nodes, 'leaf', outward)  1.38 us
  transfers between devices with their start and end apart: 5, of which 3 were waited for; matrix products, arithmetic and copies ran while one was open for 0% of the time, Pallas kernels for 39%

profile of v2, /device:TPU:16, one launch (start us, length us, event | category | flops | bytes accessed | tf_op | source)
XLA Modules:
  0.0 43.9 jit_solution(9349390615005848157)
XLA Ops:
  0.0 4.1 %front.1 = (bf16[1408,384]{1,0:T(8,128)(2,1)S(1)}, bf16[528,384]{1,0:T(8,128)(2,1)}, f32[24,128]{1,0:T(8,128)S(1)}) custom-call(bf16[2048,256]{1,0:T(8,128)(2,1)} %points_hbm.3, bf16[2048,128]{1,0:T(8,128)(2,1)} %weights_hbm.3, bf16[8,256,128]{2,1,0:T(8,128)(2,1)} %basis_hbm.3, bf16[8,128,128]{2,1,0:T(8,128)(2,1)} %lt_hbm.3, bf16[2,128,128]{2,1,0:T(8,128)(2,1)} %t_hbm.3, ...), custom_call_target="tpu_custom_call" | custom-call | flops 600000000 | tf_op jit(solution)/shard_map/front/pallas_call | solution.py:383
  4.1 0.0 copy-start
  4.1 0.1 collective-permute-start
  4.2 2.7 %collective-permute-done.other_ref.side_ref = bf16[1408,384]{1,0:T(8,128)(2,1)S(1)} collective-permute-done((bf16[1408,384]{1,0:T(8,128)(2,1)S(1)}, bf16[1408,384]{1,0:T(8,128)(2,1)S(1)}, u32[]{:S(2)}, u32[]{:S(2)}) %collective-permute-start) | collective-permute-done | bytes 1081376 | tf_op jit(solution)/shard_map/ppermute | solution.py:435
  6.9 1.1 %upper.1.nodes_ref = bf16[640,384]{1,0:T(8,128)(2,1)S(1)} custom-call(bf16[1408,384]{1,0:T(8,128)(2,1)S(1)} %get-tuple-element.8.own_ref.pack_ref, bf16[1408,384]{1,0:T(8,128)(2,1)S(1)} %collective-permute-done.other_ref.side_ref, s32[32,128]{1,0:T(8,128)} %us_hbm.1), custom_call_target="tpu_custom_call" | custom-call | flops 60000000 | tf_op jit(solution)/shard_map/upper/pallas_call | solution.py:383
  7.9 7.9 %collective-permute-start.1 = (bf16[640,384]{1,0:T(8,128)(2,1)S(1)}, bf16[640,384]{1,0:T(8,128)(2,1)S(1)}, u32[]{:S(2)}, u32[]{:S(2)}) collective-permute-start(bf16[640,384]{1,0:T(8,128)(2,1)S(1)} %upper.1.nodes_ref), channel_id=1, source_target_pairs={{0,252},{4,8},{8,4},{12,16},{16,12},{20,24},{24,20},{28,32},{32,28... | collective-permute-start | bytes 1474568 | tf_op jit(solution)/shard_map/ppermute | solution.py:443
  15.8 0.1 collective-permute-start.3
  15.9 0.0 copy-done
  15.9 0.1 copy.15.ufar_ref
  16.0 4.9 %near.1.near_ref = f32[2048,128]{1,0:T(8,128)S(1)} custom-call(bf16[2048,256]{1,0:T(8,128)(2,1)} %points_hbm.3, bf16[2048,128]{1,0:T(8,128)(2,1)} %weights_hbm.3), custom_call_target="tpu_custom_call" | custom-call | flops 2000000000 | tf_op jit(solution)/shard_map/near/pallas_call | solution.py:383
  21.0 1.4 %collective-permute-done.1.side_b_ref = bf16[640,384]{1,0:T(8,128)(2,1)S(1)} collective-permute-done((bf16[640,384]{1,0:T(8,128)(2,1)S(1)}, bf16[640,384]{1,0:T(8,128)(2,1)S(1)}, u32[]{:S(2)}, u32[]{:S(2)}) %collective-permute-start.1) | collective-permute-done | bytes 491552 | tf_op jit(solution)/shard_map/ppermute | solution.py:443
  22.3 0.0 collective-permute-start.2
  22.3 2.6 %own.1.start_ref = f32[1024,128]{1,0:T(8,128)S(1)} custom-call(bf16[1408,384]{1,0:T(8,128)(2,1)S(1)} %get-tuple-element.8.own_ref.pack_ref, f32[24,128]{1,0:T(8,128)S(1)} %get-tuple-element.10.mask_ref), custom_call_target="tpu_custom_call" | custom-call | flops 2000000000 | tf_op jit(solution)/shard_map/own/pallas_call | solution.py:383
  24.9 1.8 %collective-permute-done.3.rim_ref = bf16[528,384]{1,0:T(8,128)(2,1)} collective-permute-done((bf16[528,384]{1,0:T(8,128)(2,1)}, bf16[528,384]{1,0:T(8,128)(2,1)}, u32[]{:S(2)}, u32[]{:S(2)}) %collective-permute-start.3) | collective-permute-done | bytes 405536 | tf_op jit(solution)/shard_map/ppermute | solution.py:434
  26.8 2.0 %back.1 = bf16[512,128]{1,0:T(8,128)(2,1)S(1)} custom-call(bf16[1408,384]{1,0:T(8,128)(2,1)S(1)} %get-tuple-element.8.own_ref.pack_ref, bf16[528,384]{1,0:T(8,128)(2,1)} %collective-permute-done.3.rim_ref), custom_call_target="tpu_custom_call" | custom-call | flops 600000000 | tf_op jit(solution)/shard_map/back/pallas_call | solution.py:383
  28.8 5.3 %collective-permute-start.4 = (bf16[512,128]{1,0:T(8,128)(2,1)S(1)}, bf16[512,128]{1,0:T(8,128)(2,1)S(1)}, u32[]{:S(2)}, u32[]{:S(2)}) collective-permute-start(bf16[512,128]{1,0:T(8,128)(2,1)S(1)} %back.1), channel_id=1, source_target_pairs={{0,252},{4,8},{8,4},{12,16},{16,12},{20,24},{24,20},{28,32},{32,28... | collective-permute-start | bytes 393224 | tf_op jit(solution)/shard_map/ppermute | solution.py:460
  34.1 1.9 %side.1.start_ref = f32[1024,128]{1,0:T(8,128)S(1)} custom-call(bf16[1408,384]{1,0:T(8,128)(2,1)S(1)} %get-tuple-element.8.own_ref.pack_ref, bf16[1408,384]{1,0:T(8,128)(2,1)S(1)} %collective-permute-done.other_ref.side_ref, f32[24,128]{1,0:T(8,128)S(1)} %get-tuple-element.10.mask_ref, f32[1024,128]{1,0:T(8,128)S(1)} %own.1.start_ref), custom_call_target="tpu_custom_call" | custom-call | flops 1600000000 | tf_op jit(solution)/shard_map/side/pallas_call | solution.py:383
  36.0 2.5 %rim.1.pot_ref = f32[1024,128]{1,0:T(8,128)S(1)} custom-call(bf16[1408,384]{1,0:T(8,128)(2,1)S(1)} %get-tuple-element.8.own_ref.pack_ref, bf16[528,384]{1,0:T(8,128)(2,1)} %collective-permute-done.3.rim_ref, f32[24,128]{1,0:T(8,128)S(1)} %get-tuple-element.10.mask_ref, f32[1024,128]{1,0:T(8,128)S(1)} %side.1.start_ref), custom_call_target="tpu_custom_call" | custom-call | flops 1200000000 | tf_op jit(solution)/shard_map/rim/pallas_call | solution.py:383
  38.5 0.0 collective-permute-done.2.side_a_ref
  38.5 3.1 %node.1.pot_ref = f32[1024,128]{1,0:T(8,128)S(1)} custom-call(bf16[640,384]{1,0:T(8,128)(2,1)S(1)} %upper.1.nodes_ref, bf16[640,384]{1,0:T(8,128)(2,1)S(1)} %collective-permute-done.1.side_b_ref, bf16[640,384]{1,0:T(8,128)(2,1)S(1)} %collective-permute-done.2.side_a_ref, f32[1024,128]{1,0:T(8,128)S(1)} %rim.1.pot_ref, s32[32,12]{1,0:T(8,128)S(1)} %copy.15.ufar_ref, ...), custom_call_target="tpu_custom_call" | custom-call | flops 1000000000 | tf_op jit(solution)/shard_map/node/pallas_call | solution.py:383
  41.6 0.0 collective-permute-done.4.ret_ref
  41.6 2.1 %last.1 = bf16[2048,128]{1,0:T(8,128)(2,1)} custom-call(f32[2048,128]{1,0:T(8,128)S(1)} %near.1.near_ref, f32[1024,128]{1,0:T(8,128)S(1)} %node.1.pot_ref, bf16[512,128]{1,0:T(8,128)(2,1)S(1)} %collective-permute-done.4.ret_ref, bf16[8,256,128]{2,1,0:T(8,128)(2,1)} %basis_hbm.3), custom_call_target="tpu_custom_call" | custom-call | flops 400000000 | tf_op jit(solution)/shard_map/last/pallas_call | solution.py:383
Async XLA Ops:
  4.1 11.8 %copy-start = (s32[32,12]{0,1:T(8,128)S(1)}, s32[32,12]{0,1:T(8,128)}, u32[]{:S(2)}) copy-start(s32[32,12]{0,1:T(8,128)} %param.26) | copy-start | bytes 4612
  4.1 2.8 %collective-permute-start = (bf16[1408,384]{1,0:T(8,128)(2,1)S(1)}, bf16[1408,384]{1,0:T(8,128)(2,1)S(1)}, u32[]{:S(2)}, u32[]{:S(2)}) collective-permute-start(bf16[1408,384]{1,0:T(8,128)(2,1)S(1)} %get-tuple-element.8.own_ref.pack_ref), channel_id=1, source_target_pairs={{0,4},{4,0},{8,12},{12,8},{16,20},{20,16},{24,28},{28,24},{32,36},... | collective-permute-start | bytes 3244040 | tf_op jit(solution)/shard_map/ppermute | solution.py:435
  7.9 14.4 %collective-permute-start.1 = (bf16[640,384]{1,0:T(8,128)(2,1)S(1)}, bf16[640,384]{1,0:T(8,128)(2,1)S(1)}, u32[]{:S(2)}, u32[]{:S(2)}) collective-permute-start(bf16[640,384]{1,0:T(8,128)(2,1)S(1)} %upper.1.nodes_ref), channel_id=1, source_target_pairs={{0,252},{4,8},{8,4},{12,16},{16,12},{20,24},{24,20},{28,32},{32,28... | collective-permute-start | bytes 1474568 | tf_op jit(solution)/shard_map/ppermute | solution.py:443
  15.8 11.0 %collective-permute-start.3 = (bf16[528,384]{1,0:T(8,128)(2,1)}, bf16[528,384]{1,0:T(8,128)(2,1)}, u32[]{:S(2)}, u32[]{:S(2)}) collective-permute-start(bf16[528,384]{1,0:T(8,128)(2,1)} %get-tuple-element.9), channel_id=1, source_target_pairs={{0,252},{4,8},{8,4},{12,16},{16,12},{20,24},{24,20},{28,32},{32,28... | collective-permute-start | bytes 1216520 | tf_op jit(solution)/shard_map/ppermute | solution.py:434
  22.3 16.1 %collective-permute-start.2 = (bf16[640,384]{1,0:T(8,128)(2,1)S(1)}, bf16[640,384]{1,0:T(8,128)(2,1)S(1)}, u32[]{:S(2)}, u32[]{:S(2)}) collective-permute-start(bf16[640,384]{1,0:T(8,128)(2,1)S(1)} %collective-permute-done.1.side_b_ref), channel_id=1, source_target_pairs={{0,4},{4,0},{8,12},{12,8},{16,20},{20,16},{24,28},{28,24},{32,36},... | collective-permute-start | bytes 1474568 | tf_op jit(solution)/shard_map/ppermute | solution.py:444
  28.8 12.8 %collective-permute-start.4 = (bf16[512,128]{1,0:T(8,128)(2,1)S(1)}, bf16[512,128]{1,0:T(8,128)(2,1)S(1)}, u32[]{:S(2)}, u32[]{:S(2)}) collective-permute-start(bf16[512,128]{1,0:T(8,128)(2,1)S(1)} %back.1), channel_id=1, source_target_pairs={{0,252},{4,8},{8,4},{12,16},{16,12},{20,24},{24,20},{28,32},{32,28... | collective-permute-start | bytes 393224 | tf_op jit(solution)/shard_map/ppermute | solution.py:460

commit v3 on v2

v3 whole, which is shorter than its diff:
```python
import functools
import math

import jax
import jax.numpy as jnp
from jax import lax
from jax.experimental import pallas as pl
from jax.experimental.pallas import tpu as pltpu
from jax.sharding import PartitionSpec as P

NEG = -1e38
VMEM = pltpu.VMEM
SMEM = pltpu.SMEM
HBM = pltpu.HBM
LIMIT = 12 * 1024 * 1024


def mm(a, b):
    return jnp.dot(a, b, preferred_element_type=jnp.float32)


def mm_nt(a, b):
    return lax.dot_general(a, b, (((1,), (1,)), ((), ())), preferred_element_type=jnp.float32)


def mm_tn(a, b):
    return lax.dot_general(a, b, (((0,), (0,)), ((), ())), preferred_element_type=jnp.float32)


def scale_of(features):
    return math.log2(math.e) / math.sqrt(8.0 * features)


def norm_col(pts):
    rows, features = pts.shape
    wide = pts.astype(jnp.float32)
    total = jnp.sum(wide * wide, axis=1, keepdims=True)
    return jnp.broadcast_to(scale_of(features) * (features - total), (rows, 128))


def norm_row(col, targets):
    return jnp.transpose(col)[0:targets]


def twice(col):
    return jnp.concatenate([col, col], axis=1)


def hits(far, counts, first):
    rows, slots = far.shape
    ids = lax.broadcasted_iota(jnp.int32, (rows, 128), 1) + first
    found = jnp.zeros((rows, 128), jnp.float32)
    for k in range(slots):
        same = (far[:, k : k + 1] == ids) & (counts > k)
        found = jnp.where(same, 1.0, found)
    return found


def count_column(count_ref, rows):
    spot = lax.broadcasted_iota(jnp.int32, (rows, 128), 0)
    column = jnp.zeros((rows, 128), jnp.int32)
    for t in range(rows):
        column = jnp.where(spot == t, count_ref[t], column)
    return column


def one_hot_rows(index_columns, at, choices):
    spots = lax.broadcasted_iota(jnp.int32, (index_columns.shape[0], choices), 1)
    same = index_columns[:, at : at + 1] == spots
    return jnp.where(same, 1.0, 0.0).astype(jnp.bfloat16)


def place(total):
    me = lax.axis_index("leaf")
    core = lax.rem(me, 2)
    chips = total // 2
    chip = me // 2
    step = 2 * core - 1
    side_b = lax.rem(chip + step + chips, chips)
    side_a = lax.rem(chip - step + chips, chips)
    return me, core, chip, side_a, side_b


def outer_first(core, group, groups):
    return group + core * (groups - 1 - 2 * group)


def fetch(pairs, sems):
    copies = [pltpu.make_async_copy(s, d, sems.at[i]) for i, (s, d) in enumerate(pairs)]
    for copy in copies:
        copy.start()
    return copies


def group_rows(at):
    return pl.ds(pl.multiple_of(at * 256, 256), 256)


def fill_rows(rows_ref, at, source, used_columns, targets):
    col = norm_col(source) if source.shape[1] != 128 else source
    for half in range(2):
        term = norm_row(col[half * 128 : half * 128 + 128], targets)
        lanes = slice(half * 128, half * 128 + 128)
        rows_ref[at, :, lanes] = jnp.where(used_columns[half] > 0.0, term, NEG)


def blocks(left, col, right, row_of):
    features = left.shape[1]
    inner = mm_nt(left, right)
    parts = []
    for at in range(left.shape[0] // 128):
        own = slice(at * 128, at * 128 + 128)
        power = inner[own] * (2.0 * scale_of(features)) + twice(col[own]) + row_of(at)
        parts.append(jnp.exp2(power).astype(jnp.bfloat16))
    return jnp.concatenate(parts, axis=0) if len(parts) > 1 else parts[0]


def tree_leaf(core, at):
    return outer_first(core, at // 2, 4) * 2 + at % 2


def front_kernel(
    points_hbm, weights_hbm, basis_hbm, lt_hbm, t_hbm, ls_hbm, ns_hbm, far_hbm, count_hbm, us_hbm,
    pack_ref, rim_ref, mask_ref, us,
    points, weights, basis, lt, t, ls, ns, far, count, sems, *, total,
):
    me, core, _, _, _ = place(total)
    leaves, rows, rank = basis.shape
    nodes = t.shape[0]
    features = points.shape[1]
    cols = weights.shape[1]
    small = [(ls_hbm, ls), (ns_hbm, ns), (far_hbm, far), (count_hbm, count), (us_hbm, us)]
    pairs = list(small)
    part = leaves // 2
    for half in range(2):
        own = pl.ds(half * part * rows, part * rows)
        some = pl.ds(half * part, part)
        pairs += [
            (points_hbm.at[own], points.at[own]),
            (weights_hbm.at[own], weights.at[own]),
            (basis_hbm.at[some], basis.at[some]),
        ]
    pairs += [(lt_hbm, lt), (t_hbm, t)]
    copies = fetch(pairs, sems)
    for copy in copies[: len(small)]:
        copy.wait()
    counts = count_column(count, leaves)
    for at, first in enumerate((me, me + 1 - 2 * core, lax.rem(me + 2 * core - 1 + total, total))):
        found = hits(far[...], counts, first * leaves)
        mask_ref[at * 8 : at * 8 + 8, :] = found
    rim_ref[512:528, :] = jnp.zeros((16, rim_ref.shape[1]), jnp.bfloat16)
    rim_ref[512:528, 0:128] = jnp.concatenate(
        [found, jnp.zeros((8, 128), jnp.float32)], axis=0
    ).astype(jnp.bfloat16)
    leaf_columns = jnp.transpose(ls[...])
    node_columns = jnp.transpose(jnp.concatenate([ns[...]] * 4, axis=0))
    groups = leaves // 2
    picked, charges = [], []
    base = leaves * rank
    for leaf in range(leaves):
        if leaf % part == 0:
            first = len(small) + 3 * (leaf // part)
            for copy in copies[first : first + 3]:
                copy.wait()
        own = slice(leaf * rows, (leaf + 1) * rows)
        skel = mm(one_hot_rows(leaf_columns, leaf, rows), points[own, :]).astype(jnp.bfloat16)
        charge = mm_tn(basis[leaf], weights[own, :]).astype(jnp.bfloat16)
        start = outer_first(core, leaf // 2, groups) * 256 + (leaf % 2) * rank
        here = pl.ds(pl.multiple_of(start, 128), rank)
        pack_ref[here, 0:features] = skel
        pack_ref[here, features:] = charge
        picked.append(skel)
        charges.append(charge)
    for copy in copies[len(small) + 6 :]:
        copy.wait()
    for node in range(nodes):
        own = slice(base + node * rank, base + (node + 1) * rank)
        kids = jnp.concatenate(picked[node * 4 : node * 4 + 4], axis=0)
        rows_hot = one_hot_rows(node_columns, node, 4 * rank)
        pack_ref[own, 0:features] = mm(rows_hot, kids).astype(jnp.bfloat16)
        transfer = lt[node * 4 : node * 4 + 4].reshape(4 * rank, rank)
        charge = mm_tn(transfer, jnp.concatenate(charges[node * 4 : node * 4 + 4], axis=0))
        pack_ref[own, features:] = charge.astype(jnp.bfloat16)
        last = slice(base + 2 * rank, base + 3 * rank)
        pack_ref[last, node * rank : (node + 1) * rank] = t[node]
    pack_ref[base + 2 * rank :, 2 * rank :] = jnp.zeros((rank, rank), jnp.bfloat16)
    rim_ref[0:512, :] = pack_ref[0:512, :]


def upper_kernel(own_ref, other_ref, us_ref, out_ref, transfers, *, total):
    _, core, chip, _, _ = place(total)
    cols = 128
    features = own_ref.shape[1] - cols
    base = own_ref.shape[0] - 384
    mine = pl.multiple_of(core * 256, 256)
    theirs = pl.multiple_of((1 - core) * 256, 256)
    for start, ref in ((mine, own_ref), (theirs, other_ref)):
        out_ref[pl.ds(start, 256), :] = ref[base : base + 256, :]
        transfers[pl.ds(start, 128), :] = ref[base + 256 : base + 384, 0:128]
        transfers[pl.ds(start + 128, 128), :] = ref[base + 256 : base + 384, 128:256]
    charge = mm_tn(transfers[...], out_ref[0:512, features:])
    out_ref[512:640, features:] = charge.astype(jnp.bfloat16)
    index = us_ref[pl.ds(chip, 1), :]
    columns = jnp.transpose(jnp.broadcast_to(index, (8, index.shape[1])))
    picked = mm(one_hot_rows(columns, 0, 512), out_ref[0:512, 0:features])
    out_ref[512:640, 0:features] = picked.astype(jnp.bfloat16)


def near_kernel(
    points, weights, ufar_ref, nfar_hbm, ncount_hbm, ucount_hbm, out_ref, mask_ref,
    nfar, ncount, ucount, sems, *, rows, total,
):
    _, _, chip, side_a, side_b = place(total)
    copies = fetch([(nfar_hbm, nfar), (ncount_hbm, ncount), (ucount_hbm, ucount)], sems)
    features = points.shape[1]
    same = lax.broadcasted_iota(jnp.int32, (rows, rows), 0) == lax.broadcasted_iota(
        jnp.int32, (rows, rows), 1
    )
    for leaf in range(points.shape[0] // rows):
        own = slice(leaf * rows, (leaf + 1) * rows)
        pts = points[own, :]
        col = norm_col(pts)
        row = jnp.concatenate([norm_row(col[0:128], 1), norm_row(col[128:256], 1)], axis=1)
        power = mm_nt(pts, pts) * (2.0 * scale_of(features)) + twice(col) + row
        tile = jnp.exp2(jnp.where(same, NEG, power)).astype(jnp.bfloat16)
        out_ref[own, :] = mm(tile, weights[own, :])
    for copy in copies:
        copy.wait()
    ncounts = count_column(ncount, 2)
    for at, ident in enumerate((chip, side_b, side_a)):
        mask_ref[at * 8 : at * 8 + 2, :] = hits(nfar[...], ncounts, ident * 4)
    ufar = ufar_ref[pl.ds(chip, 1), :]
    live = ucount[chip]
    for at, ident in enumerate((side_b, side_a)):
        used = jnp.zeros((1, 128), jnp.float32)
        for k in range(ufar.shape[1]):
            hit = (jnp.broadcast_to(ufar[:, k : k + 1], (1, 128)) == ident) & (k < live)
            used = jnp.where(hit, 1.0, used)
        mask_ref[24 + at : 25 + at, :] = used


def own_kernel(pack_ref, mask_ref, pot_ref, col_ref, rows_ref, block_ref, *, total):
    _, core, _, _, _ = place(total)
    features = pack_ref.shape[1] - pot_ref.shape[1]
    found = mask_ref[0:8, :]
    col_ref[...] = norm_col(pack_ref[0:1024, 0:features])
    for tree in range(4):
        here = group_rows(outer_first(core, tree, 4))
        used = [found[:, 2 * tree + h : 2 * tree + h + 1] for h in range(2)]
        fill_rows(rows_ref, tree, col_ref[here, :], used, 8)
    left = pack_ref[0:1024, 0:features]
    for source in range(4):
        src = outer_first(core, source, 4)
        here = slice(source * 256, source * 256 + 256)
        block_ref[:, here] = blocks(
            left, col_ref[...], pack_ref[here, 0:features],
            lambda at: rows_ref[src, pl.ds(tree_leaf(core, at), 1), :],
        )
    pot_ref[...] = mm(block_ref[...], pack_ref[0:1024, features:])


def side_kernel(
    pack_ref, side_ref, mask_ref, col_ref, start_ref, pot_ref, rows_ref, block_ref, *, total
):
    _, core, _, _, _ = place(total)
    features = pack_ref.shape[1] - pot_ref.shape[1]
    found = mask_ref[8:16, :]
    for tree in range(4):
        here = group_rows(outer_first(1 - core, tree, 4))
        used = [found[:, 2 * tree + h : 2 * tree + h + 1] for h in range(2)]
        fill_rows(rows_ref, tree, side_ref[here, 0:features], used, 8)
    for source in range(4):
        src = outer_first(1 - core, source, 4)
        here = slice(source * 256, source * 256 + 256)
        first = 3 - source
        block_ref[first * 256 :, here] = blocks(
            pack_ref[first * 256 : 1024, 0:features], col_ref[first * 256 :, :],
            side_ref[here, 0:features],
            lambda at: rows_ref[src, pl.ds(tree_leaf(core, at + 2 * first), 1), :],
        )
    for group in range(4):
        own = slice(group * 256, group * 256 + 256)
        span = slice((3 - group) * 256, 1024)
        pot_ref[own, :] = start_ref[own, :] + mm(block_ref[own, span], side_ref[span, features:])


def back_kernel(pack_ref, rim_ref, col_ref, ret_ref, rows_ref, *, total):
    _, core, _, _, _ = place(total)
    features = pack_ref.shape[1] - ret_ref.shape[1]
    found = rim_ref[512:528, 0:128].astype(jnp.float32)[0:8, :]
    left = rim_ref[0:512, 0:features]
    col = norm_col(left)
    parts = []
    for source in (2, 3):
        used = []
        for half in range(2):
            one = found[:, 2 * source + half : 2 * source + half + 1]
            other = found[:, 2 * (3 - source) + half : 2 * (3 - source) + half + 1]
            used.append(jnp.where(core == 0, one, other))
        here = slice(source * 256, source * 256 + 256)
        fill_rows(rows_ref, source, col_ref[here, :], used, 8)
        rows = 512 if source == 2 else 256
        parts.append(
            blocks(
                left[0:rows], col[0:rows], pack_ref[here, 0:features],
                lambda at: rows_ref[source, pl.ds(tree_leaf(1 - core, at), 1), :],
            )
        )
    both = jnp.concatenate([parts[0][0:256], parts[1]], axis=1)
    ret_ref[0:256, :] = mm(both, pack_ref[512:1024, features:]).astype(jnp.bfloat16)
    ret_ref[256:512, :] = mm(parts[0][256:512], pack_ref[512:768, features:]).astype(jnp.bfloat16)


def rim_kernel(
    pack_ref, rim_ref, mask_ref, col_ref, start_ref, pot_ref, rows_ref, block_ref, *, total
):
    _, core, _, _, _ = place(total)
    features = pack_ref.shape[1] - pot_ref.shape[1]
    found = mask_ref[16:24, :]
    for source in range(2):
        used = []
        for half in range(2):
            zero = found[:, 2 * source + half : 2 * source + half + 1]
            one = found[:, 2 * (3 - source) + half : 2 * (3 - source) + half + 1]
            used.append(jnp.where(core == 0, one, zero))
        here = slice(source * 256, source * 256 + 256)
        fill_rows(rows_ref, source, rim_ref[here, 0:features], used, 8)
        stop = 1024 - source * 256
        block_ref[0:stop, here] = blocks(
            pack_ref[0:stop, 0:features], col_ref[0:stop, :], rim_ref[here, 0:features],
            lambda at: rows_ref[source, pl.ds(tree_leaf(core, at), 1), :],
        )
    pot_ref[0:768, :] = start_ref[0:768, :] + mm(block_ref[0:768, :], rim_ref[0:512, features:])
    pot_ref[768:, :] = start_ref[768:, :] + mm(block_ref[768:, 0:256], rim_ref[0:256, features:])


def node_part(nodes_ref, ref, mask, core, rows_ref, features):
    own = nodes_ref[group_rows(core), 0:features]
    col = norm_col(own)
    parts = []
    for source in range(2):
        here = slice(source * 256, source * 256 + 256)
        used = [mask[:, 2 * source + h : 2 * source + h + 1] for h in range(2)]
        fill_rows(rows_ref, source, ref[here, 0:features], used, 2)
        parts.append(
            blocks(
                own, col, ref[here, 0:features], lambda at: rows_ref[source, at : at + 1, :]
            )
        )
    return mm(jnp.concatenate(parts, axis=1), ref[0:512, features:])


def upper_part(nodes_ref, ref, used, features):
    own = nodes_ref[512:640, 0:features]
    source = ref[512:640, 0:features]
    row = jnp.where(used > 0.0, norm_row(norm_col(source), 1), NEG)
    power = mm_nt(own, source) * (2.0 * scale_of(features)) + norm_col(own) + row
    return mm(jnp.exp2(power).astype(jnp.bfloat16), ref[512:640, features:])


def outer_node_kernel(
    nodes_ref, side_b_ref, mask_ref, far1_ref, far2_ref, rows_own, rows_ref, *, total
):
    _, core, _, _, _ = place(total)
    features = nodes_ref.shape[1] - far1_ref.shape[1]
    far2_ref[...] = upper_part(nodes_ref, side_b_ref, mask_ref[24:25, :], features)
    far1_ref[...] = node_part(
        nodes_ref, nodes_ref, mask_ref[0:2, :], core, rows_own, features
    ) + node_part(nodes_ref, side_b_ref, mask_ref[8:10, :], core, rows_ref, features)


def node_kernel(
    nodes_ref, side_a_ref, mask_ref, far1_ref, far2_ref, t, lt, pot_ref, out_ref, rows_ref, *, total
):
    _, core, _, _, _ = place(total)
    features = nodes_ref.shape[1] - pot_ref.shape[1]
    far2 = far2_ref[...] + upper_part(nodes_ref, side_a_ref, mask_ref[25:26, :], features)
    down2 = far2.astype(jnp.bfloat16)
    far1 = far1_ref[...] + node_part(
        nodes_ref, side_a_ref, mask_ref[16:18, :], core, rows_ref, features
    )
    rank = t.shape[1]
    for node in range(2):
        down1 = (far1[node * rank : (node + 1) * rank] + mm(t[node], down2)).astype(jnp.bfloat16)
        for leaf in range(node * 4, node * 4 + 4):
            start = outer_first(core, leaf // 2, 4) * 256 + (leaf % 2) * rank
            here = pl.ds(pl.multiple_of(start, 128), rank)
            out_ref[leaf * rank : (leaf + 1) * rank, :] = pot_ref[here, :] + mm(lt[leaf], down1)


def last_kernel(near_ref, pot_ref, ret_ref, basis, out_hbm, out_ref, sems, *, total):
    _, core, _, _, _ = place(total)
    leaves, rows, rank = basis.shape
    copies = []
    for leaf in range(leaves):
        group = outer_first(core, leaf // 2, 4)
        inside = jnp.minimum(group, 1) * 256 + (leaf % 2) * rank
        back = ret_ref[pl.ds(pl.multiple_of(inside, 128), rank), :].astype(jnp.float32)
        down0 = pot_ref[leaf * rank : (leaf + 1) * rank, :] + jnp.where(group < 2, back, 0.0)
        own = slice(leaf * rows, (leaf + 1) * rows)
        result = near_ref[own, :] + mm(basis[leaf], down0.astype(jnp.bfloat16))
        out_ref[own, :] = result.astype(jnp.bfloat16)
        if leaf % 4 == 3:
            done = pl.ds((leaf - 3) * rows, 4 * rows)
            copy = pltpu.make_async_copy(out_ref.at[done], out_hbm.at[done], sems.at[leaf // 4])
            copy.start()
            copies.append(copy)
    for copy in copies:
        copy.wait()


def call(kernel, outs, args, spaces, scratch=(), us=1.0, name=None, out_space=VMEM, after=()):
    kinds = {"v": VMEM, "h": HBM, "a": pl.ANY}
    n, skip = len(args), len(after)

    def body(*refs):
        kernel(*refs[:n], *refs[n + skip :])

    args = list(args) + list(after)
    spaces = spaces + "a" * skip
    args = [
        pltpu.with_memory_space_constraint(a, HBM) if k == "h" else a for a, k in zip(args, spaces)
    ]
    return pl.pallas_call(
        body,
        out_shape=outs,
        in_specs=[pl.BlockSpec(memory_space=kinds[k]) for k in spaces],
        out_specs=[pl.BlockSpec(memory_space=out_space)] * len(outs),
        scratch_shapes=list(scratch),
        compiler_params=pltpu.CompilerParams(vmem_limit_bytes=LIMIT),
        cost_estimate=pl.CostEstimate(flops=int(us * 1.15e9), bytes_accessed=0, transcendentals=0),
        name=name,
    )(*args)


def like(array, space=None):
    return (space or VMEM)(array.shape, array.dtype)


def per_device(
    points, weights, leaf_basis, leaf_transfer, node_transfer, leaf_skeleton, node_skeleton,
    upper_skeleton, leaf_far, leaf_count, node_far, node_count, upper_far, upper_count,
):
    leaves, rows, rank = leaf_basis.shape
    features = points.shape[1]
    cols = weights.shape[1]
    total = lax.axis_size("leaf")
    width = features + cols
    bf16, f32 = jnp.bfloat16, jnp.float32
    across = [(d, d ^ 1) for d in range(total)]
    outward = [(d, (d + 1) % total if d % 2 else (d - 1) % total) for d in range(total)]
    shape = jax.ShapeDtypeStruct
    sems = pltpu.SemaphoreType.DMA
    bind = functools.partial
    rows_scratch = pltpu.VMEM((leaves // 2, leaves, 256), f32)
    node_rows = pltpu.VMEM((2, 2, 256), f32)
    pot_shape = shape((leaves * rank, cols), f32)

    pack, rim, mask, us_v = call(
        bind(front_kernel, total=total),
        [
            shape((leaves * rank + 3 * rank, width), bf16),
            shape((4 * rank + 16, width), bf16),
            shape((24, 128), f32),
            shape(upper_skeleton.shape, upper_skeleton.dtype),
        ],
        [points, weights, leaf_basis, leaf_transfer, node_transfer, leaf_skeleton, node_skeleton,
         leaf_far, leaf_count, upper_skeleton],
        "hhhhhhhhhh",
        [like(points), like(weights), like(leaf_basis), like(leaf_transfer), like(node_transfer),
         like(leaf_skeleton), like(node_skeleton), like(leaf_far), like(leaf_count, SMEM),
         sems((13,))],
        name="front", us=2.5,
    )
    rim_in = lax.ppermute(rim, "leaf", outward)
    side = lax.ppermute(pack, "leaf", across)
    near, node_mask = call(
        bind(near_kernel, rows=rows, total=total),
        [shape((leaves * rows, cols), f32), shape((32, 128), f32)],
        [points, weights, upper_far, node_far, node_count, upper_count], "vvvhhh",
        [like(node_far), like(node_count, SMEM), like(upper_count, SMEM), sems((3,))],
        name="near", us=1.7,
    )
    (nodes,) = call(
        bind(upper_kernel, total=total),
        [shape((5 * rank, width), bf16)],
        [pack, side, us_v], "vvv",
        [pltpu.VMEM((4 * rank, rank), bf16)],
        name="upper", us=0.3, after=[node_mask],
    )
    nodes_b = lax.ppermute(nodes, "leaf", outward)
    pot, col = call(
        bind(own_kernel, total=total), [pot_shape, shape((leaves * rank, 128), f32)],
        [pack, mask], "vv", [rows_scratch, pltpu.VMEM((1024, 1024), bf16)],
        name="own", us=1.7, after=[nodes],
    )
    (ret,) = call(
        bind(back_kernel, total=total), [shape((4 * rank, cols), bf16)], [pack, rim_in, col],
        "vvv", [rows_scratch], name="back", us=1.3,
    )
    ret_in = lax.ppermute(ret, "leaf", outward)
    (pot,) = call(
        bind(side_kernel, total=total), [pot_shape], [pack, side, mask, col, pot], "vvvvv",
        [rows_scratch, pltpu.VMEM((1024, 1024), bf16)], name="side", us=0.1, after=[ret],
    )
    (pot,) = call(
        bind(rim_kernel, total=total), [pot_shape], [pack, rim_in, mask, col, pot], "vvvvv",
        [rows_scratch, pltpu.VMEM((1024, 512), bf16)], name="rim", us=0.1,
    )
    nodes_b, pot = lax.optimization_barrier((nodes_b, pot))
    nodes_a = lax.ppermute(nodes_b, "leaf", across)
    far1, far2 = call(
        bind(outer_node_kernel, total=total),
        [shape((2 * rank, cols), f32), shape((rank, cols), f32)],
        [nodes, nodes_b, node_mask], "vvv", [node_rows, node_rows],
        name="outer_node", us=0.1, after=[pot],
    )
    (pot,) = call(
        bind(node_kernel, total=total), [pot_shape],
        [nodes, nodes_a, node_mask, far1, far2, node_transfer, leaf_transfer, pot], "vvvvvvvv", [node_rows],
        name="node", us=0.1,
    )
    (out,) = call(
        bind(last_kernel, total=total),
        [shape((leaves * rows, cols), bf16)],
        [near, pot, ret_in, leaf_basis], "vvvv",
        [pltpu.VMEM((leaves * rows, cols), bf16), sems((2,))],
        name="last", us=1.9, out_space=HBM,
    )
    return out


def solution(mesh):
    placed = (
        P("leaf", None),
        P("leaf", "cols"),
        P("leaf", None, None),
        P("leaf", None, None),
        P("leaf", None, None),
        P("leaf", None),
        P("leaf", None),
        P(),
        P("leaf", None),
        P("leaf"),
        P("leaf", None),
        P("leaf"),
        P(),
        P(),
    )
    return jax.shard_map(
        per_device, mesh=mesh, in_specs=placed, out_specs=P("leaf", "cols"), check_vma=False
    )
```

time: 44.2 us -> 34.8 us (0.79)
  Pallas kernels: 24.2 us -> 12 us
  waiting for transfers between devices: 5.93 us -> 12 us
  starting transfers between devices: 13.4 us -> 9.21 us
  local copies, waits for them, and re-layouts: 0.09 us -> 1.33 us
    pallas_call x9 -> x10, Pallas kernels: 24.2 us -> 12 us  [call(): pl.pallas_call(body, out_shape=outs, in_specs=[pl.BlockSpec(memory_space=...]
    ppermute x1, starting transfers between devices: 0.1 us -> 8.15 us  [per_device(): rim_in = lax.ppermute(rim, 'leaf', outward)]
    ppermute x1, starting transfers between devices: 7.88 us -> 0.09 us  [per_device(): nodes_b = lax.ppermute(nodes, 'leaf', outward)]
    ppermute x1, waiting for transfers between devices: 1.38 us -> 6.73 us  [per_device(): nodes_b = lax.ppermute(nodes, 'leaf', outward)]
    ppermute x1, waiting for transfers between devices: 0.01 us -> 4.82 us  [per_device(): ret_in = lax.ppermute(ret, 'leaf', outward)]
    ppermute x1, starting transfers between devices: 5.33 us -> 0.87 us  [per_device(): ret_in = lax.ppermute(ret, 'leaf', outward)]
    ppermute x1, waiting for transfers between devices: 2.69 us -> 0.01 us  [per_device(): side = lax.ppermute(pack, 'leaf', across)]
    ppermute x1, waiting for transfers between devices: 1.85 us -> 0.36 us  [per_device(): rim_in = lax.ppermute(rim, 'leaf', outward)]
  transfers between devices with their start and end apart: 5 -> 5, of which waited for: 3 -> 4; matrix products, arithmetic and copies ran while one was open for 0% -> 0% of each run, Pallas kernels for 39% -> 24%
where the time goes in v3:
time: 34.8 us; the launch traced here: 34.7 us
  Pallas kernels  12 us (34%)
  waiting for transfers between devices  12 us (34%)
  starting transfers between devices  9.21 us (26%)
  local copies, waits for them, and re-layouts  1.33 us (4%)
    pallas_call x10, Pallas kernels, call(): pl.pallas_call(body, out_shape=outs, in_specs=[pl.BlockSpec(memory_space=...  12 us
    ppermute x1, starting transfers between devices, per_device(): rim_in = lax.ppermute(rim, 'leaf', outward)  8.15 us
    ppermute x1, waiting for transfers between devices, per_device(): nodes_b = lax.ppermute(nodes, 'leaf', outward)  6.73 us
    ppermute x1, waiting for transfers between devices, per_device(): ret_in = lax.ppermute(ret, 'leaf', outward)  4.82 us
    unnamed x13, local copies, waits for them, and re-layouts  1.33 us
    ppermute x1, starting transfers between devices, per_device(): ret_in = lax.ppermute(ret, 'leaf', outward)  0.87 us
  transfers between devices with their start and end apart: 5, of which 4 were waited for; matrix products, arithmetic and copies ran while one was open for 0% of the time, Pallas kernels for 24%

profile of v3, /device:TPU:16, one launch (start us, length us, event | category | flops | bytes accessed | tf_op | source)
XLA Modules:
  0.0 34.7 jit_solution(1933557560803262162)
XLA Ops:
  0.0 0.0 copy-start.3
  0.0 0.0 copy-start.5
  0.0 2.6 %front.1 = (bf16[1408,384]{1,0:T(8,128)(2,1)S(1)}, bf16[528,384]{1,0:T(8,128)(2,1)S(1)}, f32[24,128]{1,0:T(8,128)S(1)}, s32[32,128]{1,0:T(8,128)S(1)}) custom-call(bf16[2048,256]{1,0:T(8,128)(2,1)} %refs_0_.3, bf16[2048,128]{1,0:T(8,128)(2,1)} %refs_1_.3, bf16[8,256,128]{2,1,0:T(8,128)(2,1)} %refs_3_.5, bf16[8,128,128]{2,1,0:T(8,128)(2,1)} %refs_6_.3, ...), custom_call_target="tpu_custom_call" | custom-call | flops 2875000064 | tf_op jit(solution)/shard_map/front/pallas_call | solution.py:424
  2.6 0.1 collective-permute-start
  2.7 8.2 %collective-permute-start.2 = (bf16[528,384]{1,0:T(8,128)(2,1)S(1)}, bf16[528,384]{1,0:T(8,128)(2,1)S(1)}, u32[]{:S(2)}, u32[]{:S(2)}) collective-permute-start(bf16[528,384]{1,0:T(8,128)(2,1)S(1)} %get-tuple-element.21), channel_id=1, source_target_pairs={{0,252},{4,8},{8,4},{12,16},{16,12},{20,24},{24,20},{28,32},{32,28... | collective-permute-start | bytes 1216520 | tf_op jit(solution)/shard_map/ppermute | solution.py:475
  10.9 0.0 copy-done.5
  10.9 0.1 copy.15.refs_2_
  11.0 0.0 copy-done.3
  11.0 0.0 copy-start.2
  11.0 1.2 %copy-done.2 = bf16[2048,256]{1,0:T(8,128)(2,1)S(1)} copy-done((bf16[2048,256]{1,0:T(8,128)(2,1)S(1)}, bf16[2048,256]{1,0:T(8,128)(2,1)}, u32[]{:S(2)}) %copy-start.2) | copy-done | bytes 1048600
  12.2 1.7 %near.1 = (f32[2048,128]{1,0:T(8,128)S(1)}, f32[32,128]{1,0:T(8,128)S(1)}) custom-call(bf16[2048,256]{1,0:T(8,128)(2,1)S(1)} %copy-done.2, bf16[2048,128]{1,0:T(8,128)(2,1)S(1)} %copy-done.3, s32[32,12]{1,0:T(8,128)S(1)} %copy.15.refs_2_, s32[2,12]{1,0:T(2,128)} %refs_3_.3, s32[2]{0:T(128)} %refs_4_.2, s32[32]{0:T(128)} %refs_5_.3), custom_call_target="tpu_custom_call" | custom-call | flops 1955000064 | tf_op jit(solution)/shard_map/near/pallas_call | solution.py:424
  13.9 0.0 collective-permute-done.refs_1_
  13.9 0.3 upper.1.refs_2_.refs_0_
  14.3 0.1 collective-permute-start.1
  14.4 1.7 %own.1 = (f32[1024,128]{1,0:T(8,128)S(1)}, f32[1024,128]{1,0:T(8,128)S(1)}) custom-call(bf16[1408,384]{1,0:T(8,128)(2,1)S(1)} %get-tuple-element.18.refs_0_, f32[24,128]{1,0:T(8,128)S(1)} %get-tuple-element.22.refs_1_.refs_2_, bf16[640,384]{1,0:T(8,128)(2,1)S(1)} %upper.1.refs_2_.refs_0_), custom_call_target="tpu_custom_call" | custom-call | flops 1955000064 | tf_op jit(solution)/shard_map/own/pallas_call | solution.py:424
  16.1 0.4 %collective-permute-done.2.refs_1_ = bf16[528,384]{1,0:T(8,128)(2,1)S(1)} collective-permute-done((bf16[528,384]{1,0:T(8,128)(2,1)S(1)}, bf16[528,384]{1,0:T(8,128)(2,1)S(1)}, u32[]{:S(2)}, u32[]{:S(2)}) %collective-permute-start.2) | collective-permute-done | bytes 405536 | tf_op jit(solution)/shard_map/ppermute | solution.py:475
  16.5 0.6 %back.1.refs_5_ = bf16[512,128]{1,0:T(8,128)(2,1)S(1)} custom-call(bf16[1408,384]{1,0:T(8,128)(2,1)S(1)} %get-tuple-element.18.refs_0_, bf16[528,384]{1,0:T(8,128)(2,1)S(1)} %collective-permute-done.2.refs_1_, f32[1024,128]{1,0:T(8,128)S(1)} %get-tuple-element.23.refs_2_.refs_3_), custom_call_target="tpu_custom_call" | custom-call | flops 1495000064 | tf_op jit(solution)/shard_map/back/pallas_call | solution.py:424
  17.1 1.3 %side.1.refs_4_ = f32[1024,128]{1,0:T(8,128)S(1)} custom-call(bf16[1408,384]{1,0:T(8,128)(2,1)S(1)} %get-tuple-element.18.refs_0_, bf16[1408,384]{1,0:T(8,128)(2,1)S(1)} %collective-permute-done.refs_1_, f32[24,128]{1,0:T(8,128)S(1)} %get-tuple-element.22.refs_1_.refs_2_, f32[1024,128]{1,0:T(8,128)S(1)} %get-tuple-element.23.refs_2_.refs_3_, ...), custom_call_target="tpu_custom_call" | custom-call | flops 115000000 | tf_op jit(solution)/shard_map/side/pallas_call | solution.py:424
  18.3 0.8 %rim.1.refs_3_.refs_7_ = f32[1024,128]{1,0:T(8,128)S(1)} custom-call(bf16[1408,384]{1,0:T(8,128)(2,1)S(1)} %get-tuple-element.18.refs_0_, bf16[528,384]{1,0:T(8,128)(2,1)S(1)} %collective-permute-done.2.refs_1_, f32[24,128]{1,0:T(8,128)S(1)} %get-tuple-element.22.refs_1_.refs_2_, f32[1024,128]{1,0:T(8,128)S(1)} %get-tuple-element.23.refs_2_.refs_3_, ...), custom_call_target="tpu_custom_call" | custom-call | flops 115000000 | tf_op jit(solution)/shard_map/rim/pallas_call | solution.py:424
  19.2 0.0 copy-start
  19.2 0.0 copy-start.1
  19.2 6.7 %collective-permute-done.1.refs_1_ = bf16[640,384]{1,0:T(8,128)(2,1)S(1)} collective-permute-done((bf16[640,384]{1,0:T(8,128)(2,1)S(1)}, bf16[640,384]{1,0:T(8,128)(2,1)S(1)}, u32[]{:S(2)}, u32[]{:S(2)}) %collective-permute-start.1) | collective-permute-done | bytes 491552 | tf_op jit(solution)/shard_map/ppermute | solution.py:491
  25.9 0.0 collective-permute-start.3
  25.9 0.9 %collective-permute-start.4 = (bf16[512,128]{1,0:T(8,128)(2,1)S(1)}, bf16[512,128]{1,0:T(8,128)(2,1)S(1)}, u32[]{:S(2)}, u32[]{:S(2)}) collective-permute-start(bf16[512,128]{1,0:T(8,128)(2,1)S(1)} %back.1.refs_5_), channel_id=1, source_target_pairs={{0,252},{4,8},{8,4},{12,16},{16,12},{20,24},{24,20},{28,32},{32,28... | collective-permute-start | bytes 393224 | tf_op jit(solution)/shard_map/ppermute | solution.py:501
  26.8 0.9 %outer_node.1 = (f32[256,128]{1,0:T(8,128)S(1)}, f32[128,128]{1,0:T(8,128)S(1)}) custom-call(bf16[640,384]{1,0:T(8,128)(2,1)S(1)} %upper.1.refs_2_.refs_0_, bf16[640,384]{1,0:T(8,128)(2,1)S(1)} %collective-permute-done.1.refs_1_, f32[32,128]{1,0:T(8,128)S(1)} %get-tuple-element.20.refs_3_.refs_2_, f32[1024,128]{1,0:T(8,128)S(1)} %rim.1.refs_3_.refs_7_), custom_call_target="tpu_custom_call" | custom-call | flops 115000000 | tf_op jit(solution)/shard_map/outer_node/pallas_call | solution.py:424
  27.7 0.1 collective-permute-done.3.refs_1_
  27.8 0.0 copy-done
  27.8 0.0 copy-done.1
  27.8 1.0 %node.1.refs_1_ = f32[1024,128]{1,0:T(8,128)S(1)} custom-call(bf16[640,384]{1,0:T(8,128)(2,1)S(1)} %upper.1.refs_2_.refs_0_, bf16[640,384]{1,0:T(8,128)(2,1)S(1)} %collective-permute-done.3.refs_1_, f32[32,128]{1,0:T(8,128)S(1)} %get-tuple-element.20.refs_3_.refs_2_, f32[256,128]{1,0:T(8,128)S(1)} %get-tuple-element.27.refs_3_, ...), custom_call_target="tpu_custom_call" | custom-call | flops 115000000 | tf_op jit(solution)/shard_map/node/pallas_call | solution.py:424
  28.8 4.8 %collective-permute-done.4.refs_2_ = bf16[512,128]{1,0:T(8,128)(2,1)S(1)} collective-permute-done((bf16[512,128]{1,0:T(8,128)(2,1)S(1)}, bf16[512,128]{1,0:T(8,128)(2,1)S(1)}, u32[]{:S(2)}, u32[]{:S(2)}) %collective-permute-start.4) | collective-permute-done | bytes 131104 | tf_op jit(solution)/shard_map/ppermute | solution.py:501
  33.6 0.0 copy-done.4
  33.6 1.0 %last.1 = bf16[2048,128]{1,0:T(8,128)(2,1)} custom-call(f32[2048,128]{1,0:T(8,128)S(1)} %get-tuple-element.17.refs_0_, f32[1024,128]{1,0:T(8,128)S(1)} %node.1.refs_1_, bf16[512,128]{1,0:T(8,128)(2,1)S(1)} %collective-permute-done.4.refs_2_, bf16[8,256,128]{2,1,0:T(8,128)(2,1)S(1)} %copy-done.4), custom_call_target="tpu_custom_call" | custom-call | flops 2184999936 | tf_op jit(solution)/shard_map/last/pallas_call | solution.py:424
  (1 shorter events, 0.0 us)
Async XLA Ops:
  0.0 11.0 %copy-start.3 = (bf16[2048,128]{1,0:T(8,128)(2,1)S(1)}, bf16[2048,128]{1,0:T(8,128)(2,1)}, u32[]{:S(2)}) copy-start(bf16[2048,128]{1,0:T(8,128)(2,1)} %refs_1_.3) | copy-start | bytes 1572868
  0.0 10.9 %copy-start.5 = (s32[32,12]{0,1:T(8,128)S(1)}, s32[32,12]{0,1:T(8,128)}, u32[]{:S(2)}) copy-start(s32[32,12]{0,1:T(8,128)} %param.26) | copy-start | bytes 4612
  2.6 11.3 %collective-permute-start = (bf16[1408,384]{1,0:T(8,128)(2,1)S(1)}, bf16[1408,384]{1,0:T(8,128)(2,1)S(1)}, u32[]{:S(2)}, u32[]{:S(2)}) collective-permute-start(bf16[1408,384]{1,0:T(8,128)(2,1)S(1)} %get-tuple-element.18.refs_0_), channel_id=1, source_target_pairs={{0,4},{4,0},{8,12},{12,8},{16,20},{20,16},{24,28},{28,24},{32,36},... | collective-permute-start | bytes 3244040 | tf_op jit(solution)/shard_map/ppermute | solution.py:476
  2.7 13.7 %collective-permute-start.2 = (bf16[528,384]{1,0:T(8,128)(2,1)S(1)}, bf16[528,384]{1,0:T(8,128)(2,1)S(1)}, u32[]{:S(2)}, u32[]{:S(2)}) collective-permute-start(bf16[528,384]{1,0:T(8,128)(2,1)S(1)} %get-tuple-element.21), channel_id=1, source_target_pairs={{0,252},{4,8},{8,4},{12,16},{16,12},{20,24},{24,20},{28,32},{32,28... | collective-permute-start | bytes 1216520 | tf_op jit(solution)/shard_map/ppermute | solution.py:475
  11.0 1.2 %copy-start.2 = (bf16[2048,256]{1,0:T(8,128)(2,1)S(1)}, bf16[2048,256]{1,0:T(8,128)(2,1)}, u32[]{:S(2)}) copy-start(bf16[2048,256]{1,0:T(8,128)(2,1)} %refs_0_.3) | copy-start | bytes 3145732
  14.3 11.7 %collective-permute-start.1 = (bf16[640,384]{1,0:T(8,128)(2,1)S(1)}, bf16[640,384]{1,0:T(8,128)(2,1)S(1)}, u32[]{:S(2)}, u32[]{:S(2)}) collective-permute-start(bf16[640,384]{1,0:T(8,128)(2,1)S(1)} %upper.1.refs_2_.refs_0_), channel_id=1, source_target_pairs={{0,252},{4,8},{8,4},{12,16},{16,12},{20,24},{24,20},{28,32},{32,28... | collective-permute-start | bytes 1474568 | tf_op jit(solution)/shard_map/ppermute | solution.py:491
  19.2 8.6 %copy-start = (bf16[8,128,128]{2,1,0:T(8,128)(2,1)S(1)}, bf16[8,128,128]{2,1,0:T(8,128)(2,1)}, u32[]{:S(2)}) copy-start(bf16[8,128,128]{2,1,0:T(8,128)(2,1)} %refs_6_.3) | copy-start | bytes 786436
  19.2 8.6 %copy-start.1 = (bf16[2,128,128]{2,1,0:T(8,128)(2,1)S(1)}, bf16[2,128,128]{2,1,0:T(8,128)(2,1)}, u32[]{:S(2)}) copy-start(bf16[2,128,128]{2,1,0:T(8,128)(2,1)} %refs_5_.5) | copy-start | bytes 196612
  25.9 1.9 %collective-permute-start.3 = (bf16[640,384]{1,0:T(8,128)(2,1)S(1)}, bf16[640,384]{1,0:T(8,128)(2,1)S(1)}, u32[]{:S(2)}, u32[]{:S(2)}) collective-permute-start(bf16[640,384]{1,0:T(8,128)(2,1)S(1)} %collective-permute-done.1.refs_1_), channel_id=1, source_target_pairs={{0,4},{4,0},{8,12},{12,8},{16,20},{20,16},{24,28},{28,24},{32,36},... | collective-permute-start | bytes 1474568 | tf_op jit(solution)/shard_map/ppermute | solution.py:511
  25.9 7.7 %collective-permute-start.4 = (bf16[512,128]{1,0:T(8,128)(2,1)S(1)}, bf16[512,128]{1,0:T(8,128)(2,1)S(1)}, u32[]{:S(2)}, u32[]{:S(2)}) collective-permute-start(bf16[512,128]{1,0:T(8,128)(2,1)S(1)} %back.1.refs_5_), channel_id=1, source_target_pairs={{0,252},{4,8},{8,4},{12,16},{16,12},{20,24},{24,20},{28,32},{32,28... | collective-permute-start | bytes 393224 | tf_op jit(solution)/shard_map/ppermute | solution.py:501
  27.8 5.8 %copy-start.4 = (bf16[8,256,128]{2,1,0:T(8,128)(2,1)S(1)}, bf16[8,256,128]{2,1,0:T(8,128)(2,1)}, u32[]{:S(2)}) copy-start(bf16[8,256,128]{2,1,0:T(8,128)(2,1)} %refs_3_.5) | copy-start | bytes 1572868

commit v4 on v3

--- a/solution.py
+++ b/solution.py
@@ -207,11 +207,13 @@
 
 
 def near_kernel(
-    points, weights, ufar_ref, nfar_hbm, ncount_hbm, ucount_hbm, out_ref, mask_ref,
-    nfar, ncount, ucount, sems, *, rows, total,
+    points, weights, ufar_hbm, nfar_hbm, ncount_hbm, ucount_hbm, out_ref, mask_ref,
+    ufar, nfar, ncount, ucount, sems, *, rows, total,
 ):
     _, _, chip, side_a, side_b = place(total)
-    copies = fetch([(nfar_hbm, nfar), (ncount_hbm, ncount), (ucount_hbm, ucount)], sems)
+    copies = fetch(
+        [(ufar_hbm, ufar), (nfar_hbm, nfar), (ncount_hbm, ncount), (ucount_hbm, ucount)], sems
+    )
     features = points.shape[1]
     same = lax.broadcasted_iota(jnp.int32, (rows, rows), 0) == lax.broadcasted_iota(
         jnp.int32, (rows, rows), 1
@@ -229,14 +231,14 @@
     ncounts = count_column(ncount, 2)
     for at, ident in enumerate((chip, side_b, side_a)):
         mask_ref[at * 8 : at * 8 + 2, :] = hits(nfar[...], ncounts, ident * 4)
-    ufar = ufar_ref[pl.ds(chip, 1), :]
+    lists = ufar[...]
     live = ucount[chip]
+    mine = lax.broadcasted_iota(jnp.int32, lists.shape, 1) == chip
+    mine = mine & (lax.broadcasted_iota(jnp.int32, lists.shape, 0) < live)
     for at, ident in enumerate((side_b, side_a)):
-        used = jnp.zeros((1, 128), jnp.float32)
-        for k in range(ufar.shape[1]):
-            hit = (jnp.broadcast_to(ufar[:, k : k + 1], (1, 128)) == ident) & (k < live)
-            used = jnp.where(hit, 1.0, used)
-        mask_ref[24 + at : 25 + at, :] = used
+        hit = jnp.where(mine & (lists == ident), 1.0, 0.0)
+        used = jnp.max(jnp.max(hit, axis=0, keepdims=True), axis=1, keepdims=True)
+        mask_ref[24 + at : 25 + at, :] = jnp.broadcast_to(used, (1, 128))
 
 
 def own_kernel(pack_ref, mask_ref, pot_ref, col_ref, rows_ref, block_ref, *, total):
@@ -369,55 +371,63 @@
     ) + node_part(nodes_ref, side_b_ref, mask_ref[8:10, :], core, rows_ref, features)
 
 
-def node_kernel(
-    nodes_ref, side_a_ref, mask_ref, far1_ref, far2_ref, t, lt, pot_ref, out_ref, rows_ref, *, total
+def merge_kernel(pot_ref, ret_ref, out_ref, *, total):
+    _, core, _, _, _ = place(total)
+    for group in range(4):
+        own = slice(group * 256, group * 256 + 256)
+        part = pot_ref[own, :]
+        if group < 2:
+            part = part + ret_ref[own, :].astype(jnp.float32)
+        out_ref[group_rows(outer_first(core, group, 4)), :] = part
+
+
+def final_kernel(
+    nodes_ref, side_a_ref, mask_ref, far1_ref, far2_ref, t, lt, pot_ref, near_ref, basis,
+    out_hbm, rows_ref, out_ref, sems, *, total,
 ):
     _, core, _, _, _ = place(total)
     features = nodes_ref.shape[1] - pot_ref.shape[1]
+    leaves, rows, rank = basis.shape
     far2 = far2_ref[...] + upper_part(nodes_ref, side_a_ref, mask_ref[25:26, :], features)
-    down2 = far2.astype(jnp.bfloat16)
     far1 = far1_ref[...] + node_part(
         nodes_ref, side_a_ref, mask_ref[16:18, :], core, rows_ref, features
     )
-    rank = t.shape[1]
+    down2 = far2.astype(jnp.bfloat16)
+    down1 = (far1 + mm(t[...].reshape(2 * rank, rank), down2)).astype(jnp.bfloat16)
+    down0 = []
     for node in range(2):
-        down1 = (far1[node * rank : (node + 1) * rank] + mm(t[node], down2)).astype(jnp.bfloat16)
-        for leaf in range(node * 4, node * 4 + 4):
-            start = outer_first(core, leaf // 2, 4) * 256 + (leaf % 2) * rank
-            here = pl.ds(pl.multiple_of(start, 128), rank)
-            out_ref[leaf * rank : (leaf + 1) * rank, :] = pot_ref[here, :] + mm(lt[leaf], down1)
-
-
-def last_kernel(near_ref, pot_ref, ret_ref, basis, out_hbm, out_ref, sems, *, total):
-    _, core, _, _, _ = place(total)
-    leaves, rows, rank = basis.shape
+        own = slice(node * 4 * rank, (node + 1) * 4 * rank)
+        transfer = lt[node * 4 : node * 4 + 4].reshape(4 * rank, rank)
+        lower = pot_ref[own, :] + mm(transfer, down1[node * rank : (node + 1) * rank])
+        down0.append(lower.astype(jnp.bfloat16))
     copies = []
-    for leaf in range(leaves):
-        group = outer_first(core, leaf // 2, 4)
-        inside = jnp.minimum(group, 1) * 256 + (leaf % 2) * rank
-        back = ret_ref[pl.ds(pl.multiple_of(inside, 128), rank), :].astype(jnp.float32)
-        down0 = pot_ref[leaf * rank : (leaf + 1) * rank, :] + jnp.where(group < 2, back, 0.0)
-        own = slice(leaf * rows, (leaf + 1) * rows)
-        result = near_ref[own, :] + mm(basis[leaf], down0.astype(jnp.bfloat16))
-        out_ref[own, :] = result.astype(jnp.bfloat16)
-        if leaf % 4 == 3:
-            done = pl.ds((leaf - 3) * rows, 4 * rows)
-            copy = pltpu.make_async_copy(out_ref.at[done], out_hbm.at[done], sems.at[leaf // 4])
-            copy.start()
-            copies.append(copy)
+    for node in range(2):
+        results = []
+        for leaf in range(4):
+            at = node * 4 + leaf
+            lower = down0[node][leaf * rank : (leaf + 1) * rank]
+            own = slice(at * rows, (at + 1) * rows)
+            results.append((near_ref[own, :] + mm(basis[at], lower)).astype(jnp.bfloat16))
+        for leaf in range(4):
+            at = node * 4 + leaf
+            out_ref[at * rows : (at + 1) * rows, :] = results[leaf]
+        done = pl.ds(node * 4 * rows, 4 * rows)
+        copy = pltpu.make_async_copy(out_ref.at[done], out_hbm.at[done], sems.at[node])
+        copy.start()
+        copies.append(copy)
     for copy in copies:
         copy.wait()
 
 
-def call(kernel, outs, args, spaces, scratch=(), us=1.0, name=None, out_space=VMEM, after=()):
+def call(kernel, outs, args, spaces, scratch=(), us=1.0, name=None, out_space=VMEM, after=(), early=()):
     kinds = {"v": VMEM, "h": HBM, "a": pl.ANY}
-    n, skip = len(args), len(after)
+    n, skip = len(args), len(after) + len(early)
 
     def body(*refs):
         kernel(*refs[:n], *refs[n + skip :])
 
-    args = list(args) + list(after)
-    spaces = spaces + "a" * skip
+    args = list(args) + list(after) + list(early)
+    spaces = spaces + "a" * len(after) + "v" * len(early)
     args = [
         pltpu.with_memory_space_constraint(a, HBM) if k == "h" else a for a, k in zip(args, spaces)
     ]
@@ -474,29 +484,30 @@
     )
     rim_in = lax.ppermute(rim, "leaf", outward)
     side = lax.ppermute(pack, "leaf", across)
-    near, node_mask = call(
-        bind(near_kernel, rows=rows, total=total),
-        [shape((leaves * rows, cols), f32), shape((32, 128), f32)],
-        [points, weights, upper_far, node_far, node_count, upper_count], "vvvhhh",
-        [like(node_far), like(node_count, SMEM), like(upper_count, SMEM), sems((3,))],
-        name="near", us=1.7,
+    pot, col = call(
+        bind(own_kernel, total=total), [pot_shape, shape((leaves * rank, 128), f32)],
+        [pack, mask], "vv", [rows_scratch, pltpu.VMEM((1024, 1024), bf16)],
+        name="own", us=1.7,
     )
     (nodes,) = call(
         bind(upper_kernel, total=total),
         [shape((5 * rank, width), bf16)],
         [pack, side, us_v], "vvv",
         [pltpu.VMEM((4 * rank, rank), bf16)],
-        name="upper", us=0.3, after=[node_mask],
+        name="upper", us=0.3, after=[col],
     )
     nodes_b = lax.ppermute(nodes, "leaf", outward)
-    pot, col = call(
-        bind(own_kernel, total=total), [pot_shape, shape((leaves * rank, 128), f32)],
-        [pack, mask], "vv", [rows_scratch, pltpu.VMEM((1024, 1024), bf16)],
-        name="own", us=1.7, after=[nodes],
+    upper_lists = jnp.transpose(upper_far)
+    near, node_mask = call(
+        bind(near_kernel, rows=rows, total=total),
+        [shape((leaves * rows, cols), f32), shape((32, 128), f32)],
+        [points, weights, upper_lists, node_far, node_count, upper_count], "vvhhhh",
+        [like(upper_lists), like(node_far), like(node_count, SMEM), like(upper_count, SMEM), sems((4,))],
+        name="near", us=1.7, after=[nodes],
     )
     (ret,) = call(
         bind(back_kernel, total=total), [shape((4 * rank, cols), bf16)], [pack, rim_in, col],
-        "vvv", [rows_scratch], name="back", us=1.3,
+        "vvv", [rows_scratch], name="back", us=1.3, after=[node_mask],
     )
     ret_in = lax.ppermute(ret, "leaf", outward)
     (pot,) = call(
@@ -505,7 +516,7 @@
     )
     (pot,) = call(
         bind(rim_kernel, total=total), [pot_shape], [pack, rim_in, mask, col, pot], "vvvvv",
-        [rows_scratch, pltpu.VMEM((1024, 512), bf16)], name="rim", us=0.1,
+        [rows_scratch, pltpu.VMEM((1024, 512), bf16)], name="rim", us=0.1, early=[leaf_basis, leaf_transfer, node_transfer],
     )
     nodes_b, pot = lax.optimization_barrier((nodes_b, pot))
     nodes_a = lax.ppermute(nodes_b, "leaf", across)
@@ -516,16 +527,17 @@
         name="outer_node", us=0.1, after=[pot],
     )
     (pot,) = call(
-        bind(node_kernel, total=total), [pot_shape],
-        [nodes, nodes_a, node_mask, far1, far2, node_transfer, leaf_transfer, pot], "vvvvvvvv", [node_rows],
-        name="node", us=0.1,
+        bind(merge_kernel, total=total), [pot_shape], [pot, ret_in], "vv", name="merge", us=5.0,
+        after=[far2],
     )
     (out,) = call(
-        bind(last_kernel, total=total),
+        bind(final_kernel, total=total),
         [shape((leaves * rows, cols), bf16)],
-        [near, pot, ret_in, leaf_basis], "vvvv",
-        [pltpu.VMEM((leaves * rows, cols), bf16), sems((2,))],
-        name="last", us=1.9, out_space=HBM,
+        [nodes, nodes_a, node_mask, far1, far2, node_transfer, leaf_transfer, pot, near,
+         leaf_basis],
+        "vvvvvvvvvv",
+        [node_rows, pltpu.VMEM((leaves * rows, cols), bf16), sems((2,))],
+        name="final", us=1.9, out_space=HBM,
     )
     return out
 

time: 34.8 us -> 29.6 us (0.85)
  the two profiles are of different devices: /device:TPU:16 before, /device:TPU:1 now
where the time goes in v4:
time: 29.6 us; the launch traced here: 29.4 us
  starting transfers between devices  12.4 us (42%)
  Pallas kernels  12 us (41%)
  waiting for transfers between devices  4.91 us (17%)
    pallas_call x10, Pallas kernels, call(): pl.pallas_call(body, out_shape=outs, in_specs=[pl.BlockSpec(memory_space=...  12 us
    ppermute x1, starting transfers between devices, per_device(): nodes_a = lax.ppermute(nodes_b, 'leaf', across)  7.66 us
    ppermute x1, starting transfers between devices, per_device(): side = lax.ppermute(pack, 'leaf', across)  3.33 us
    ppermute x1, waiting for transfers between devices, per_device(): nodes_b = lax.ppermute(nodes, 'leaf', outward)  2.01 us
    ppermute x1, waiting for transfers between devices, per_device(): rim_in = lax.ppermute(rim, 'leaf', outward)  1.87 us
    ppermute x1, starting transfers between devices, per_device(): nodes_b = lax.ppermute(nodes, 'leaf', outward)  1.33 us
  transfers between devices with their start and end apart: 5, of which 4 were waited for; matrix products, arithmetic and copies ran while one was open for 0% of the time, Pallas kernels for 26%

profile of v4, /device:TPU:1, one launch (start us, length us, event | category | flops | bytes accessed | tf_op | source)
XLA Modules:
  0.0 29.4 jit_solution(691367112370615865)
XLA Ops:
  0.0 2.5 %front.1 = (bf16[1408,384]{1,0:T(8,128)(2,1)S(1)}, bf16[528,384]{1,0:T(8,128)(2,1)S(1)}, f32[24,128]{1,0:T(8,128)S(1)}, s32[32,128]{1,0:T(8,128)S(1)}) custom-call(bf16[2048,256]{1,0:T(8,128)(2,1)} %refs_0_.3, bf16[2048,128]{1,0:T(8,128)(2,1)} %refs_1_.3, bf16[8,256,128]{2,1,0:T(8,128)(2,1)} %refs_9_.3, bf16[8,128,128]{2,1,0:T(8,128)(2,1)} %refs_6_.5, ...), custom_call_target="tpu_custom_call" | custom-call | flops 2875000064 | tf_op jit(solution)/shard_map/front/pallas_call | solution.py:434
  2.5 3.3 %collective-permute-start = (bf16[1408,384]{1,0:T(8,128)(2,1)S(1)}, bf16[1408,384]{1,0:T(8,128)(2,1)S(1)}, u32[]{:S(2)}, u32[]{:S(2)}) collective-permute-start(bf16[1408,384]{1,0:T(8,128)(2,1)S(1)} %get-tuple-element.17.refs_0_), channel_id=1, source_target_pairs={{0,4},{4,0},{8,12},{12,8},{16,20},{20,16},{24,28},{28,24},{32,36},... | collective-permute-start | bytes 3244040 | tf_op jit(solution)/shard_map/ppermute | solution.py:486
  5.9 0.0 collective-permute-start.2
  5.9 1.8 %own.1 = (f32[1024,128]{1,0:T(8,128)S(1)}, f32[1024,128]{1,0:T(8,128)S(1)}) custom-call(bf16[1408,384]{1,0:T(8,128)(2,1)S(1)} %get-tuple-element.17.refs_0_, f32[24,128]{1,0:T(8,128)S(1)} %get-tuple-element.19.refs_1_.refs_2_), custom_call_target="tpu_custom_call" | custom-call | flops 1955000064 | tf_op jit(solution)/shard_map/own/pallas_call | solution.py:434
  7.7 0.5 %collective-permute-done.refs_1_ = bf16[1408,384]{1,0:T(8,128)(2,1)S(1)} collective-permute-done((bf16[1408,384]{1,0:T(8,128)(2,1)S(1)}, bf16[1408,384]{1,0:T(8,128)(2,1)S(1)}, u32[]{:S(2)}, u32[]{:S(2)}) %collective-permute-start) | collective-permute-done | bytes 1081376 | tf_op jit(solution)/shard_map/ppermute | solution.py:486
  8.2 0.0 copy-start.3
  8.2 0.0 copy-start.4
  8.2 0.3 %upper.1.refs_6_.refs_0_ = bf16[640,384]{1,0:T(8,128)(2,1)S(1)} custom-call(bf16[1408,384]{1,0:T(8,128)(2,1)S(1)} %get-tuple-element.17.refs_0_, bf16[1408,384]{1,0:T(8,128)(2,1)S(1)} %collective-permute-done.refs_1_, s32[32,128]{1,0:T(8,128)S(1)} %get-tuple-element.18.refs_2_, f32[1024,128]{1,0:T(8,128)S(1)} %get-tuple-element.20.refs_3_.refs_2_), custom_call_target="tpu_custom_call" | custom-call | flops 345000000 | tf_op jit(solution)/shard_map/upper/pallas_call | solution.py:434
  8.5 1.3 %collective-permute-start.1 = (bf16[640,384]{1,0:T(8,128)(2,1)S(1)}, bf16[640,384]{1,0:T(8,128)(2,1)S(1)}, u32[]{:S(2)}, u32[]{:S(2)}) collective-permute-start(bf16[640,384]{1,0:T(8,128)(2,1)S(1)} %upper.1.refs_6_.refs_0_), channel_id=1, source_target_pairs={{0,252},{4,8},{8,4},{12,16},{16,12},{20,24},{24,20},{28,32},{32,28... | collective-permute-start | bytes 1474568 | tf_op jit(solution)/shard_map/ppermute | solution.py:499
  9.9 0.0 copy-done.3
  9.9 0.0 copy-done.4
  9.9 1.7 %near.1 = (f32[2048,128]{1,0:T(8,128)S(1)}, f32[32,128]{1,0:T(8,128)S(1)}) custom-call(bf16[2048,256]{1,0:T(8,128)(2,1)S(1)} %copy-done.3, bf16[2048,128]{1,0:T(8,128)(2,1)S(1)} %copy-done.4, s32[12,32]{1,0:T(8,128)} %bitcast.1, s32[2,12]{1,0:T(2,128)} %refs_3_.3, s32[2]{0:T(128)} %refs_4_.3, s32[32]{0:T(128)} %refs_5_.5, ...), custom_call_target="tpu_custom_call" | custom-call | flops 1955000064 | tf_op jit(solution)/shard_map/near/pallas_call | solution.py:434
  11.6 1.9 %collective-permute-done.2.refs_1_ = bf16[528,384]{1,0:T(8,128)(2,1)S(1)} collective-permute-done((bf16[528,384]{1,0:T(8,128)(2,1)S(1)}, bf16[528,384]{1,0:T(8,128)(2,1)S(1)}, u32[]{:S(2)}, u32[]{:S(2)}) %collective-permute-start.2) | collective-permute-done | bytes 405536 | tf_op jit(solution)/shard_map/ppermute | solution.py:485
  13.5 0.6 %back.1.refs_5_ = bf16[512,128]{1,0:T(8,128)(2,1)S(1)} custom-call(bf16[1408,384]{1,0:T(8,128)(2,1)S(1)} %get-tuple-element.17.refs_0_, bf16[528,384]{1,0:T(8,128)(2,1)S(1)} %collective-permute-done.2.refs_1_, f32[1024,128]{1,0:T(8,128)S(1)} %get-tuple-element.20.refs_3_.refs_2_, f32[32,128]{1,0:T(8,128)S(1)} %get-tuple-element.23.refs_3_.refs_2_), custom_call_target="tpu_custom_call" | custom-call | flops 1495000064 | tf_op jit(solution)/shard_map/back/pallas_call | solution.py:434
  14.1 0.1 collective-permute-start.4
  14.2 0.0 copy-start
  14.2 0.0 copy-start.1
  14.2 0.0 copy-start.2
  14.3 1.3 %side.1.refs_4_ = f32[1024,128]{1,0:T(8,128)S(1)} custom-call(bf16[1408,384]{1,0:T(8,128)(2,1)S(1)} %get-tuple-element.17.refs_0_, bf16[1408,384]{1,0:T(8,128)(2,1)S(1)} %collective-permute-done.refs_1_, f32[24,128]{1,0:T(8,128)S(1)} %get-tuple-element.19.refs_1_.refs_2_, f32[1024,128]{1,0:T(8,128)S(1)} %get-tuple-element.20.refs_3_.refs_2_, ...), custom_call_target="tpu_custom_call" | custom-call | flops 115000000 | tf_op jit(solution)/shard_map/side/pallas_call | solution.py:434
  15.6 0.0 copy-done
  15.6 0.0 copy-done.1
  15.6 0.0 copy-done.2
  15.6 0.8 %rim.1.refs_3_.refs_0_ = f32[1024,128]{1,0:T(8,128)S(1)} custom-call(bf16[1408,384]{1,0:T(8,128)(2,1)S(1)} %get-tuple-element.17.refs_0_, bf16[528,384]{1,0:T(8,128)(2,1)S(1)} %collective-permute-done.2.refs_1_, f32[24,128]{1,0:T(8,128)S(1)} %get-tuple-element.19.refs_1_.refs_2_, f32[1024,128]{1,0:T(8,128)S(1)} %get-tuple-element.20.refs_3_.refs_2_, ...), custom_call_target="tpu_custom_call" | custom-call | flops 115000000 | tf_op jit(solution)/shard_map/rim/pallas_call | solution.py:434
  16.5 2.0 %collective-permute-done.1.refs_1_ = bf16[640,384]{1,0:T(8,128)(2,1)S(1)} collective-permute-done((bf16[640,384]{1,0:T(8,128)(2,1)S(1)}, bf16[640,384]{1,0:T(8,128)(2,1)S(1)}, u32[]{:S(2)}, u32[]{:S(2)}) %collective-permute-start.1) | collective-permute-done | bytes 491552 | tf_op jit(solution)/shard_map/ppermute | solution.py:499
  18.5 7.7 %collective-permute-start.3 = (bf16[640,384]{1,0:T(8,128)(2,1)S(1)}, bf16[640,384]{1,0:T(8,128)(2,1)S(1)}, u32[]{:S(2)}, u32[]{:S(2)}) collective-permute-start(bf16[640,384]{1,0:T(8,128)(2,1)S(1)} %collective-permute-done.1.refs_1_), channel_id=1, source_target_pairs={{0,4},{4,0},{8,12},{12,8},{16,20},{20,16},{24,28},{28,24},{32,36},... | collective-permute-start | bytes 1474568 | tf_op jit(solution)/shard_map/ppermute | solution.py:522
  26.1 0.9 %outer_node.1 = (f32[256,128]{1,0:T(8,128)S(1)}, f32[128,128]{1,0:T(8,128)S(1)}) custom-call(bf16[640,384]{1,0:T(8,128)(2,1)S(1)} %upper.1.refs_6_.refs_0_, bf16[640,384]{1,0:T(8,128)(2,1)S(1)} %collective-permute-done.1.refs_1_, f32[32,128]{1,0:T(8,128)S(1)} %get-tuple-element.23.refs_3_.refs_2_, f32[1024,128]{1,0:T(8,128)S(1)} %rim.1.refs_3_.refs_0_), custom_call_target="tpu_custom_call" | custom-call | flops 115000000 | tf_op jit(solution)/shard_map/outer_node/pallas_call | solution.py:434
  27.1 0.0 collective-permute-done.4.refs_1_
  27.1 0.1 merge.1.refs_7_
  27.1 0.5 %collective-permute-done.3.refs_1_ = bf16[640,384]{1,0:T(8,128)(2,1)S(1)} collective-permute-done((bf16[640,384]{1,0:T(8,128)(2,1)S(1)}, bf16[640,384]{1,0:T(8,128)(2,1)S(1)}, u32[]{:S(2)}, u32[]{:S(2)}) %collective-permute-start.3) | collective-permute-done | bytes 491552 | tf_op jit(solution)/shard_map/ppermute | solution.py:522
  27.6 1.8 %final.1 = bf16[2048,128]{1,0:T(8,128)(2,1)} custom-call(bf16[640,384]{1,0:T(8,128)(2,1)S(1)} %upper.1.refs_6_.refs_0_, bf16[640,384]{1,0:T(8,128)(2,1)S(1)} %collective-permute-done.3.refs_1_, f32[32,128]{1,0:T(8,128)S(1)} %get-tuple-element.23.refs_3_.refs_2_, f32[256,128]{1,0:T(8,128)S(1)} %get-tuple-element.26.refs_3_, ...), custom_call_target="tpu_custom_call" | custom-call | flops 2184999936 | tf_op jit(solution)/shard_map/final/pallas_call | solution.py:434
Async XLA Ops:
  2.5 5.7 %collective-permute-start = (bf16[1408,384]{1,0:T(8,128)(2,1)S(1)}, bf16[1408,384]{1,0:T(8,128)(2,1)S(1)}, u32[]{:S(2)}, u32[]{:S(2)}) collective-permute-start(bf16[1408,384]{1,0:T(8,128)(2,1)S(1)} %get-tuple-element.17.refs_0_), channel_id=1, source_target_pairs={{0,4},{4,0},{8,12},{12,8},{16,20},{20,16},{24,28},{28,24},{32,36},... | collective-permute-start | bytes 3244040 | tf_op jit(solution)/shard_map/ppermute | solution.py:486
  5.9 7.6 %collective-permute-start.2 = (bf16[528,384]{1,0:T(8,128)(2,1)S(1)}, bf16[528,384]{1,0:T(8,128)(2,1)S(1)}, u32[]{:S(2)}, u32[]{:S(2)}) collective-permute-start(bf16[528,384]{1,0:T(8,128)(2,1)S(1)} %get-tuple-element.21), channel_id=1, source_target_pairs={{0,252},{4,8},{8,4},{12,16},{16,12},{20,24},{24,20},{28,32},{32,28... | collective-permute-start | bytes 1216520 | tf_op jit(solution)/shard_map/ppermute | solution.py:485
  8.2 1.7 %copy-start.3 = (bf16[2048,256]{1,0:T(8,128)(2,1)S(1)}, bf16[2048,256]{1,0:T(8,128)(2,1)}, u32[]{:S(2)}) copy-start(bf16[2048,256]{1,0:T(8,128)(2,1)} %refs_0_.3) | copy-start | bytes 3145732
  8.2 1.7 %copy-start.4 = (bf16[2048,128]{1,0:T(8,128)(2,1)S(1)}, bf16[2048,128]{1,0:T(8,128)(2,1)}, u32[]{:S(2)}) copy-start(bf16[2048,128]{1,0:T(8,128)(2,1)} %refs_1_.3) | copy-start | bytes 1572868
  8.5 9.9 %collective-permute-start.1 = (bf16[640,384]{1,0:T(8,128)(2,1)S(1)}, bf16[640,384]{1,0:T(8,128)(2,1)S(1)}, u32[]{:S(2)}, u32[]{:S(2)}) collective-permute-start(bf16[640,384]{1,0:T(8,128)(2,1)S(1)} %upper.1.refs_6_.refs_0_), channel_id=1, source_target_pairs={{0,252},{4,8},{8,4},{12,16},{16,12},{20,24},{24,20},{28,32},{32,28... | collective-permute-start | bytes 1474568 | tf_op jit(solution)/shard_map/ppermute | solution.py:499
  14.1 12.9 %collective-permute-start.4 = (bf16[512,128]{1,0:T(8,128)(2,1)S(1)}, bf16[512,128]{1,0:T(8,128)(2,1)S(1)}, u32[]{:S(2)}, u32[]{:S(2)}) collective-permute-start(bf16[512,128]{1,0:T(8,128)(2,1)S(1)} %back.1.refs_5_), channel_id=1, source_target_pairs={{0,252},{4,8},{8,4},{12,16},{16,12},{20,24},{24,20},{28,32},{32,28... | collective-permute-start | bytes 393224 | tf_op jit(solution)/shard_map/ppermute | solution.py:512
  14.2 1.4 %copy-start = (bf16[8,256,128]{2,1,0:T(8,128)(2,1)S(1)}, bf16[8,256,128]{2,1,0:T(8,128)(2,1)}, u32[]{:S(2)}) copy-start(bf16[8,256,128]{2,1,0:T(8,128)(2,1)} %refs_9_.3) | copy-start | bytes 1572868
  14.2 1.4 %copy-start.1 = (bf16[8,128,128]{2,1,0:T(8,128)(2,1)S(1)}, bf16[8,128,128]{2,1,0:T(8,128)(2,1)}, u32[]{:S(2)}) copy-start(bf16[8,128,128]{2,1,0:T(8,128)(2,1)} %refs_6_.5) | copy-start | bytes 786436
  14.2 1.4 %copy-start.2 = (bf16[2,128,128]{2,1,0:T(8,128)(2,1)S(1)}, bf16[2,128,128]{2,1,0:T(8,128)(2,1)}, u32[]{:S(2)}) copy-start(bf16[2,128,128]{2,1,0:T(8,128)(2,1)} %refs_5_.7) | copy-start | bytes 196612
  18.5 9.2 %collective-permute-start.3 = (bf16[640,384]{1,0:T(8,128)(2,1)S(1)}, bf16[640,384]{1,0:T(8,128)(2,1)S(1)}, u32[]{:S(2)}, u32[]{:S(2)}) collective-permute-start(bf16[640,384]{1,0:T(8,128)(2,1)S(1)} %collective-permute-done.1.refs_1_), channel_id=1, source_target_pairs={{0,4},{4,0},{8,12},{12,8},{16,20},{20,16},{24,28},{28,24},{32,36},... | collective-permute-start | bytes 1474568 | tf_op jit(solution)/shard_map/ppermute | solution.py:522

commit v5 on v4

--- a/solution.py
+++ b/solution.py
@@ -130,7 +130,8 @@
     features = points.shape[1]
     cols = weights.shape[1]
     small = [(ls_hbm, ls), (ns_hbm, ns), (far_hbm, far), (count_hbm, count), (us_hbm, us)]
-    pairs = list(small)
+    pairs = small + [(lt_hbm, lt), (t_hbm, t)]
+    ahead = len(pairs)
     part = leaves // 2
     for half in range(2):
         own = pl.ds(half * part * rows, part * rows)
@@ -140,7 +141,6 @@
             (weights_hbm.at[own], weights.at[own]),
             (basis_hbm.at[some], basis.at[some]),
         ]
-    pairs += [(lt_hbm, lt), (t_hbm, t)]
     copies = fetch(pairs, sems)
     for copy in copies[: len(small)]:
         copy.wait()
@@ -159,7 +159,7 @@
     base = leaves * rank
     for leaf in range(leaves):
         if leaf % part == 0:
-            first = len(small) + 3 * (leaf // part)
+            first = ahead + 3 * (leaf // part)
             for copy in copies[first : first + 3]:
                 copy.wait()
         own = slice(leaf * rows, (leaf + 1) * rows)
@@ -171,7 +171,7 @@
         pack_ref[here, features:] = charge
         picked.append(skel)
         charges.append(charge)
-    for copy in copies[len(small) + 6 :]:
+    for copy in copies[len(small) : ahead]:
         copy.wait()
     for node in range(nodes):
         own = slice(base + node * rank, base + (node + 1) * rank)
@@ -187,23 +187,30 @@
     rim_ref[0:512, :] = pack_ref[0:512, :]
 
 
-def upper_kernel(own_ref, other_ref, us_ref, out_ref, transfers, *, total):
+def upper_points(points, index):
+    columns = jnp.transpose(jnp.broadcast_to(index, (8, index.shape[1])))
+    return mm(one_hot_rows(columns, 0, 512), points).astype(jnp.bfloat16)
+
+
+def node_points(ref, start, count):
+    stop = start + count
+    return jnp.concatenate([ref[start:stop, :], ref[512 + start : 512 + stop, :]], axis=1)
+
+
+def upper_kernel(own_ref, other_ref, us_ref, out_ref, points_ref, transfers, *, total):
     _, core, chip, _, _ = place(total)
-    cols = 128
-    features = own_ref.shape[1] - cols
     base = own_ref.shape[0] - 384
     mine = pl.multiple_of(core * 256, 256)
     theirs = pl.multiple_of((1 - core) * 256, 256)
     for start, ref in ((mine, own_ref), (theirs, other_ref)):
-        out_ref[pl.ds(start, 256), :] = ref[base : base + 256, :]
+        for chunk in range(3):
+            lanes = slice(chunk * 128, chunk * 128 + 128)
+            out_ref[pl.ds(chunk * 512 + start, 256), :] = ref[base : base + 256, lanes]
         transfers[pl.ds(start, 128), :] = ref[base + 256 : base + 384, 0:128]
         transfers[pl.ds(start + 128, 128), :] = ref[base + 256 : base + 384, 128:256]
-    charge = mm_tn(transfers[...], out_ref[0:512, features:])
-    out_ref[512:640, features:] = charge.astype(jnp.bfloat16)
-    index = us_ref[pl.ds(chip, 1), :]
-    columns = jnp.transpose(jnp.broadcast_to(index, (8, index.shape[1])))
-    picked = mm(one_hot_rows(columns, 0, 512), out_ref[0:512, 0:features])
-    out_ref[512:640, 0:features] = picked.astype(jnp.bfloat16)
+    charge = mm_tn(transfers[...], out_ref[1024:1536, :])
+    out_ref[1536:1664, :] = charge.astype(jnp.bfloat16)
+    points_ref[...] = upper_points(node_points(out_ref, 0, 512), us_ref[pl.ds(chip, 1), :])
 
 
 def near_kernel(
@@ -261,10 +268,7 @@
     pot_ref[...] = mm(block_ref[...], pack_ref[0:1024, features:])
 
 
-def side_kernel(
-    pack_ref, side_ref, mask_ref, col_ref, start_ref, pot_ref, rows_ref, block_ref, *, total
-):
-    _, core, _, _, _ = place(total)
+def side_work(core, pack_ref, side_ref, mask_ref, col_ref, start_ref, pot_ref, rows_ref, block_ref):
     features = pack_ref.shape[1] - pot_ref.shape[1]
     found = mask_ref[8:16, :]
     for tree in range(4):
@@ -313,10 +317,7 @@
     ret_ref[256:512, :] = mm(parts[0][256:512], pack_ref[512:768, features:]).astype(jnp.bfloat16)
 
 
-def rim_kernel(
-    pack_ref, rim_ref, mask_ref, col_ref, start_ref, pot_ref, rows_ref, block_ref, *, total
-):
-    _, core, _, _, _ = place(total)
+def rim_work(core, pack_ref, rim_ref, mask_ref, col_ref, start_ref, pot_ref, rows_ref, block_ref):
     features = pack_ref.shape[1] - pot_ref.shape[1]
     found = mask_ref[16:24, :]
     for source in range(2):
@@ -332,43 +333,75 @@
             pack_ref[0:stop, 0:features], col_ref[0:stop, :], rim_ref[here, 0:features],
             lambda at: rows_ref[source, pl.ds(tree_leaf(core, at), 1), :],
         )
-    pot_ref[0:768, :] = start_ref[0:768, :] + mm(block_ref[0:768, :], rim_ref[0:512, features:])
+    pot_ref[0:768, :] = start_ref[0:768, :] + mm(block_ref[0:768, 0:512], rim_ref[0:512, features:])
     pot_ref[768:, :] = start_ref[768:, :] + mm(block_ref[768:, 0:256], rim_ref[0:256, features:])
 
 
-def node_part(nodes_ref, ref, mask, core, rows_ref, features):
-    own = nodes_ref[group_rows(core), 0:features]
+def early_kernel(
+    work, pack_ref, other_ref, mask_ref, col_ref, start_ref, pot_ref, rows_ref, block_ref, *, total
+):
+    _, core, _, _, _ = place(total)
+
+    @pl.when(core == 1)
+    def _():
+        work(core, pack_ref, other_ref, mask_ref, col_ref, start_ref, pot_ref, rows_ref, block_ref)
+
+    @pl.when(core == 0)
+    def _():
+        pot_ref[...] = start_ref[...]
+
+
+def late_kernel(
+    pack_ref, side_ref, rim_ref, mask_ref, col_ref, start_ref, pot_ref, rows_ref, block_ref, *, total
+):
+    _, core, _, _, _ = place(total)
+    rest = (mask_ref, col_ref)
+
+    @pl.when(core == 0)
+    def _():
+        side_work(core, pack_ref, side_ref, *rest, start_ref, pot_ref, rows_ref, block_ref)
+        rim_work(core, pack_ref, rim_ref, *rest, pot_ref, pot_ref, rows_ref, block_ref)
+
+    @pl.when(core == 1)
+    def _():
+        pot_ref[...] = start_ref[...]
+
+
+def node_part(own, ref, mask, rows_ref):
     col = norm_col(own)
     parts = []
     for source in range(2):
-        here = slice(source * 256, source * 256 + 256)
+        pts = node_points(ref, source * 256, 256)
         used = [mask[:, 2 * source + h : 2 * source + h + 1] for h in range(2)]
-        fill_rows(rows_ref, source, ref[here, 0:features], used, 2)
-        parts.append(
-            blocks(
-                own, col, ref[here, 0:features], lambda at: rows_ref[source, at : at + 1, :]
-            )
-        )
-    return mm(jnp.concatenate(parts, axis=1), ref[0:512, features:])
-
-
-def upper_part(nodes_ref, ref, used, features):
-    own = nodes_ref[512:640, 0:features]
-    source = ref[512:640, 0:features]
+        fill_rows(rows_ref, source, pts, used, 2)
+        parts.append(blocks(own, col, pts, lambda at: rows_ref[source, at : at + 1, :]))
+    return mm(jnp.concatenate(parts, axis=1), ref[1024:1536, :])
+
+
+def own_nodes(ref, core):
+    start = pl.multiple_of(core * 256, 256)
+    both = [ref[pl.ds(start, 256), :], ref[pl.ds(start + 512, 256), :]]
+    return jnp.concatenate(both, axis=1)
+
+
+def upper_part(own, ref, index, used):
+    source = upper_points(node_points(ref, 0, 512), index)
     row = jnp.where(used > 0.0, norm_row(norm_col(source), 1), NEG)
-    power = mm_nt(own, source) * (2.0 * scale_of(features)) + norm_col(own) + row
-    return mm(jnp.exp2(power).astype(jnp.bfloat16), ref[512:640, features:])
+    power = mm_nt(own, source) * (2.0 * scale_of(own.shape[1])) + norm_col(own) + row
+    return mm(jnp.exp2(power).astype(jnp.bfloat16), ref[1536:1664, :])
 
 
 def outer_node_kernel(
-    nodes_ref, side_b_ref, mask_ref, far1_ref, far2_ref, rows_own, rows_ref, *, total
+    nodes_ref, upper_ref, side_b_ref, us_ref, mask_ref, far1_ref, far2_ref, rows_own, rows_ref,
+    *, total,
 ):
-    _, core, _, _, _ = place(total)
-    features = nodes_ref.shape[1] - far1_ref.shape[1]
-    far2_ref[...] = upper_part(nodes_ref, side_b_ref, mask_ref[24:25, :], features)
-    far1_ref[...] = node_part(
-        nodes_ref, nodes_ref, mask_ref[0:2, :], core, rows_own, features
-    ) + node_part(nodes_ref, side_b_ref, mask_ref[8:10, :], core, rows_ref, features)
+    _, core, _, _, side_b = place(total)
+    index = us_ref[pl.ds(side_b, 1), :]
+    far2_ref[...] = upper_part(upper_ref[...], side_b_ref, index, mask_ref[24:25, :])
+    own = own_nodes(nodes_ref, core)
+    far1_ref[...] = node_part(own, nodes_ref, mask_ref[0:2, :], rows_own) + node_part(
+        own, side_b_ref, mask_ref[8:10, :], rows_ref
+    )
 
 
 def merge_kernel(pot_ref, ret_ref, out_ref, *, total):
@@ -382,15 +415,15 @@
 
 
 def final_kernel(
-    nodes_ref, side_a_ref, mask_ref, far1_ref, far2_ref, t, lt, pot_ref, near_ref, basis,
-    out_hbm, rows_ref, out_ref, sems, *, total,
+    nodes_ref, upper_ref, side_a_ref, us_ref, mask_ref, far1_ref, far2_ref, t, lt, pot_ref,
+    near_ref, basis, out_hbm, rows_ref, out_ref, sems, *, total,
 ):
-    _, core, _, _, _ = place(total)
-    features = nodes_ref.shape[1] - pot_ref.shape[1]
+    _, core, _, side_a, _ = place(total)
     leaves, rows, rank = basis.shape
-    far2 = far2_ref[...] + upper_part(nodes_ref, side_a_ref, mask_ref[25:26, :], features)
+    index = us_ref[pl.ds(side_a, 1), :]
+    far2 = far2_ref[...] + upper_part(upper_ref[...], side_a_ref, index, mask_ref[25:26, :])
     far1 = far1_ref[...] + node_part(
-        nodes_ref, side_a_ref, mask_ref[16:18, :], core, rows_ref, features
+        own_nodes(nodes_ref, core), side_a_ref, mask_ref[16:18, :], rows_ref
     )
     down2 = far2.astype(jnp.bfloat16)
     down1 = (far1 + mm(t[...].reshape(2 * rank, rank), down2)).astype(jnp.bfloat16)
@@ -411,10 +444,11 @@
         for leaf in range(4):
             at = node * 4 + leaf
             out_ref[at * rows : (at + 1) * rows, :] = results[leaf]
-        done = pl.ds(node * 4 * rows, 4 * rows)
-        copy = pltpu.make_async_copy(out_ref.at[done], out_hbm.at[done], sems.at[node])
-        copy.start()
-        copies.append(copy)
+            if leaf % 2 == 1:
+                done = pl.ds((at - 1) * rows, 2 * rows)
+                copy = pltpu.make_async_copy(out_ref.at[done], out_hbm.at[done], sems.at[at // 2])
+                copy.start()
+                copies.append(copy)
     for copy in copies:
         copy.wait()
 
@@ -484,46 +518,52 @@
     )
     rim_in = lax.ppermute(rim, "leaf", outward)
     side = lax.ppermute(pack, "leaf", across)
+    nodes, upper = call(
+        bind(upper_kernel, total=total),
+        [shape((13 * rank, cols), bf16), shape((rank, features), bf16)],
+        [pack, side, us_v], "vvv",
+        [pltpu.VMEM((4 * rank, rank), bf16)],
+        name="upper", us=0.3,
+    )
+    nodes_b = lax.ppermute(nodes, "leaf", outward)
     pot, col = call(
         bind(own_kernel, total=total), [pot_shape, shape((leaves * rank, 128), f32)],
         [pack, mask], "vv", [rows_scratch, pltpu.VMEM((1024, 1024), bf16)],
-        name="own", us=1.7,
-    )
-    (nodes,) = call(
-        bind(upper_kernel, total=total),
-        [shape((5 * rank, width), bf16)],
-        [pack, side, us_v], "vvv",
-        [pltpu.VMEM((4 * rank, rank), bf16)],
-        name="upper", us=0.3, after=[col],
-    )
-    nodes_b = lax.ppermute(nodes, "leaf", outward)
+        name="own", us=1.7, after=[nodes],
+    )
     upper_lists = jnp.transpose(upper_far)
     near, node_mask = call(
         bind(near_kernel, rows=rows, total=total),
         [shape((leaves * rows, cols), f32), shape((32, 128), f32)],
         [points, weights, upper_lists, node_far, node_count, upper_count], "vvhhhh",
         [like(upper_lists), like(node_far), like(node_count, SMEM), like(upper_count, SMEM), sems((4,))],
-        name="near", us=1.7, after=[nodes],
+        name="near", us=1.7, after=[col],
+    )
+    far_scratch = [rows_scratch, pltpu.VMEM((1024, 1024), bf16)]
+    (pot,) = call(
+        bind(early_kernel, side_work, total=total), [pot_shape], [pack, side, mask, col, pot],
+        "vvvvv", far_scratch, name="side", us=1.3, after=[node_mask],
     )
     (ret,) = call(
         bind(back_kernel, total=total), [shape((4 * rank, cols), bf16)], [pack, rim_in, col],
-        "vvv", [rows_scratch], name="back", us=1.3, after=[node_mask],
+        "vvv", [rows_scratch], name="back", us=1.3, after=[pot],
     )
     ret_in = lax.ppermute(ret, "leaf", outward)
     (pot,) = call(
-        bind(side_kernel, total=total), [pot_shape], [pack, side, mask, col, pot], "vvvvv",
-        [rows_scratch, pltpu.VMEM((1024, 1024), bf16)], name="side", us=0.1, after=[ret],
-    )
-    (pot,) = call(
-        bind(rim_kernel, total=total), [pot_shape], [pack, rim_in, mask, col, pot], "vvvvv",
-        [rows_scratch, pltpu.VMEM((1024, 512), bf16)], name="rim", us=0.1, early=[leaf_basis, leaf_transfer, node_transfer],
+        bind(early_kernel, rim_work, total=total), [pot_shape], [pack, rim_in, mask, col, pot],
+        "vvvvv", far_scratch, name="rim", us=0.1, after=[ret],
+        early=[leaf_basis, leaf_transfer, node_transfer],
     )
     nodes_b, pot = lax.optimization_barrier((nodes_b, pot))
     nodes_a = lax.ppermute(nodes_b, "leaf", across)
+    (pot,) = call(
+        bind(late_kernel, total=total), [pot_shape], [pack, side, rim_in, mask, col, pot],
+        "vvvvvv", far_scratch, name="late", us=0.1,
+    )
     far1, far2 = call(
         bind(outer_node_kernel, total=total),
         [shape((2 * rank, cols), f32), shape((rank, cols), f32)],
-        [nodes, nodes_b, node_mask], "vvv", [node_rows, node_rows],
+        [nodes, upper, nodes_b, us_v, node_mask], "vvvvv", [node_rows, node_rows],
         name="outer_node", us=0.1, after=[pot],
     )
     (pot,) = call(
@@ -533,10 +573,10 @@
     (out,) = call(
         bind(final_kernel, total=total),
         [shape((leaves * rows, cols), bf16)],
-        [nodes, nodes_a, node_mask, far1, far2, node_transfer, leaf_transfer, pot, near,
-         leaf_basis],
-        "vvvvvvvvvv",
-        [node_rows, pltpu.VMEM((leaves * rows, cols), bf16), sems((2,))],
+        [nodes, upper, nodes_a, us_v, node_mask, far1, far2, node_transfer, leaf_transfer, pot,
+         near, leaf_basis],
+        "vvvvvvvvvvvv",
+        [node_rows, pltpu.VMEM((leaves * rows, cols), bf16), sems((4,))],
         name="final", us=1.9, out_space=HBM,
     )
     return out

time: 29.6 us -> 28 us (0.946)
  the two profiles are of different devices: /device:TPU:1 before, /device:TPU:16 now
where the time goes in v5:
time: 28 us; the launch traced here: 27.9 us
  starting transfers between devices  15 us (54%)
  Pallas kernels  12.3 us (44%)
  waiting for transfers between devices  0.4 us (1%)
    pallas_call x11, Pallas kernels, call(): pl.pallas_call(body, out_shape=outs, in_specs=[pl.BlockSpec(memory_space=...  12.3 us
    ppermute x1, starting transfers between devices, per_device(): rim_in = lax.ppermute(rim, 'leaf', outward)  8.15 us
    ppermute x1, starting transfers between devices, per_device(): ret_in = lax.ppermute(ret, 'leaf', outward)  4.28 us
    ppermute x1, starting transfers between devices, per_device(): nodes_b = lax.ppermute(nodes, 'leaf', outward)  2.41 us
  transfers between devices with their start and end apart: 5, of which 1 were waited for; matrix products, arithmetic and copies ran while one was open for 0% of the time, Pallas kernels for 27%

profile of v5, /device:TPU:16, one launch (start us, length us, event | category | flops | bytes accessed | tf_op | source)
XLA Modules:
  0.0 27.9 jit_solution(9572153956481752768)
XLA Ops:
  0.0 2.6 %front.1 = (bf16[1408,384]{1,0:T(8,128)(2,1)S(1)}, bf16[528,384]{1,0:T(8,128)(2,1)S(1)}, f32[24,128]{1,0:T(8,128)S(1)}, s32[32,128]{1,0:T(8,128)S(1)}) custom-call(bf16[2048,256]{1,0:T(8,128)(2,1)} %refs_0_.3, bf16[2048,128]{1,0:T(8,128)(2,1)} %refs_1_.3, bf16[8,256,128]{2,1,0:T(8,128)(2,1)} %refs_11_.1, bf16[8,128,128]{2,1,0:T(8,128)(2,1)} %refs_8_.5, ...), custom_call_target="tpu_custom_call" | custom-call | flops 2875000064 | tf_op jit(solution)/shard_map/front/pallas_call | solution.py:468
  2.7 0.1 collective-permute-start
  2.8 8.2 %collective-permute-start.2 = (bf16[528,384]{1,0:T(8,128)(2,1)S(1)}, bf16[528,384]{1,0:T(8,128)(2,1)S(1)}, u32[]{:S(2)}, u32[]{:S(2)}) collective-permute-start(bf16[528,384]{1,0:T(8,128)(2,1)S(1)} %get-tuple-element.23), channel_id=1, source_target_pairs={{0,252},{4,8},{8,4},{12,16},{16,12},{20,24},{24,20},{28,32},{32,28... | collective-permute-start | bytes 1216520 | tf_op jit(solution)/shard_map/ppermute | solution.py:519
  10.9 0.0 collective-permute-done.refs_1_
  10.9 0.4 %upper.1 = (bf16[1664,128]{1,0:T(8,128)(2,1)S(1)}, bf16[128,256]{1,0:T(8,128)(2,1)S(1)}) custom-call(bf16[1408,384]{1,0:T(8,128)(2,1)S(1)} %get-tuple-element.19.refs_0_, bf16[1408,384]{1,0:T(8,128)(2,1)S(1)} %collective-permute-done.refs_1_, s32[32,128]{1,0:T(8,128)S(1)} %get-tuple-element.20.refs_2_.refs_3_), custom_call_target="tpu_custom_call" | custom-call | flops 345000000 | tf_op jit(solution)/shard_map/upper/pallas_call | solution.py:468
  11.3 2.4 %collective-permute-start.1 = (bf16[1664,128]{1,0:T(8,128)(2,1)S(1)}, bf16[1664,128]{1,0:T(8,128)(2,1)S(1)}, u32[]{:S(2)}, u32[]{:S(2)}) collective-permute-start(bf16[1664,128]{1,0:T(8,128)(2,1)S(1)} %get-tuple-element.21.refs_2_.refs_0_), channel_id=1, source_target_pairs={{0,252},{4,8},{8,4},{12,16},{16,12},{20,24},{24,20},{28,32},{32,28... | collective-permute-start | bytes 1277960 | tf_op jit(solution)/shard_map/ppermute | solution.py:528
  13.7 0.0 copy-start.3
  13.7 0.0 copy-start.4
  13.7 1.8 %own.1 = (f32[1024,128]{1,0:T(8,128)S(1)}, f32[1024,128]{1,0:T(8,128)S(1)}) custom-call(bf16[1408,384]{1,0:T(8,128)(2,1)S(1)} %get-tuple-element.19.refs_0_, f32[24,128]{1,0:T(8,128)S(1)} %get-tuple-element.24.refs_1_.refs_2_.refs_3_, bf16[1664,128]{1,0:T(8,128)(2,1)S(1)} %get-tuple-element.21.refs_2_.refs_0_), custom_call_target="tpu_custom_call" | custom-call | flops 1955000064 | tf_op jit(solution)/shard_map/own/pallas_call | solution.py:468
  15.5 0.0 copy-done.3
  15.5 0.0 copy-done.4
  15.5 1.7 %near.1 = (f32[2048,128]{1,0:T(8,128)S(1)}, f32[32,128]{1,0:T(8,128)S(1)}) custom-call(bf16[2048,256]{1,0:T(8,128)(2,1)S(1)} %copy-done.3, bf16[2048,128]{1,0:T(8,128)(2,1)S(1)} %copy-done.4, s32[12,32]{1,0:T(8,128)} %bitcast.1, s32[2,12]{1,0:T(2,128)} %refs_3_.3, s32[2]{0:T(128)} %refs_4_.3, s32[32]{0:T(128)} %refs_5_.3, ...), custom_call_target="tpu_custom_call" | custom-call | flops 1955000064 | tf_op jit(solution)/shard_map/near/pallas_call | solution.py:468
  17.3 0.1 side.1.refs_3_.refs_4_
  17.3 0.0 copy-start
  17.3 0.0 copy-start.1
  17.3 0.0 copy-start.2
  17.4 0.0 collective-permute-done.2.refs_1_.refs_2_
  17.4 0.6 %back.1.refs_5_ = bf16[512,128]{1,0:T(8,128)(2,1)S(1)} custom-call(bf16[1408,384]{1,0:T(8,128)(2,1)S(1)} %get-tuple-element.19.refs_0_, bf16[528,384]{1,0:T(8,128)(2,1)S(1)} %collective-permute-done.2.refs_1_.refs_2_, f32[1024,128]{1,0:T(8,128)S(1)} %get-tuple-element.25.refs_6_.refs_3_.refs_2_.refs_4_, f32[1024,128]{1,0:T(8,128)S(1)} %side.1.refs_3_.refs_4_), custom_call_target="tpu_custom_call" | custom-call | flops 1495000064 | tf_op jit(solution)/shard_map/back/pallas_call | solution.py:468
  18.0 4.3 %collective-permute-start.4 = (bf16[512,128]{1,0:T(8,128)(2,1)S(1)}, bf16[512,128]{1,0:T(8,128)(2,1)S(1)}, u32[]{:S(2)}, u32[]{:S(2)}) collective-permute-start(bf16[512,128]{1,0:T(8,128)(2,1)S(1)} %back.1.refs_5_), channel_id=1, source_target_pairs={{0,252},{4,8},{8,4},{12,16},{16,12},{20,24},{24,20},{28,32},{32,28... | collective-permute-start | bytes 393224 | tf_op jit(solution)/shard_map/ppermute | solution.py:551
  22.3 0.0 copy-done
  22.3 0.0 copy-done.1
  22.3 0.0 copy-done.2
  22.3 0.1 rim.1.refs_5_
  22.3 0.0 collective-permute-done.1.refs_2_
  22.3 0.1 collective-permute-start.3
  22.4 1.9 %late.1.refs_5_.refs_0_ = f32[1024,128]{1,0:T(8,128)S(1)} custom-call(bf16[1408,384]{1,0:T(8,128)(2,1)S(1)} %get-tuple-element.19.refs_0_, bf16[1408,384]{1,0:T(8,128)(2,1)S(1)} %collective-permute-done.refs_1_, bf16[528,384]{1,0:T(8,128)(2,1)S(1)} %collective-permute-done.2.refs_1_.refs_2_, f32[24,128]{1,0:T(8,128)S(1)} %get-tuple-element.24.refs_1_.refs_2_.refs_3_, ...), custom_call_target="tpu_custom_call" | custom-call | flops 115000000 | tf_op jit(solution)/shard_map/late/pallas_call | solution.py:468
  24.3 1.1 %outer_node.1 = (f32[256,128]{1,0:T(8,128)S(1)}, f32[128,128]{1,0:T(8,128)S(1)}) custom-call(bf16[1664,128]{1,0:T(8,128)(2,1)S(1)} %get-tuple-element.21.refs_2_.refs_0_, bf16[128,256]{1,0:T(8,128)(2,1)S(1)} %get-tuple-element.22.refs_1_, bf16[1664,128]{1,0:T(8,128)(2,1)S(1)} %collective-permute-done.1.refs_2_, ...), custom_call_target="tpu_custom_call" | custom-call | flops 115000000 | tf_op jit(solution)/shard_map/outer_node/pallas_call | solution.py:468
  25.4 0.4 %collective-permute-done.4.refs_1_ = bf16[512,128]{1,0:T(8,128)(2,1)S(1)} collective-permute-done((bf16[512,128]{1,0:T(8,128)(2,1)S(1)}, bf16[512,128]{1,0:T(8,128)(2,1)S(1)}, u32[]{:S(2)}, u32[]{:S(2)}) %collective-permute-start.4) | collective-permute-done | bytes 131104 | tf_op jit(solution)/shard_map/ppermute | solution.py:551
  25.8 0.1 merge.1.refs_9_
  25.9 0.0 collective-permute-done.3.refs_2_
  25.9 2.0 %final.1 = bf16[2048,128]{1,0:T(8,128)(2,1)} custom-call(bf16[1664,128]{1,0:T(8,128)(2,1)S(1)} %get-tuple-element.21.refs_2_.refs_0_, bf16[128,256]{1,0:T(8,128)(2,1)S(1)} %get-tuple-element.22.refs_1_, bf16[1664,128]{1,0:T(8,128)(2,1)S(1)} %collective-permute-done.3.refs_2_, s32[32,128]{1,0:T(8,128)S(1)} %get-tuple-element.20.refs_2_.refs_3_, ...), custom_call_target="tpu_custom_call" | custom-call | flops 2184999936 | tf_op jit(solution)/shard_map/final/pallas_call | solution.py:468
Async XLA Ops:
  2.7 8.3 %collective-permute-start = (bf16[1408,384]{1,0:T(8,128)(2,1)S(1)}, bf16[1408,384]{1,0:T(8,128)(2,1)S(1)}, u32[]{:S(2)}, u32[]{:S(2)}) collective-permute-start(bf16[1408,384]{1,0:T(8,128)(2,1)S(1)} %get-tuple-element.19.refs_0_), channel_id=1, source_target_pairs={{0,4},{4,0},{8,12},{12,8},{16,20},{20,16},{24,28},{28,24},{32,36},... | collective-permute-start | bytes 3244040 | tf_op jit(solution)/shard_map/ppermute | solution.py:520
  2.8 14.6 %collective-permute-start.2 = (bf16[528,384]{1,0:T(8,128)(2,1)S(1)}, bf16[528,384]{1,0:T(8,128)(2,1)S(1)}, u32[]{:S(2)}, u32[]{:S(2)}) collective-permute-start(bf16[528,384]{1,0:T(8,128)(2,1)S(1)} %get-tuple-element.23), channel_id=1, source_target_pairs={{0,252},{4,8},{8,4},{12,16},{16,12},{20,24},{24,20},{28,32},{32,28... | collective-permute-start | bytes 1216520 | tf_op jit(solution)/shard_map/ppermute | solution.py:519
  11.3 11.1 %collective-permute-start.1 = (bf16[1664,128]{1,0:T(8,128)(2,1)S(1)}, bf16[1664,128]{1,0:T(8,128)(2,1)S(1)}, u32[]{:S(2)}, u32[]{:S(2)}) collective-permute-start(bf16[1664,128]{1,0:T(8,128)(2,1)S(1)} %get-tuple-element.21.refs_2_.refs_0_), channel_id=1, source_target_pairs={{0,252},{4,8},{8,4},{12,16},{16,12},{20,24},{24,20},{28,32},{32,28... | collective-permute-start | bytes 1277960 | tf_op jit(solution)/shard_map/ppermute | solution.py:528
  13.7 1.8 %copy-start.3 = (bf16[2048,256]{1,0:T(8,128)(2,1)S(1)}, bf16[2048,256]{1,0:T(8,128)(2,1)}, u32[]{:S(2)}) copy-start(bf16[2048,256]{1,0:T(8,128)(2,1)} %refs_0_.3) | copy-start | bytes 3145732
  13.7 1.8 %copy-start.4 = (bf16[2048,128]{1,0:T(8,128)(2,1)S(1)}, bf16[2048,128]{1,0:T(8,128)(2,1)}, u32[]{:S(2)}) copy-start(bf16[2048,128]{1,0:T(8,128)(2,1)} %refs_1_.3) | copy-start | bytes 1572868
  17.3 4.9 %copy-start = (bf16[8,256,128]{2,1,0:T(8,128)(2,1)S(1)}, bf16[8,256,128]{2,1,0:T(8,128)(2,1)}, u32[]{:S(2)}) copy-start(bf16[8,256,128]{2,1,0:T(8,128)(2,1)} %refs_11_.1) | copy-start | bytes 1572868
  17.3 4.9 %copy-start.1 = (bf16[8,128,128]{2,1,0:T(8,128)(2,1)S(1)}, bf16[8,128,128]{2,1,0:T(8,128)(2,1)}, u32[]{:S(2)}) copy-start(bf16[8,128,128]{2,1,0:T(8,128)(2,1)} %refs_8_.5) | copy-start | bytes 786436
  17.3 4.9 %copy-start.2 = (bf16[2,128,128]{2,1,0:T(8,128)(2,1)S(1)}, bf16[2,128,128]{2,1,0:T(8,128)(2,1)}, u32[]{:S(2)}) copy-start(bf16[2,128,128]{2,1,0:T(8,128)(2,1)} %refs_7_.5) | copy-start | bytes 196612
  18.0 7.8 %collective-permute-start.4 = (bf16[512,128]{1,0:T(8,128)(2,1)S(1)}, bf16[512,128]{1,0:T(8,128)(2,1)S(1)}, u32[]{:S(2)}, u32[]{:S(2)}) collective-permute-start(bf16[512,128]{1,0:T(8,128)(2,1)S(1)} %back.1.refs_5_), channel_id=1, source_target_pairs={{0,252},{4,8},{8,4},{12,16},{16,12},{20,24},{24,20},{28,32},{32,28... | collective-permute-start | bytes 393224 | tf_op jit(solution)/shard_map/ppermute | solution.py:551
  22.3 3.5 %collective-permute-start.3 = (bf16[1664,128]{1,0:T(8,128)(2,1)S(1)}, bf16[1664,128]{1,0:T(8,128)(2,1)S(1)}, u32[]{:S(2)}, u32[]{:S(2)}) collective-permute-start(bf16[1664,128]{1,0:T(8,128)(2,1)S(1)} %collective-permute-done.1.refs_2_), channel_id=1, source_target_pairs={{0,4},{4,0},{8,12},{12,8},{16,20},{20,16},{24,28},{28,24},{32,36},... | collective-permute-start | bytes 1277960 | tf_op jit(solution)/shard_map/ppermute | solution.py:558

commit v6 on v5

--- a/solution.py
+++ b/solution.py
@@ -130,7 +130,7 @@
     features = points.shape[1]
     cols = weights.shape[1]
     small = [(ls_hbm, ls), (ns_hbm, ns), (far_hbm, far), (count_hbm, count), (us_hbm, us)]
-    pairs = small + [(lt_hbm, lt), (t_hbm, t)]
+    pairs = list(small)
     ahead = len(pairs)
     part = leaves // 2
     for half in range(2):
@@ -141,6 +141,7 @@
             (weights_hbm.at[own], weights.at[own]),
             (basis_hbm.at[some], basis.at[some]),
         ]
+    pairs += [(lt_hbm, lt), (t_hbm, t)]
     copies = fetch(pairs, sems)
     for copy in copies[: len(small)]:
         copy.wait()
@@ -171,7 +172,7 @@
         pack_ref[here, features:] = charge
         picked.append(skel)
         charges.append(charge)
-    for copy in copies[len(small) : ahead]:
+    for copy in copies[ahead + 6 :]:
         copy.wait()
     for node in range(nodes):
         own = slice(base + node * rank, base + (node + 1) * rank)
@@ -187,9 +188,9 @@
     rim_ref[0:512, :] = pack_ref[0:512, :]
 
 
-def upper_points(points, index):
+def upper_hot(index):
     columns = jnp.transpose(jnp.broadcast_to(index, (8, index.shape[1])))
-    return mm(one_hot_rows(columns, 0, 512), points).astype(jnp.bfloat16)
+    return one_hot_rows(columns, 0, 512)
 
 
 def node_points(ref, start, count):
@@ -210,7 +211,8 @@
         transfers[pl.ds(start + 128, 128), :] = ref[base + 256 : base + 384, 128:256]
     charge = mm_tn(transfers[...], out_ref[1024:1536, :])
     out_ref[1536:1664, :] = charge.astype(jnp.bfloat16)
-    points_ref[...] = upper_points(node_points(out_ref, 0, 512), us_ref[pl.ds(chip, 1), :])
+    hot = upper_hot(us_ref[pl.ds(chip, 1), :])
+    points_ref[...] = mm(hot, node_points(out_ref, 0, 512)).astype(jnp.bfloat16)
 
 
 def near_kernel(
@@ -367,14 +369,18 @@
         pot_ref[...] = start_ref[...]
 
 
-def node_part(own, ref, mask, rows_ref):
-    col = norm_col(own)
+def node_part(own, col, ref, mask):
     parts = []
     for source in range(2):
         pts = node_points(ref, source * 256, 256)
-        used = [mask[:, 2 * source + h : 2 * source + h + 1] for h in range(2)]
-        fill_rows(rows_ref, source, pts, used, 2)
-        parts.append(blocks(own, col, pts, lambda at: rows_ref[source, at : at + 1, :]))
+        norms = norm_col(pts)
+        rows = []
+        for half in range(2):
+            j = 2 * source + half
+            term = norm_row(norms[half * 128 : half * 128 + 128], 2)
+            rows.append(jnp.where(mask[:, j : j + 1] > 0.0, term, NEG))
+        row = jnp.concatenate(rows, axis=1)
+        parts.append(blocks(own, col, pts, lambda at: row[at : at + 1]))
     return mm(jnp.concatenate(parts, axis=1), ref[1024:1536, :])
 
 
@@ -384,23 +390,29 @@
     return jnp.concatenate(both, axis=1)
 
 
-def upper_part(own, ref, index, used):
-    source = upper_points(node_points(ref, 0, 512), index)
+def upper_part(own, col, ref, hot, used):
+    source = mm(hot, node_points(ref, 0, 512)).astype(jnp.bfloat16)
     row = jnp.where(used > 0.0, norm_row(norm_col(source), 1), NEG)
-    power = mm_nt(own, source) * (2.0 * scale_of(own.shape[1])) + norm_col(own) + row
+    power = mm_nt(own, source) * (2.0 * scale_of(own.shape[1])) + col + row
     return mm(jnp.exp2(power).astype(jnp.bfloat16), ref[1536:1664, :])
 
 
 def outer_node_kernel(
-    nodes_ref, upper_ref, side_b_ref, us_ref, mask_ref, far1_ref, far2_ref, rows_own, rows_ref,
-    *, total,
+    nodes_ref, upper_ref, side_b_ref, us_ref, mask_ref, far1_ref, far2_ref, own_ref, col_ref,
+    hot_ref, *, total,
 ):
-    _, core, _, _, side_b = place(total)
-    index = us_ref[pl.ds(side_b, 1), :]
-    far2_ref[...] = upper_part(upper_ref[...], side_b_ref, index, mask_ref[24:25, :])
+    _, core, _, side_a, side_b = place(total)
     own = own_nodes(nodes_ref, core)
-    far1_ref[...] = node_part(own, nodes_ref, mask_ref[0:2, :], rows_own) + node_part(
-        own, side_b_ref, mask_ref[8:10, :], rows_ref
+    col = norm_col(own)
+    upper_col = norm_col(upper_ref[...])
+    own_ref[...] = own
+    col_ref[0:256, :] = col
+    col_ref[256:384, :] = upper_col
+    hot_ref[...] = upper_hot(us_ref[pl.ds(side_a, 1), :])
+    hot = upper_hot(us_ref[pl.ds(side_b, 1), :])
+    far2_ref[...] = upper_part(upper_ref[...], upper_col, side_b_ref, hot, mask_ref[24:25, :])
+    far1_ref[...] = node_part(own, col, nodes_ref, mask_ref[0:2, :]) + node_part(
+        own, col, side_b_ref, mask_ref[8:10, :]
     )
 
 
@@ -415,15 +427,15 @@
 
 
 def final_kernel(
-    nodes_ref, upper_ref, side_a_ref, us_ref, mask_ref, far1_ref, far2_ref, t, lt, pot_ref,
-    near_ref, basis, out_hbm, rows_ref, out_ref, sems, *, total,
+    own_ref, upper_ref, col_ref, hot_ref, side_a_ref, mask_ref, far1_ref, far2_ref, t, lt, pot_ref,
+    near_ref, basis, out_hbm, out_ref, sems,
 ):
-    _, core, _, side_a, _ = place(total)
     leaves, rows, rank = basis.shape
-    index = us_ref[pl.ds(side_a, 1), :]
-    far2 = far2_ref[...] + upper_part(upper_ref[...], side_a_ref, index, mask_ref[25:26, :])
+    far2 = far2_ref[...] + upper_part(
+        upper_ref[...], col_ref[256:384, :], side_a_ref, hot_ref[...], mask_ref[25:26, :]
+    )
     far1 = far1_ref[...] + node_part(
-        own_nodes(nodes_ref, core), side_a_ref, mask_ref[16:18, :], rows_ref
+        own_ref[...], col_ref[0:256, :], side_a_ref, mask_ref[16:18, :]
     )
     down2 = far2.astype(jnp.bfloat16)
     down1 = (far1 + mm(t[...].reshape(2 * rank, rank), down2)).astype(jnp.bfloat16)
@@ -497,7 +509,6 @@
     sems = pltpu.SemaphoreType.DMA
     bind = functools.partial
     rows_scratch = pltpu.VMEM((leaves // 2, leaves, 256), f32)
-    node_rows = pltpu.VMEM((2, 2, 256), f32)
     pot_shape = shape((leaves * rank, cols), f32)
 
     pack, rim, mask, us_v = call(
@@ -560,10 +571,14 @@
         bind(late_kernel, total=total), [pot_shape], [pack, side, rim_in, mask, col, pot],
         "vvvvvv", far_scratch, name="late", us=0.1,
     )
-    far1, far2 = call(
+    far1, far2, own_points, node_col, hot = call(
         bind(outer_node_kernel, total=total),
-        [shape((2 * rank, cols), f32), shape((rank, cols), f32)],
-        [nodes, upper, nodes_b, us_v, node_mask], "vvvvv", [node_rows, node_rows],
+        [
+            shape((2 * rank, cols), f32), shape((rank, cols), f32),
+            shape((2 * rank, features), bf16), shape((3 * rank, 128), f32),
+            shape((rank, 4 * rank), bf16),
+        ],
+        [nodes, upper, nodes_b, us_v, node_mask], "vvvvv",
         name="outer_node", us=0.1, after=[pot],
     )
     (pot,) = call(
@@ -571,12 +586,12 @@
         after=[far2],
     )
     (out,) = call(
-        bind(final_kernel, total=total),
+        final_kernel,
         [shape((leaves * rows, cols), bf16)],
-        [nodes, upper, nodes_a, us_v, node_mask, far1, far2, node_transfer, leaf_transfer, pot,
-         near, leaf_basis],
-        "vvvvvvvvvvvv",
-        [node_rows, pltpu.VMEM((leaves * rows, cols), bf16), sems((4,))],
+        [own_points, upper, node_col, hot, nodes_a, node_mask, far1, far2, node_transfer,
+         leaf_transfer, pot, near, leaf_basis],
+        "vvvvvvvvvvvvv",
+        [pltpu.VMEM((leaves * rows, cols), bf16), sems((4,))],
         name="final", us=1.9, out_space=HBM,
     )
     return out

time: 28 us -> 27.8 us (level)
  transfers between devices with their start and end apart: 5 -> 5, of which waited for: 1 -> 1; matrix products, arithmetic and copies ran while one was open for 0% -> 0% of each run, Pallas kernels for 27% -> 28%
where the time goes in v6:
time: 27.8 us; the launch traced here: 27.7 us
  starting transfers between devices  15 us (54%)
  Pallas kernels  12.1 us (44%)
  waiting for transfers between devices  0.32 us (1%)
    pallas_call x11, Pallas kernels, call(): pl.pallas_call(body, out_shape=outs, in_specs=[pl.BlockSpec(memory_space=...  12.1 us
    ppermute x1, starting transfers between devices, per_device(): rim_in = lax.ppermute(rim, 'leaf', outward)  8.15 us
    ppermute x1, starting transfers between devices, per_device(): ret_in = lax.ppermute(ret, 'leaf', outward)  4.28 us
    ppermute x1, starting transfers between devices, per_device(): nodes_b = lax.ppermute(nodes, 'leaf', outward)  2.41 us
  transfers between devices with their start and end apart: 5, of which 1 were waited for; matrix products, arithmetic and copies ran while one was open for 0% of the time, Pallas kernels for 28%

profile of v6, /device:TPU:16, one launch (start us, length us, event | category | flops | bytes accessed | tf_op | source)
XLA Modules:
  0.0 27.7 jit_solution(18259481243163925142)
XLA Ops:
  0.0 2.5 %front.1 = (bf16[1408,384]{1,0:T(8,128)(2,1)S(1)}, bf16[528,384]{1,0:T(8,128)(2,1)S(1)}, f32[24,128]{1,0:T(8,128)S(1)}, s32[32,128]{1,0:T(8,128)S(1)}) custom-call(bf16[2048,256]{1,0:T(8,128)(2,1)} %refs_0_.3, bf16[2048,128]{1,0:T(8,128)(2,1)} %refs_1_.3, bf16[8,256,128]{2,1,0:T(8,128)(2,1)} %refs_12_.1, bf16[8,128,128]{2,1,0:T(8,128)(2,1)} %refs_9_.3, ...), custom_call_target="tpu_custom_call" | custom-call | flops 2875000064 | tf_op jit(solution)/shard_map/front/pallas_call | solution.py:480
  2.5 0.1 collective-permute-start
  2.6 8.2 %collective-permute-start.2 = (bf16[528,384]{1,0:T(8,128)(2,1)S(1)}, bf16[528,384]{1,0:T(8,128)(2,1)S(1)}, u32[]{:S(2)}, u32[]{:S(2)}) collective-permute-start(bf16[528,384]{1,0:T(8,128)(2,1)S(1)} %get-tuple-element.26), channel_id=1, source_target_pairs={{0,252},{4,8},{8,4},{12,16},{16,12},{20,24},{24,20},{28,32},{32,28... | collective-permute-start | bytes 1216520 | tf_op jit(solution)/shard_map/ppermute | solution.py:530
  10.8 0.0 collective-permute-done.refs_1_
  10.8 0.4 %upper.1 = (bf16[1664,128]{1,0:T(8,128)(2,1)S(1)}, bf16[128,256]{1,0:T(8,128)(2,1)S(1)}) custom-call(bf16[1408,384]{1,0:T(8,128)(2,1)S(1)} %get-tuple-element.22.refs_0_, bf16[1408,384]{1,0:T(8,128)(2,1)S(1)} %collective-permute-done.refs_1_, s32[32,128]{1,0:T(8,128)S(1)} %get-tuple-element.23.refs_2_.refs_3_), custom_call_target="tpu_custom_call" | custom-call | flops 345000000 | tf_op jit(solution)/shard_map/upper/pallas_call | solution.py:480
  11.2 2.4 %collective-permute-start.1 = (bf16[1664,128]{1,0:T(8,128)(2,1)S(1)}, bf16[1664,128]{1,0:T(8,128)(2,1)S(1)}, u32[]{:S(2)}, u32[]{:S(2)}) collective-permute-start(bf16[1664,128]{1,0:T(8,128)(2,1)S(1)} %get-tuple-element.24.refs_2_.refs_0_), channel_id=1, source_target_pairs={{0,252},{4,8},{8,4},{12,16},{16,12},{20,24},{24,20},{28,32},{32,28... | collective-permute-start | bytes 1277960 | tf_op jit(solution)/shard_map/ppermute | solution.py:539
  13.6 0.0 copy-start.3
  13.6 0.0 copy-start.4
  13.6 1.8 %own.1 = (f32[1024,128]{1,0:T(8,128)S(1)}, f32[1024,128]{1,0:T(8,128)S(1)}) custom-call(bf16[1408,384]{1,0:T(8,128)(2,1)S(1)} %get-tuple-element.22.refs_0_, f32[24,128]{1,0:T(8,128)S(1)} %get-tuple-element.27.refs_1_.refs_2_.refs_3_, bf16[1664,128]{1,0:T(8,128)(2,1)S(1)} %get-tuple-element.24.refs_2_.refs_0_), custom_call_target="tpu_custom_call" | custom-call | flops 1955000064 | tf_op jit(solution)/shard_map/own/pallas_call | solution.py:480
  15.4 0.0 copy-done.3
  15.4 0.0 copy-done.4
  15.4 1.7 %near.1 = (f32[2048,128]{1,0:T(8,128)S(1)}, f32[32,128]{1,0:T(8,128)S(1)}) custom-call(bf16[2048,256]{1,0:T(8,128)(2,1)S(1)} %copy-done.3, bf16[2048,128]{1,0:T(8,128)(2,1)S(1)} %copy-done.4, s32[12,32]{1,0:T(8,128)} %bitcast.1, s32[2,12]{1,0:T(2,128)} %refs_3_.3, s32[2]{0:T(128)} %refs_4_.3, s32[32]{0:T(128)} %refs_5_.3, ...), custom_call_target="tpu_custom_call" | custom-call | flops 1955000064 | tf_op jit(solution)/shard_map/near/pallas_call | solution.py:480
  17.1 0.1 side.1.refs_3_.refs_4_
  17.2 0.0 copy-start
  17.2 0.0 copy-start.1
  17.2 0.0 copy-start.2
  17.2 0.0 collective-permute-done.2.refs_1_.refs_2_
  17.3 0.6 %back.1.refs_5_ = bf16[512,128]{1,0:T(8,128)(2,1)S(1)} custom-call(bf16[1408,384]{1,0:T(8,128)(2,1)S(1)} %get-tuple-element.22.refs_0_, bf16[528,384]{1,0:T(8,128)(2,1)S(1)} %collective-permute-done.2.refs_1_.refs_2_, f32[1024,128]{1,0:T(8,128)S(1)} %get-tuple-element.28.refs_6_.refs_3_.refs_2_.refs_4_, f32[1024,128]{1,0:T(8,128)S(1)} %side.1.refs_3_.refs_4_), custom_call_target="tpu_custom_call" | custom-call | flops 1495000064 | tf_op jit(solution)/shard_map/back/pallas_call | solution.py:480
  17.9 4.3 %collective-permute-start.4 = (bf16[512,128]{1,0:T(8,128)(2,1)S(1)}, bf16[512,128]{1,0:T(8,128)(2,1)S(1)}, u32[]{:S(2)}, u32[]{:S(2)}) collective-permute-start(bf16[512,128]{1,0:T(8,128)(2,1)S(1)} %back.1.refs_5_), channel_id=1, source_target_pairs={{0,252},{4,8},{8,4},{12,16},{16,12},{20,24},{24,20},{28,32},{32,28... | collective-permute-start | bytes 393224 | tf_op jit(solution)/shard_map/ppermute | solution.py:562
  22.2 0.0 copy-done
  22.2 0.0 copy-done.1
  22.2 0.0 copy-done.2
  22.2 0.1 rim.1.refs_5_
  22.2 0.0 collective-permute-done.1.refs_2_
  22.2 0.1 collective-permute-start.3
  22.3 1.9 %late.1.refs_5_.refs_0_ = f32[1024,128]{1,0:T(8,128)S(1)} custom-call(bf16[1408,384]{1,0:T(8,128)(2,1)S(1)} %get-tuple-element.22.refs_0_, bf16[1408,384]{1,0:T(8,128)(2,1)S(1)} %collective-permute-done.refs_1_, bf16[528,384]{1,0:T(8,128)(2,1)S(1)} %collective-permute-done.2.refs_1_.refs_2_, f32[24,128]{1,0:T(8,128)S(1)} %get-tuple-element.27.refs_1_.refs_2_.refs_3_, ...), custom_call_target="tpu_custom_call" | custom-call | flops 115000000 | tf_op jit(solution)/shard_map/late/pallas_call | solution.py:480
  24.2 1.2 %outer_node.1 = (f32[256,128]{1,0:T(8,128)S(1)}, f32[128,128]{1,0:T(8,128)S(1)}, bf16[256,256]{1,0:T(8,128)(2,1)S(1)}, f32[384,128]{1,0:T(8,128)S(1)}, bf16[128,512]{1,0:T(8,128)(2,1)S(1)}) custom-call(bf16[1664,128]{1,0:T(8,128)(2,1)S(1)} %get-tuple-element.24.refs_2_.refs_0_, bf16[128,256]{1,0:T(8,128)(2,1)S(1)} %get-tuple-element.25.refs_1_, ...), custom_call_target="tpu_custom_call" | custom-call | flops 115000000 | tf_op jit(solution)/shard_map/outer_node/pallas_call | solution.py:480
  25.4 0.3 %collective-permute-done.4.refs_1_ = bf16[512,128]{1,0:T(8,128)(2,1)S(1)} collective-permute-done((bf16[512,128]{1,0:T(8,128)(2,1)S(1)}, bf16[512,128]{1,0:T(8,128)(2,1)S(1)}, u32[]{:S(2)}, u32[]{:S(2)}) %collective-permute-start.4) | collective-permute-done | bytes 131104 | tf_op jit(solution)/shard_map/ppermute | solution.py:562
  25.7 0.1 merge.1.refs_10_
  25.7 0.0 collective-permute-done.3.refs_4_
  25.8 1.9 %final.1 = bf16[2048,128]{1,0:T(8,128)(2,1)} custom-call(bf16[256,256]{1,0:T(8,128)(2,1)S(1)} %get-tuple-element.33.refs_0_, bf16[128,256]{1,0:T(8,128)(2,1)S(1)} %get-tuple-element.25.refs_1_, f32[384,128]{1,0:T(8,128)S(1)} %get-tuple-element.34.refs_2_, bf16[128,512]{1,0:T(8,128)(2,1)S(1)} %get-tuple-element.35.refs_3_, ...), custom_call_target="tpu_custom_call" | custom-call | flops 2184999936 | tf_op jit(solution)/shard_map/final/pallas_call | solution.py:480
Async XLA Ops:
  2.5 8.3 %collective-permute-start = (bf16[1408,384]{1,0:T(8,128)(2,1)S(1)}, bf16[1408,384]{1,0:T(8,128)(2,1)S(1)}, u32[]{:S(2)}, u32[]{:S(2)}) collective-permute-start(bf16[1408,384]{1,0:T(8,128)(2,1)S(1)} %get-tuple-element.22.refs_0_), channel_id=1, source_target_pairs={{0,4},{4,0},{8,12},{12,8},{16,20},{20,16},{24,28},{28,24},{32,36},... | collective-permute-start | bytes 3244040 | tf_op jit(solution)/shard_map/ppermute | solution.py:531
  2.6 14.6 %collective-permute-start.2 = (bf16[528,384]{1,0:T(8,128)(2,1)S(1)}, bf16[528,384]{1,0:T(8,128)(2,1)S(1)}, u32[]{:S(2)}, u32[]{:S(2)}) collective-permute-start(bf16[528,384]{1,0:T(8,128)(2,1)S(1)} %get-tuple-element.26), channel_id=1, source_target_pairs={{0,252},{4,8},{8,4},{12,16},{16,12},{20,24},{24,20},{28,32},{32,28... | collective-permute-start | bytes 1216520 | tf_op jit(solution)/shard_map/ppermute | solution.py:530
  11.2 11.1 %collective-permute-start.1 = (bf16[1664,128]{1,0:T(8,128)(2,1)S(1)}, bf16[1664,128]{1,0:T(8,128)(2,1)S(1)}, u32[]{:S(2)}, u32[]{:S(2)}) collective-permute-start(bf16[1664,128]{1,0:T(8,128)(2,1)S(1)} %get-tuple-element.24.refs_2_.refs_0_), channel_id=1, source_target_pairs={{0,252},{4,8},{8,4},{12,16},{16,12},{20,24},{24,20},{28,32},{32,28... | collective-permute-start | bytes 1277960 | tf_op jit(solution)/shard_map/ppermute | solution.py:539
  13.6 1.8 %copy-start.3 = (bf16[2048,256]{1,0:T(8,128)(2,1)S(1)}, bf16[2048,256]{1,0:T(8,128)(2,1)}, u32[]{:S(2)}) copy-start(bf16[2048,256]{1,0:T(8,128)(2,1)} %refs_0_.3) | copy-start | bytes 3145732
  13.6 1.8 %copy-start.4 = (bf16[2048,128]{1,0:T(8,128)(2,1)S(1)}, bf16[2048,128]{1,0:T(8,128)(2,1)}, u32[]{:S(2)}) copy-start(bf16[2048,128]{1,0:T(8,128)(2,1)} %refs_1_.3) | copy-start | bytes 1572868
  17.2 4.9 %copy-start = (bf16[8,256,128]{2,1,0:T(8,128)(2,1)S(1)}, bf16[8,256,128]{2,1,0:T(8,128)(2,1)}, u32[]{:S(2)}) copy-start(bf16[8,256,128]{2,1,0:T(8,128)(2,1)} %refs_12_.1) | copy-start | bytes 1572868
  17.2 4.9 %copy-start.1 = (bf16[8,128,128]{2,1,0:T(8,128)(2,1)S(1)}, bf16[8,128,128]{2,1,0:T(8,128)(2,1)}, u32[]{:S(2)}) copy-start(bf16[8,128,128]{2,1,0:T(8,128)(2,1)} %refs_9_.3) | copy-start | bytes 786436
  17.2 4.9 %copy-start.2 = (bf16[2,128,128]{2,1,0:T(8,128)(2,1)S(1)}, bf16[2,128,128]{2,1,0:T(8,128)(2,1)}, u32[]{:S(2)}) copy-start(bf16[2,128,128]{2,1,0:T(8,128)(2,1)} %refs_8_.5) | copy-start | bytes 196612
  17.9 7.8 %collective-permute-start.4 = (bf16[512,128]{1,0:T(8,128)(2,1)S(1)}, bf16[512,128]{1,0:T(8,128)(2,1)S(1)}, u32[]{:S(2)}, u32[]{:S(2)}) collective-permute-start(bf16[512,128]{1,0:T(8,128)(2,1)S(1)} %back.1.refs_5_), channel_id=1, source_target_pairs={{0,252},{4,8},{8,4},{12,16},{16,12},{20,24},{24,20},{28,32},{32,28... | collective-permute-start | bytes 393224 | tf_op jit(solution)/shard_map/ppermute | solution.py:562
  22.2 3.5 %collective-permute-start.3 = (bf16[1664,128]{1,0:T(8,128)(2,1)S(1)}, bf16[1664,128]{1,0:T(8,128)(2,1)S(1)}, u32[]{:S(2)}, u32[]{:S(2)}) collective-permute-start(bf16[1664,128]{1,0:T(8,128)(2,1)S(1)} %collective-permute-done.1.refs_2_), channel_id=1, source_target_pairs={{0,4},{4,0},{8,12},{12,8},{16,20},{20,16},{24,28},{28,24},{32,36},... | collective-permute-start | bytes 1277960 | tf_op jit(solution)/shard_map/ppermute | solution.py:569

commit v7 on v6

--- a/solution.py
+++ b/solution.py
@@ -215,14 +215,7 @@
     points_ref[...] = mm(hot, node_points(out_ref, 0, 512)).astype(jnp.bfloat16)
 
 
-def near_kernel(
-    points, weights, ufar_hbm, nfar_hbm, ncount_hbm, ucount_hbm, out_ref, mask_ref,
-    ufar, nfar, ncount, ucount, sems, *, rows, total,
-):
-    _, _, chip, side_a, side_b = place(total)
-    copies = fetch(
-        [(ufar_hbm, ufar), (nfar_hbm, nfar), (ncount_hbm, ncount), (ucount_hbm, ucount)], sems
-    )
+def near_work(points, weights, out_ref, rows):
     features = points.shape[1]
     same = lax.broadcasted_iota(jnp.int32, (rows, rows), 0) == lax.broadcasted_iota(
         jnp.int32, (rows, rows), 1
@@ -235,6 +228,21 @@
         power = mm_nt(pts, pts) * (2.0 * scale_of(features)) + twice(col) + row
         tile = jnp.exp2(jnp.where(same, NEG, power)).astype(jnp.bfloat16)
         out_ref[own, :] = mm(tile, weights[own, :])
+
+
+def near_kernel(
+    points, weights, ufar_hbm, nfar_hbm, ncount_hbm, ucount_hbm, out_ref, mask_ref,
+    ufar, nfar, ncount, ucount, sems, *, rows, total,
+):
+    _, core, chip, side_a, side_b = place(total)
+    copies = fetch(
+        [(ufar_hbm, ufar), (nfar_hbm, nfar), (ncount_hbm, ncount), (ucount_hbm, ucount)], sems
+    )
+
+    @pl.when(core >= 0)
+    def _():
+        near_work(points, weights, out_ref, rows)
+
     for copy in copies:
         copy.wait()
     ncounts = count_column(ncount, 2)

time: 27.8 us -> 27.5 us (0.989)
  Pallas kernels: 12.1 us -> 11.7 us
  starting transfers between devices: 15 us -> 15.4 us
  waiting for transfers between devices: 0.32 us -> 0.01 us
    ppermute x1, starting transfers between devices: 4.28 us -> 4.69 us  [per_device(): ret_in = lax.ppermute(ret, 'leaf', outward)]
    pallas_call x11, Pallas kernels: 12.1 us -> 11.7 us  [call(): pl.pallas_call(body, out_shape=outs, in_specs=[pl.BlockSpec(memory_space=...]
    ppermute x1, waiting for transfers between devices: 0.31 us -> 0.01 us  [per_device(): ret_in = lax.ppermute(ret, 'leaf', outward)]
  transfers between devices with their start and end apart: 5 -> 5, of which waited for: 1 -> 0; matrix products, arithmetic and copies ran while one was open for 0% -> 0% of each run, Pallas kernels for 28% -> 27%
where the time goes in v7:
time: 27.5 us; the launch traced here: 27.4 us
  starting transfers between devices  15.4 us (56%)
  Pallas kernels  11.7 us (43%)
    pallas_call x11, Pallas kernels, call(): pl.pallas_call(body, out_shape=outs, in_specs=[pl.BlockSpec(memory_space=...  11.7 us
    ppermute x1, starting transfers between devices, per_device(): rim_in = lax.ppermute(rim, 'leaf', outward)  8.15 us
    ppermute x1, starting transfers between devices, per_device(): ret_in = lax.ppermute(ret, 'leaf', outward)  4.69 us
    ppermute x1, starting transfers between devices, per_device(): nodes_b = lax.ppermute(nodes, 'leaf', outward)  2.41 us
  transfers between devices with their start and end apart: 5, of which 0 were waited for; matrix products, arithmetic and copies ran while one was open for 0% of the time, Pallas kernels for 27%

profile of v7, /device:TPU:16, one launch (start us, length us, event | category | flops | bytes accessed | tf_op | source)
XLA Modules:
  0.0 27.4 jit_solution(7723544791515451200)
XLA Ops:
  0.0 2.5 %front.1 = (bf16[1408,384]{1,0:T(8,128)(2,1)S(1)}, bf16[528,384]{1,0:T(8,128)(2,1)S(1)}, f32[24,128]{1,0:T(8,128)S(1)}, s32[32,128]{1,0:T(8,128)S(1)}) custom-call(bf16[2048,256]{1,0:T(8,128)(2,1)} %refs_0_.3, bf16[2048,128]{1,0:T(8,128)(2,1)} %refs_1_.3, bf16[8,256,128]{2,1,0:T(8,128)(2,1)} %refs_12_.1, bf16[8,128,128]{2,1,0:T(8,128)(2,1)} %refs_9_.3, ...), custom_call_target="tpu_custom_call" | custom-call | flops 2875000064 | tf_op jit(solution)/shard_map/front/pallas_call | solution.py:488
  2.5 0.1 collective-permute-start
  2.6 8.2 %collective-permute-start.2 = (bf16[528,384]{1,0:T(8,128)(2,1)S(1)}, bf16[528,384]{1,0:T(8,128)(2,1)S(1)}, u32[]{:S(2)}, u32[]{:S(2)}) collective-permute-start(bf16[528,384]{1,0:T(8,128)(2,1)S(1)} %get-tuple-element.26), channel_id=1, source_target_pairs={{0,252},{4,8},{8,4},{12,16},{16,12},{20,24},{24,20},{28,32},{32,28... | collective-permute-start | bytes 1216520 | tf_op jit(solution)/shard_map/ppermute | solution.py:538
  10.8 0.0 collective-permute-done.refs_1_
  10.8 0.4 %upper.1 = (bf16[1664,128]{1,0:T(8,128)(2,1)S(1)}, bf16[128,256]{1,0:T(8,128)(2,1)S(1)}) custom-call(bf16[1408,384]{1,0:T(8,128)(2,1)S(1)} %get-tuple-element.22.refs_0_, bf16[1408,384]{1,0:T(8,128)(2,1)S(1)} %collective-permute-done.refs_1_, s32[32,128]{1,0:T(8,128)S(1)} %get-tuple-element.23.refs_2_.refs_3_), custom_call_target="tpu_custom_call" | custom-call | flops 345000000 | tf_op jit(solution)/shard_map/upper/pallas_call | solution.py:488
  11.2 2.4 %collective-permute-start.1 = (bf16[1664,128]{1,0:T(8,128)(2,1)S(1)}, bf16[1664,128]{1,0:T(8,128)(2,1)S(1)}, u32[]{:S(2)}, u32[]{:S(2)}) collective-permute-start(bf16[1664,128]{1,0:T(8,128)(2,1)S(1)} %get-tuple-element.24.refs_2_.refs_0_), channel_id=1, source_target_pairs={{0,252},{4,8},{8,4},{12,16},{16,12},{20,24},{24,20},{28,32},{32,28... | collective-permute-start | bytes 1277960 | tf_op jit(solution)/shard_map/ppermute | solution.py:547
  13.6 0.0 copy-start.3
  13.6 0.0 copy-start.4
  13.6 1.8 %own.1 = (f32[1024,128]{1,0:T(8,128)S(1)}, f32[1024,128]{1,0:T(8,128)S(1)}) custom-call(bf16[1408,384]{1,0:T(8,128)(2,1)S(1)} %get-tuple-element.22.refs_0_, f32[24,128]{1,0:T(8,128)S(1)} %get-tuple-element.27.refs_1_.refs_2_.refs_3_, bf16[1664,128]{1,0:T(8,128)(2,1)S(1)} %get-tuple-element.24.refs_2_.refs_0_), custom_call_target="tpu_custom_call" | custom-call | flops 1955000064 | tf_op jit(solution)/shard_map/own/pallas_call | solution.py:488
  15.4 0.0 copy-done.3
  15.4 0.0 copy-done.4
  15.4 1.3 %near.1 = (f32[2048,128]{1,0:T(8,128)S(1)}, f32[32,128]{1,0:T(8,128)S(1)}) custom-call(bf16[2048,256]{1,0:T(8,128)(2,1)S(1)} %copy-done.3, bf16[2048,128]{1,0:T(8,128)(2,1)S(1)} %copy-done.4, s32[12,32]{1,0:T(8,128)} %bitcast.1, s32[2,12]{1,0:T(2,128)} %refs_3_.3, s32[2]{0:T(128)} %refs_4_.3, s32[32]{0:T(128)} %refs_5_.3, ...), custom_call_target="tpu_custom_call" | custom-call | flops 1955000064 | tf_op jit(solution)/shard_map/near/pallas_call | solution.py:488
  16.7 0.1 side.1.refs_3_.refs_4_
  16.8 0.0 copy-start
  16.8 0.0 copy-start.1
  16.8 0.0 copy-start.2
  16.8 0.0 collective-permute-done.2.refs_1_.refs_2_
  16.8 0.6 %back.1.refs_5_ = bf16[512,128]{1,0:T(8,128)(2,1)S(1)} custom-call(bf16[1408,384]{1,0:T(8,128)(2,1)S(1)} %get-tuple-element.22.refs_0_, bf16[528,384]{1,0:T(8,128)(2,1)S(1)} %collective-permute-done.2.refs_1_.refs_2_, f32[1024,128]{1,0:T(8,128)S(1)} %get-tuple-element.28.refs_6_.refs_3_.refs_2_.refs_4_, f32[1024,128]{1,0:T(8,128)S(1)} %side.1.refs_3_.refs_4_), custom_call_target="tpu_custom_call" | custom-call | flops 1495000064 | tf_op jit(solution)/shard_map/back/pallas_call | solution.py:488
  17.5 4.7 %collective-permute-start.4 = (bf16[512,128]{1,0:T(8,128)(2,1)S(1)}, bf16[512,128]{1,0:T(8,128)(2,1)S(1)}, u32[]{:S(2)}, u32[]{:S(2)}) collective-permute-start(bf16[512,128]{1,0:T(8,128)(2,1)S(1)} %back.1.refs_5_), channel_id=1, source_target_pairs={{0,252},{4,8},{8,4},{12,16},{16,12},{20,24},{24,20},{28,32},{32,28... | collective-permute-start | bytes 393224 | tf_op jit(solution)/shard_map/ppermute | solution.py:570
  22.2 0.0 copy-done
  22.2 0.0 copy-done.1
  22.2 0.0 copy-done.2
  22.2 0.1 rim.1.refs_5_
  22.2 0.0 collective-permute-done.1.refs_2_
  22.2 0.1 collective-permute-start.3
  22.3 1.9 %late.1.refs_5_.refs_0_ = f32[1024,128]{1,0:T(8,128)S(1)} custom-call(bf16[1408,384]{1,0:T(8,128)(2,1)S(1)} %get-tuple-element.22.refs_0_, bf16[1408,384]{1,0:T(8,128)(2,1)S(1)} %collective-permute-done.refs_1_, bf16[528,384]{1,0:T(8,128)(2,1)S(1)} %collective-permute-done.2.refs_1_.refs_2_, f32[24,128]{1,0:T(8,128)S(1)} %get-tuple-element.27.refs_1_.refs_2_.refs_3_, ...), custom_call_target="tpu_custom_call" | custom-call | flops 115000000 | tf_op jit(solution)/shard_map/late/pallas_call | solution.py:488
  24.2 1.2 %outer_node.1 = (f32[256,128]{1,0:T(8,128)S(1)}, f32[128,128]{1,0:T(8,128)S(1)}, bf16[256,256]{1,0:T(8,128)(2,1)S(1)}, f32[384,128]{1,0:T(8,128)S(1)}, bf16[128,512]{1,0:T(8,128)(2,1)S(1)}) custom-call(bf16[1664,128]{1,0:T(8,128)(2,1)S(1)} %get-tuple-element.24.refs_2_.refs_0_, bf16[128,256]{1,0:T(8,128)(2,1)S(1)} %get-tuple-element.25.refs_1_, ...), custom_call_target="tpu_custom_call" | custom-call | flops 115000000 | tf_op jit(solution)/shard_map/outer_node/pallas_call | solution.py:488
  25.4 0.0 collective-permute-done.4.refs_1_
  25.4 0.1 merge.1.refs_10_
  25.5 0.0 collective-permute-done.3.refs_4_
  25.5 1.9 %final.1 = bf16[2048,128]{1,0:T(8,128)(2,1)} custom-call(bf16[256,256]{1,0:T(8,128)(2,1)S(1)} %get-tuple-element.33.refs_0_, bf16[128,256]{1,0:T(8,128)(2,1)S(1)} %get-tuple-element.25.refs_1_, f32[384,128]{1,0:T(8,128)S(1)} %get-tuple-element.34.refs_2_, bf16[128,512]{1,0:T(8,128)(2,1)S(1)} %get-tuple-element.35.refs_3_, ...), custom_call_target="tpu_custom_call" | custom-call | flops 2184999936 | tf_op jit(solution)/shard_map/final/pallas_call | solution.py:488
Async XLA Ops:
  2.5 8.3 %collective-permute-start = (bf16[1408,384]{1,0:T(8,128)(2,1)S(1)}, bf16[1408,384]{1,0:T(8,128)(2,1)S(1)}, u32[]{:S(2)}, u32[]{:S(2)}) collective-permute-start(bf16[1408,384]{1,0:T(8,128)(2,1)S(1)} %get-tuple-element.22.refs_0_), channel_id=1, source_target_pairs={{0,4},{4,0},{8,12},{12,8},{16,20},{20,16},{24,28},{28,24},{32,36},... | collective-permute-start | bytes 3244040 | tf_op jit(solution)/shard_map/ppermute | solution.py:539
  2.6 14.2 %collective-permute-start.2 = (bf16[528,384]{1,0:T(8,128)(2,1)S(1)}, bf16[528,384]{1,0:T(8,128)(2,1)S(1)}, u32[]{:S(2)}, u32[]{:S(2)}) collective-permute-start(bf16[528,384]{1,0:T(8,128)(2,1)S(1)} %get-tuple-element.26), channel_id=1, source_target_pairs={{0,252},{4,8},{8,4},{12,16},{16,12},{20,24},{24,20},{28,32},{32,28... | collective-permute-start | bytes 1216520 | tf_op jit(solution)/shard_map/ppermute | solution.py:538
  11.2 11.1 %collective-permute-start.1 = (bf16[1664,128]{1,0:T(8,128)(2,1)S(1)}, bf16[1664,128]{1,0:T(8,128)(2,1)S(1)}, u32[]{:S(2)}, u32[]{:S(2)}) collective-permute-start(bf16[1664,128]{1,0:T(8,128)(2,1)S(1)} %get-tuple-element.24.refs_2_.refs_0_), channel_id=1, source_target_pairs={{0,252},{4,8},{8,4},{12,16},{16,12},{20,24},{24,20},{28,32},{32,28... | collective-permute-start | bytes 1277960 | tf_op jit(solution)/shard_map/ppermute | solution.py:547
  13.6 1.8 %copy-start.3 = (bf16[2048,256]{1,0:T(8,128)(2,1)S(1)}, bf16[2048,256]{1,0:T(8,128)(2,1)}, u32[]{:S(2)}) copy-start(bf16[2048,256]{1,0:T(8,128)(2,1)} %refs_0_.3) | copy-start | bytes 3145732
  13.6 1.8 %copy-start.4 = (bf16[2048,128]{1,0:T(8,128)(2,1)S(1)}, bf16[2048,128]{1,0:T(8,128)(2,1)}, u32[]{:S(2)}) copy-start(bf16[2048,128]{1,0:T(8,128)(2,1)} %refs_1_.3) | copy-start | bytes 1572868
  16.8 5.4 %copy-start = (bf16[8,256,128]{2,1,0:T(8,128)(2,1)S(1)}, bf16[8,256,128]{2,1,0:T(8,128)(2,1)}, u32[]{:S(2)}) copy-start(bf16[8,256,128]{2,1,0:T(8,128)(2,1)} %refs_12_.1) | copy-start | bytes 1572868
  16.8 5.4 %copy-start.1 = (bf16[8,128,128]{2,1,0:T(8,128)(2,1)S(1)}, bf16[8,128,128]{2,1,0:T(8,128)(2,1)}, u32[]{:S(2)}) copy-start(bf16[8,128,128]{2,1,0:T(8,128)(2,1)} %refs_9_.3) | copy-start | bytes 786436
  16.8 5.3 %copy-start.2 = (bf16[2,128,128]{2,1,0:T(8,128)(2,1)S(1)}, bf16[2,128,128]{2,1,0:T(8,128)(2,1)}, u32[]{:S(2)}) copy-start(bf16[2,128,128]{2,1,0:T(8,128)(2,1)} %refs_8_.5) | copy-start | bytes 196612
  17.5 7.9 %collective-permute-start.4 = (bf16[512,128]{1,0:T(8,128)(2,1)S(1)}, bf16[512,128]{1,0:T(8,128)(2,1)S(1)}, u32[]{:S(2)}, u32[]{:S(2)}) collective-permute-start(bf16[512,128]{1,0:T(8,128)(2,1)S(1)} %back.1.refs_5_), channel_id=1, source_target_pairs={{0,252},{4,8},{8,4},{12,16},{16,12},{20,24},{24,20},{28,32},{32,28... | collective-permute-start | bytes 393224 | tf_op jit(solution)/shard_map/ppermute | solution.py:570
  22.2 3.2 %collective-permute-start.3 = (bf16[1664,128]{1,0:T(8,128)(2,1)S(1)}, bf16[1664,128]{1,0:T(8,128)(2,1)S(1)}, u32[]{:S(2)}, u32[]{:S(2)}) collective-permute-start(bf16[1664,128]{1,0:T(8,128)(2,1)S(1)} %collective-permute-done.1.refs_2_), channel_id=1, source_target_pairs={{0,4},{4,0},{8,12},{12,8},{16,20},{20,16},{24,28},{28,24},{32,36},... | collective-permute-start | bytes 1277960 | tf_op jit(solution)/shard_map/ppermute | solution.py:577

commit v8 on v7

--- a/solution.py
+++ b/solution.py
@@ -405,8 +405,14 @@
     return mm(jnp.exp2(power).astype(jnp.bfloat16), ref[1536:1664, :])
 
 
+def chip_node_kernel(nodes_ref, mask_ref, far1_ref, *, total):
+    _, core, _, _, _ = place(total)
+    own = own_nodes(nodes_ref, core)
+    far1_ref[...] = node_part(own, norm_col(own), nodes_ref, mask_ref[0:2, :])
+
+
 def outer_node_kernel(
-    nodes_ref, upper_ref, side_b_ref, us_ref, mask_ref, far1_ref, far2_ref, own_ref, col_ref,
+    nodes_ref, upper_ref, side_b_ref, us_ref, mask_ref, start_ref, far1_ref, far2_ref, own_ref, col_ref,
     hot_ref, *, total,
 ):
     _, core, _, side_a, side_b = place(total)
@@ -419,7 +425,7 @@
     hot_ref[...] = upper_hot(us_ref[pl.ds(side_a, 1), :])
     hot = upper_hot(us_ref[pl.ds(side_b, 1), :])
     far2_ref[...] = upper_part(upper_ref[...], upper_col, side_b_ref, hot, mask_ref[24:25, :])
-    far1_ref[...] = node_part(own, col, nodes_ref, mask_ref[0:2, :]) + node_part(
+    far1_ref[...] = start_ref[...] + node_part(
         own, col, side_b_ref, mask_ref[8:10, :]
     )
 
@@ -558,10 +564,14 @@
         [like(upper_lists), like(node_far), like(node_count, SMEM), like(upper_count, SMEM), sems((4,))],
         name="near", us=1.7, after=[col],
     )
+    (far1,) = call(
+        bind(chip_node_kernel, total=total), [shape((2 * rank, cols), f32)], [nodes, node_mask],
+        "vv", name="chip_node", us=0.5,
+    )
     far_scratch = [rows_scratch, pltpu.VMEM((1024, 1024), bf16)]
     (pot,) = call(
         bind(early_kernel, side_work, total=total), [pot_shape], [pack, side, mask, col, pot],
-        "vvvvv", far_scratch, name="side", us=1.3, after=[node_mask],
+        "vvvvv", far_scratch, name="side", us=1.3, after=[far1],
     )
     (ret,) = call(
         bind(back_kernel, total=total), [shape((4 * rank, cols), bf16)], [pack, rim_in, col],
@@ -586,7 +596,7 @@
             shape((2 * rank, features), bf16), shape((3 * rank, 128), f32),
             shape((rank, 4 * rank), bf16),
         ],
-        [nodes, upper, nodes_b, us_v, node_mask], "vvvvv",
+        [nodes, upper, nodes_b, us_v, node_mask, far1], "vvvvvv",
         name="outer_node", us=0.1, after=[pot],
     )
     (pot,) = call(

time: 27.5 us -> 27.9 us (1.015)
  waiting for transfers between devices: 0.01 us -> 0.73 us
  starting transfers between devices: 15.4 us -> 14.9 us
  Pallas kernels: 11.7 us -> 12.1 us
    ppermute x1, waiting for transfers between devices: 0.01 us -> 0.72 us  [per_device(): ret_in = lax.ppermute(ret, 'leaf', outward)]
    ppermute x1, starting transfers between devices: 4.69 us -> 4.1 us  [per_device(): ret_in = lax.ppermute(ret, 'leaf', outward)]
    pallas_call x11 -> x12, Pallas kernels: 11.7 us -> 12.1 us  [call(): pl.pallas_call(body, out_shape=outs, in_specs=[pl.BlockSpec(memory_space=...]
  transfers between devices with their start and end apart: 5 -> 5, of which waited for: 0 -> 1; matrix products, arithmetic and copies ran while one was open for 0% -> 0% of each run, Pallas kernels for 27% -> 27%
where the time goes in v8:
time: 27.9 us; the launch traced here: 27.8 us
  starting transfers between devices  14.9 us (53%)
  Pallas kernels  12.1 us (43%)
  waiting for transfers between devices  0.73 us (3%)
    pallas_call x12, Pallas kernels, call(): pl.pallas_call(body, out_shape=outs, in_specs=[pl.BlockSpec(memory_space=...  12.1 us
    ppermute x1, starting transfers between devices, per_device(): rim_in = lax.ppermute(rim, 'leaf', outward)  8.15 us
    ppermute x1, starting transfers between devices, per_device(): ret_in = lax.ppermute(ret, 'leaf', outward)  4.1 us
    ppermute x1, starting transfers between devices, per_device(): nodes_b = lax.ppermute(nodes, 'leaf', outward)  2.41 us
    ppermute x1, waiting for transfers between devices, per_device(): ret_in = lax.ppermute(ret, 'leaf', outward)  0.72 us
  transfers between devices with their start and end apart: 5, of which 1 were waited for; matrix products, arithmetic and copies ran while one was open for 0% of the time, Pallas kernels for 27%

profile of v8, /device:TPU:16, one launch (start us, length us, event | category | flops | bytes accessed | tf_op | source)
XLA Modules:
  0.0 27.8 jit_solution(5630459027700008433)
XLA Ops:
  0.0 2.5 %front.1 = (bf16[1408,384]{1,0:T(8,128)(2,1)S(1)}, bf16[528,384]{1,0:T(8,128)(2,1)S(1)}, f32[24,128]{1,0:T(8,128)S(1)}, s32[32,128]{1,0:T(8,128)S(1)}) custom-call(bf16[2048,256]{1,0:T(8,128)(2,1)} %refs_0_.3, bf16[2048,128]{1,0:T(8,128)(2,1)} %refs_1_.3, bf16[8,256,128]{2,1,0:T(8,128)(2,1)} %refs_12_.1, bf16[8,128,128]{2,1,0:T(8,128)(2,1)} %refs_9_.3, ...), custom_call_target="tpu_custom_call" | custom-call | flops 2875000064 | tf_op jit(solution)/shard_map/front/pallas_call | solution.py:494
  2.5 0.1 collective-permute-start
  2.6 8.2 %collective-permute-start.2 = (bf16[528,384]{1,0:T(8,128)(2,1)S(1)}, bf16[528,384]{1,0:T(8,128)(2,1)S(1)}, u32[]{:S(2)}, u32[]{:S(2)}) collective-permute-start(bf16[528,384]{1,0:T(8,128)(2,1)S(1)} %get-tuple-element.26), channel_id=1, source_target_pairs={{0,252},{4,8},{8,4},{12,16},{16,12},{20,24},{24,20},{28,32},{32,28... | collective-permute-start | bytes 1216520 | tf_op jit(solution)/shard_map/ppermute | solution.py:544
  10.8 0.0 collective-permute-done.refs_1_
  10.8 0.4 %upper.1 = (bf16[1664,128]{1,0:T(8,128)(2,1)S(1)}, bf16[128,256]{1,0:T(8,128)(2,1)S(1)}) custom-call(bf16[1408,384]{1,0:T(8,128)(2,1)S(1)} %get-tuple-element.22.refs_0_, bf16[1408,384]{1,0:T(8,128)(2,1)S(1)} %collective-permute-done.refs_1_, s32[32,128]{1,0:T(8,128)S(1)} %get-tuple-element.23.refs_2_.refs_3_), custom_call_target="tpu_custom_call" | custom-call | flops 345000000 | tf_op jit(solution)/shard_map/upper/pallas_call | solution.py:494
  11.2 2.4 %collective-permute-start.1 = (bf16[1664,128]{1,0:T(8,128)(2,1)S(1)}, bf16[1664,128]{1,0:T(8,128)(2,1)S(1)}, u32[]{:S(2)}, u32[]{:S(2)}) collective-permute-start(bf16[1664,128]{1,0:T(8,128)(2,1)S(1)} %get-tuple-element.24.refs_2_.refs_0_), channel_id=1, source_target_pairs={{0,252},{4,8},{8,4},{12,16},{16,12},{20,24},{24,20},{28,32},{32,28... | collective-permute-start | bytes 1277960 | tf_op jit(solution)/shard_map/ppermute | solution.py:553
  13.6 0.0 copy-start.3
  13.6 0.0 copy-start.4
  13.6 1.8 %own.1 = (f32[1024,128]{1,0:T(8,128)S(1)}, f32[1024,128]{1,0:T(8,128)S(1)}) custom-call(bf16[1408,384]{1,0:T(8,128)(2,1)S(1)} %get-tuple-element.22.refs_0_, f32[24,128]{1,0:T(8,128)S(1)} %get-tuple-element.27.refs_1_.refs_2_.refs_3_, bf16[1664,128]{1,0:T(8,128)(2,1)S(1)} %get-tuple-element.24.refs_2_.refs_0_), custom_call_target="tpu_custom_call" | custom-call | flops 1955000064 | tf_op jit(solution)/shard_map/own/pallas_call | solution.py:494
  15.4 0.0 copy-done.3
  15.4 0.0 copy-done.4
  15.4 1.3 %near.1 = (f32[2048,128]{1,0:T(8,128)S(1)}, f32[32,128]{1,0:T(8,128)S(1)}) custom-call(bf16[2048,256]{1,0:T(8,128)(2,1)S(1)} %copy-done.3, bf16[2048,128]{1,0:T(8,128)(2,1)S(1)} %copy-done.4, s32[12,32]{1,0:T(8,128)} %bitcast.1, s32[2,12]{1,0:T(2,128)} %refs_3_.3, s32[2]{0:T(128)} %refs_4_.3, s32[32]{0:T(128)} %refs_5_.3, ...), custom_call_target="tpu_custom_call" | custom-call | flops 1955000064 | tf_op jit(solution)/shard_map/near/pallas_call | solution.py:494
  16.7 0.6 %chip_node.1.refs_5_ = f32[256,128]{1,0:T(8,128)S(1)} custom-call(bf16[1664,128]{1,0:T(8,128)(2,1)S(1)} %get-tuple-element.24.refs_2_.refs_0_, f32[32,128]{1,0:T(8,128)S(1)} %get-tuple-element.30.refs_1_.refs_4_.refs_5_), custom_call_target="tpu_custom_call" | custom-call | flops 575000000 | tf_op jit(solution)/shard_map/chip_node/pallas_call | solution.py:494
  17.3 0.1 side.1.refs_3_.refs_4_
  17.4 0.0 copy-start
  17.4 0.0 copy-start.1
  17.4 0.0 copy-start.2
  17.4 0.0 collective-permute-done.2.refs_1_.refs_2_
  17.4 0.6 %back.1.refs_5_ = bf16[512,128]{1,0:T(8,128)(2,1)S(1)} custom-call(bf16[1408,384]{1,0:T(8,128)(2,1)S(1)} %get-tuple-element.22.refs_0_, bf16[528,384]{1,0:T(8,128)(2,1)S(1)} %collective-permute-done.2.refs_1_.refs_2_, f32[1024,128]{1,0:T(8,128)S(1)} %get-tuple-element.28.refs_6_.refs_3_.refs_2_.refs_4_, f32[1024,128]{1,0:T(8,128)S(1)} %side.1.refs_3_.refs_4_), custom_call_target="tpu_custom_call" | custom-call | flops 1495000064 | tf_op jit(solution)/shard_map/back/pallas_call | solution.py:494
  18.1 4.1 %collective-permute-start.4 = (bf16[512,128]{1,0:T(8,128)(2,1)S(1)}, bf16[512,128]{1,0:T(8,128)(2,1)S(1)}, u32[]{:S(2)}, u32[]{:S(2)}) collective-permute-start(bf16[512,128]{1,0:T(8,128)(2,1)S(1)} %back.1.refs_5_), channel_id=1, source_target_pairs={{0,252},{4,8},{8,4},{12,16},{16,12},{20,24},{24,20},{28,32},{32,28... | collective-permute-start | bytes 393224 | tf_op jit(solution)/shard_map/ppermute | solution.py:580
  22.2 0.0 copy-done
  22.2 0.0 copy-done.1
  22.2 0.0 copy-done.2
  22.2 0.1 rim.1.refs_5_
  22.2 0.0 collective-permute-done.1.refs_2_
  22.2 0.1 collective-permute-start.3
  22.3 1.9 %late.1.refs_6_.refs_0_ = f32[1024,128]{1,0:T(8,128)S(1)} custom-call(bf16[1408,384]{1,0:T(8,128)(2,1)S(1)} %get-tuple-element.22.refs_0_, bf16[1408,384]{1,0:T(8,128)(2,1)S(1)} %collective-permute-done.refs_1_, bf16[528,384]{1,0:T(8,128)(2,1)S(1)} %collective-permute-done.2.refs_1_.refs_2_, f32[24,128]{1,0:T(8,128)S(1)} %get-tuple-element.27.refs_1_.refs_2_.refs_3_, ...), custom_call_target="tpu_custom_call" | custom-call | flops 115000000 | tf_op jit(solution)/shard_map/late/pallas_call | solution.py:494
  24.2 0.9 %outer_node.1 = (f32[256,128]{1,0:T(8,128)S(1)}, f32[128,128]{1,0:T(8,128)S(1)}, bf16[256,256]{1,0:T(8,128)(2,1)S(1)}, f32[384,128]{1,0:T(8,128)S(1)}, bf16[128,512]{1,0:T(8,128)(2,1)S(1)}) custom-call(bf16[1664,128]{1,0:T(8,128)(2,1)S(1)} %get-tuple-element.24.refs_2_.refs_0_, bf16[128,256]{1,0:T(8,128)(2,1)S(1)} %get-tuple-element.25.refs_1_, ...), custom_call_target="tpu_custom_call" | custom-call | flops 115000000 | tf_op jit(solution)/shard_map/outer_node/pallas_call | solution.py:494
  25.1 0.7 %collective-permute-done.4.refs_1_ = bf16[512,128]{1,0:T(8,128)(2,1)S(1)} collective-permute-done((bf16[512,128]{1,0:T(8,128)(2,1)S(1)}, bf16[512,128]{1,0:T(8,128)(2,1)S(1)}, u32[]{:S(2)}, u32[]{:S(2)}) %collective-permute-start.4) | collective-permute-done | bytes 131104 | tf_op jit(solution)/shard_map/ppermute | solution.py:580
  25.9 0.1 merge.1.refs_10_
  25.9 0.0 collective-permute-done.3.refs_4_
  25.9 1.9 %final.1 = bf16[2048,128]{1,0:T(8,128)(2,1)} custom-call(bf16[256,256]{1,0:T(8,128)(2,1)S(1)} %get-tuple-element.33.refs_0_, bf16[128,256]{1,0:T(8,128)(2,1)S(1)} %get-tuple-element.25.refs_1_, f32[384,128]{1,0:T(8,128)S(1)} %get-tuple-element.34.refs_2_, bf16[128,512]{1,0:T(8,128)(2,1)S(1)} %get-tuple-element.35.refs_3_, ...), custom_call_target="tpu_custom_call" | custom-call | flops 2184999936 | tf_op jit(solution)/shard_map/final/pallas_call | solution.py:494
Async XLA Ops:
  2.5 8.3 %collective-permute-start = (bf16[1408,384]{1,0:T(8,128)(2,1)S(1)}, bf16[1408,384]{1,0:T(8,128)(2,1)S(1)}, u32[]{:S(2)}, u32[]{:S(2)}) collective-permute-start(bf16[1408,384]{1,0:T(8,128)(2,1)S(1)} %get-tuple-element.22.refs_0_), channel_id=1, source_target_pairs={{0,4},{4,0},{8,12},{12,8},{16,20},{20,16},{24,28},{28,24},{32,36},... | collective-permute-start | bytes 3244040 | tf_op jit(solution)/shard_map/ppermute | solution.py:545
  2.6 14.8 %collective-permute-start.2 = (bf16[528,384]{1,0:T(8,128)(2,1)S(1)}, bf16[528,384]{1,0:T(8,128)(2,1)S(1)}, u32[]{:S(2)}, u32[]{:S(2)}) collective-permute-start(bf16[528,384]{1,0:T(8,128)(2,1)S(1)} %get-tuple-element.26), channel_id=1, source_target_pairs={{0,252},{4,8},{8,4},{12,16},{16,12},{20,24},{24,20},{28,32},{32,28... | collective-permute-start | bytes 1216520 | tf_op jit(solution)/shard_map/ppermute | solution.py:544
  11.2 11.1 %collective-permute-start.1 = (bf16[1664,128]{1,0:T(8,128)(2,1)S(1)}, bf16[1664,128]{1,0:T(8,128)(2,1)S(1)}, u32[]{:S(2)}, u32[]{:S(2)}) collective-permute-start(bf16[1664,128]{1,0:T(8,128)(2,1)S(1)} %get-tuple-element.24.refs_2_.refs_0_), channel_id=1, source_target_pairs={{0,252},{4,8},{8,4},{12,16},{16,12},{20,24},{24,20},{28,32},{32,28... | collective-permute-start | bytes 1277960 | tf_op jit(solution)/shard_map/ppermute | solution.py:553
  13.6 1.8 %copy-start.3 = (bf16[2048,256]{1,0:T(8,128)(2,1)S(1)}, bf16[2048,256]{1,0:T(8,128)(2,1)}, u32[]{:S(2)}) copy-start(bf16[2048,256]{1,0:T(8,128)(2,1)} %refs_0_.3) | copy-start | bytes 3145732
  13.6 1.8 %copy-start.4 = (bf16[2048,128]{1,0:T(8,128)(2,1)S(1)}, bf16[2048,128]{1,0:T(8,128)(2,1)}, u32[]{:S(2)}) copy-start(bf16[2048,128]{1,0:T(8,128)(2,1)} %refs_1_.3) | copy-start | bytes 1572868
  17.4 4.8 %copy-start = (bf16[8,256,128]{2,1,0:T(8,128)(2,1)S(1)}, bf16[8,256,128]{2,1,0:T(8,128)(2,1)}, u32[]{:S(2)}) copy-start(bf16[8,256,128]{2,1,0:T(8,128)(2,1)} %refs_12_.1) | copy-start | bytes 1572868
  17.4 4.8 %copy-start.1 = (bf16[8,128,128]{2,1,0:T(8,128)(2,1)S(1)}, bf16[8,128,128]{2,1,0:T(8,128)(2,1)}, u32[]{:S(2)}) copy-start(bf16[8,128,128]{2,1,0:T(8,128)(2,1)} %refs_9_.3) | copy-start | bytes 786436
  17.4 4.8 %copy-start.2 = (bf16[2,128,128]{2,1,0:T(8,128)(2,1)S(1)}, bf16[2,128,128]{2,1,0:T(8,128)(2,1)}, u32[]{:S(2)}) copy-start(bf16[2,128,128]{2,1,0:T(8,128)(2,1)} %refs_8_.5) | copy-start | bytes 196612
  18.1 7.8 %collective-permute-start.4 = (bf16[512,128]{1,0:T(8,128)(2,1)S(1)}, bf16[512,128]{1,0:T(8,128)(2,1)S(1)}, u32[]{:S(2)}, u32[]{:S(2)}) collective-permute-start(bf16[512,128]{1,0:T(8,128)(2,1)S(1)} %back.1.refs_5_), channel_id=1, source_target_pairs={{0,252},{4,8},{8,4},{12,16},{16,12},{20,24},{24,20},{28,32},{32,28... | collective-permute-start | bytes 393224 | tf_op jit(solution)/shard_map/ppermute | solution.py:580
  22.2 3.7 %collective-permute-start.3 = (bf16[1664,128]{1,0:T(8,128)(2,1)S(1)}, bf16[1664,128]{1,0:T(8,128)(2,1)S(1)}, u32[]{:S(2)}, u32[]{:S(2)}) collective-permute-start(bf16[1664,128]{1,0:T(8,128)(2,1)S(1)} %collective-permute-done.1.refs_2_), channel_id=1, source_target_pairs={{0,4},{4,0},{8,12},{12,8},{16,20},{20,16},{24,28},{28,24},{32,36},... | collective-permute-start | bytes 1277960 | tf_op jit(solution)/shard_map/ppermute | solution.py:587
